TPU v7x, 32 devices: a whole 2x2x4 slice. The times are simulated.
32 devices in a mesh: seq: 8 (over z, core), fsdp: 4 (over y, x).
Axes of the slice: x: 2, y: 2, z: 4, core: 2. Of those that a mesh axis runs over, the one named last changes fastest.
Arguments:
- layer_input: bfloat16 [8, 512, 1152], P('fsdp', 'seq'), may hold values from -6 to 6
- document_numbers: int32 [8, 512], P('fsdp', 'seq'), may hold values from 0 to 14, as said below
- cotangent: bfloat16 [8, 512, 1152], P('fsdp', 'seq'), may hold values from -6 to 6
- shared_qkv_weight: bfloat16 [1152, 1536], P(('seq', 'fsdp')), may hold values from -0.1875 to 0.1875
- qkv_adapter_a: bfloat16 [1152, 768], P(('seq', 'fsdp')), may hold values from -0.1875 to 0.1875
- query_adapter_b: bfloat16 [256, 1024], P(('seq', 'fsdp')), may hold values from -0.375 to 0.375
- keyvalue_adapter_b: bfloat16 [2, 256, 256], P(None, ('seq', 'fsdp')), may hold values from -0.375 to 0.375
- shared_outproj_weight: bfloat16 [1024, 1152], P(('seq', 'fsdp')), may hold values from -0.75 to 0.75
- outproj_adapter_a: bfloat16 [1024, 256], P(('seq', 'fsdp')), may hold values from -0.75 to 0.75
- outproj_adapter_b: bfloat16 [256, 1152], P(('seq', 'fsdp')), may hold values from -0.375 to 0.375
- shared_gateup_weight: bfloat16 [1152, 13824], P(('seq', 'fsdp')), may hold values from -0.1875 to 0.1875
- gateup_adapter_a: bfloat16 [1152, 512], P(('seq', 'fsdp')), may hold values from -0.1875 to 0.1875
- gateup_adapter_b: bfloat16 [2, 256, 6912], P(None, ('seq', 'fsdp')), may hold values from -0.375 to 0.375
- shared_down_weight: bfloat16 [6912, 1152], P(('seq', 'fsdp')), may hold values from -0.078125 to 0.078125
- down_adapter_a: bfloat16 [6912, 256], P(('seq', 'fsdp')), may hold values from -0.078125 to 0.078125
- down_adapter_b: bfloat16 [256, 1152], P(('seq', 'fsdp')), may hold values from -0.375 to 0.375
- attention_norm_gain: bfloat16 [1152], P(('seq', 'fsdp')), may hold values from 0.099609375 to 1.8984375
- feedforward_norm_gain: bfloat16 [1152], P(('seq', 'fsdp')), may hold values from 0.099609375 to 1.8984375
Outputs:
- activations: bfloat16 [8, 512, 1152], P('fsdp', 'seq')
- grad_input: float32 [8, 512, 1152], P('fsdp', 'seq')
- grad_w_qkv: float32 [1152, 1536], P(('seq', 'fsdp'))
- qkv_adapter_a_gradient: float32 [1152, 768], P(('seq', 'fsdp'))
- query_adapter_b_gradient: float32 [256, 1024], P(('seq', 'fsdp'))
- keyvalue_adapter_b_gradient: float32 [2, 256, 256], P(None, ('seq', 'fsdp'))
- grad_w_out: float32 [1024, 1152], P(('seq', 'fsdp'))
- outproj_adapter_a_gradient: float32 [1024, 256], P(('seq', 'fsdp'))
- outproj_adapter_b_gradient: float32 [256, 1152], P(('seq', 'fsdp'))
- grad_w_gate_up: float32 [1152, 13824], P(('seq', 'fsdp'))
- gateup_adapter_a_gradient: float32 [1152, 512], P(('seq', 'fsdp'))
- gateup_adapter_b_gradient: float32 [2, 256, 6912], P(None, ('seq', 'fsdp'))
- grad_w_down: float32 [6912, 1152], P(('seq', 'fsdp'))
- down_adapter_a_gradient: float32 [6912, 256], P(('seq', 'fsdp'))
- down_adapter_b_gradient: float32 [256, 1152], P(('seq', 'fsdp'))
- grad_gain_attn: float32 [1152], P(('seq', 'fsdp'))
- grad_gain_ffn: float32 [1152], P(('seq', 'fsdp'))
Inputs may be any that keep to these rules, and one draw needn't show every extreme that they name: `document_numbers`: along each row the ids never fall, and the tokens of one id are contiguous.
All inputs are finite; a program needn't handle non-finite values.
Results may differ from a plain program's by a relative error of at most 0.022.
Values may be sent and summed in bfloat16 or wider, within the bound.
A program may use at most 512 MiB of HBM per device.

v0:
```python
import math

import jax
import jax.numpy as jnp
from jax import lax
from jax.sharding import PartitionSpec as P

QUERY_HEADS = 4
HEAD_SIZE = 256
HIDDEN_UNITS = 6912
ADAPTER_RANK = 256


EPSILON = 1e-06
ROPE_BASE = 10000.0
MASKED = -1e30


def norm_apply(hidden, gain):
    return hidden * lax.rsqrt(jnp.mean(hidden * hidden, axis=-1, keepdims=True) + EPSILON) * gain


def rope_tables(positions):
    half_dim = HEAD_SIZE // 2
    spacing = jnp.exp(
        -(2.0 * jnp.arange(half_dim).astype(jnp.float32) / HEAD_SIZE) * math.log(ROPE_BASE)
    )
    angle = positions.astype(jnp.float32)[..., None] * spacing
    return (jnp.cos(angle), jnp.sin(angle))


def rotate(values, cosine, sine_part):
    half_dim = values.shape[-1] // 2
    first = values[..., :half_dim]
    second = values[..., half_dim:]
    return jnp.concatenate(
        [first * cosine - second * sine_part, second * cosine + first * sine_part], axis=-1
    )


def unrotate(grads, cosine, sine_part):
    half_dim = grads.shape[-1] // 2
    first = grads[..., :half_dim]
    second = grads[..., half_dim:]
    return jnp.concatenate(
        [first * cosine + second * sine_part, second * cosine - first * sine_part], axis=-1
    )


def dot_plain(left, right):
    return jnp.dot(left, right, preferred_element_type=jnp.float32)


def dot_transposed_left(left, right):
    return lax.dot_general(
        left, right, (((0,), (0,)), ((), ())), preferred_element_type=jnp.float32
    )


def dot_right_t(left, right):
    return lax.dot_general(
        left, right, (((1,), (1,)), ((), ())), preferred_element_type=jnp.float32
    )


def shards(
    layer_input,
    document_numbers,
    cotangent,
    shared_qkv_weight,
    qkv_adapter_a,
    query_adapter_b,
    keyvalue_adapter_b,
    shared_outproj_weight,
    outproj_adapter_a,
    outproj_adapter_b,
    shared_gateup_weight,
    gateup_adapter_a,
    gateup_adapter_b,
    shared_down_weight,
    down_adapter_a,
    down_adapter_b,
    attention_norm_gain,
    feedforward_norm_gain,
):
    rows_here, seg_len, width = layer_input.shape
    tok_count = rows_here * seg_len
    total_head_width = QUERY_HEADS * HEAD_SIZE
    scale = HEAD_SIZE ** (-0.5)
    seq_rank = lax.axis_index("seq")
    row_ids = lax.all_gather(document_numbers, "seq", axis=1, tiled=True)
    row_len = row_ids.shape[1]
    query_place = seq_rank * seg_len + jnp.arange(seg_len, dtype=jnp.int32)
    key_place = jnp.arange(row_len, dtype=jnp.int32)
    same_doc = row_ids[:, None, :] == document_numbers[:, :, None]
    positions = jnp.sum(
        (same_doc & (key_place[None, :] < query_place[:, None])[None]).astype(jnp.int32), axis=2
    )
    allowed = same_doc & (key_place[None, :] <= query_place[:, None])[None]
    cosine, sine_part = rope_tables(positions)
    attn_set = (
        lax.all_gather(shared_qkv_weight, ("seq", "fsdp"), axis=0, tiled=True),
        lax.all_gather(qkv_adapter_a, ("seq", "fsdp"), axis=0, tiled=True),
        lax.all_gather(query_adapter_b, ("seq", "fsdp"), axis=0, tiled=True),
        lax.all_gather(keyvalue_adapter_b, ("seq", "fsdp"), axis=1, tiled=True),
        lax.all_gather(shared_outproj_weight, ("seq", "fsdp"), axis=0, tiled=True),
        lax.all_gather(outproj_adapter_a, ("seq", "fsdp"), axis=0, tiled=True),
        lax.all_gather(outproj_adapter_b, ("seq", "fsdp"), axis=0, tiled=True),
        lax.all_gather(attention_norm_gain, ("seq", "fsdp"), axis=0, tiled=True),
        lax.all_gather(feedforward_norm_gain, ("seq", "fsdp"), axis=0, tiled=True),
    )
    ffn_set = (
        lax.all_gather(shared_gateup_weight, ("seq", "fsdp"), axis=0, tiled=True),
        lax.all_gather(gateup_adapter_a, ("seq", "fsdp"), axis=0, tiled=True),
        lax.all_gather(gateup_adapter_b, ("seq", "fsdp"), axis=1, tiled=True),
        lax.all_gather(shared_down_weight, ("seq", "fsdp"), axis=0, tiled=True),
        lax.all_gather(down_adapter_a, ("seq", "fsdp"), axis=0, tiled=True),
        lax.all_gather(down_adapter_b, ("seq", "fsdp"), axis=0, tiled=True),
    )
    (
        full_qkv,
        full_qkv_a,
        full_q_b,
        full_kv_b,
        full_out,
        full_out_a,
        full_out_b,
        full_gain_a,
        full_gain_f,
    ) = attn_set
    full_gate_up, full_gu_a, full_gu_b, full_down, full_down_a, full_down_b = ffn_set
    gain_one = full_gain_a.astype(jnp.float32)
    gain_two = full_gain_f.astype(jnp.float32)
    input_f = layer_input.astype(jnp.float32).reshape(tok_count, width)
    first_norm_output = norm_apply(input_f, gain_one).astype(jnp.bfloat16)
    qkv_update = dot_plain(first_norm_output, full_qkv_a).astype(jnp.bfloat16)
    projection_output = dot_plain(first_norm_output, full_qkv) + jnp.concatenate(
        [
            dot_plain(qkv_update[:, :ADAPTER_RANK], full_q_b),
            dot_plain(qkv_update[:, ADAPTER_RANK : 2 * ADAPTER_RANK], full_kv_b[0]),
            dot_plain(qkv_update[:, 2 * ADAPTER_RANK :], full_kv_b[1]),
        ],
        axis=1,
    )
    query_low = rotate(
        projection_output[:, :total_head_width].reshape(rows_here, seg_len, QUERY_HEADS, HEAD_SIZE),
        cosine[:, :, None, :],
        sine_part[:, :, None, :],
    ).astype(jnp.bfloat16)
    key_low = rotate(
        projection_output[:, total_head_width : total_head_width + HEAD_SIZE].reshape(
            rows_here, seg_len, HEAD_SIZE
        ),
        cosine,
        sine_part,
    ).astype(jnp.bfloat16)
    value_low = (
        projection_output[:, total_head_width + HEAD_SIZE :]
        .reshape(rows_here, seg_len, HEAD_SIZE)
        .astype(jnp.bfloat16)
    )
    keys_all, values_all = (
        lax.all_gather(key_low, "seq", axis=1, tiled=True),
        lax.all_gather(value_low, "seq", axis=1, tiled=True),
    )
    mixed_rows = []
    lse_rows = []
    for row_num in range(rows_here):
        row_mask = allowed[row_num][None]
        scores = (
            jnp.einsum(
                "shd,ld->hsl",
                query_low[row_num],
                keys_all[row_num],
                preferred_element_type=jnp.float32,
            )
            * scale
        )
        scores = jnp.where(row_mask, scores, MASKED)
        row_max = jnp.max(scores, axis=-1)
        log_total = row_max + jnp.log(jnp.sum(jnp.exp(scores - row_max[..., None]), axis=-1))
        probs = jnp.where(row_mask, jnp.exp(scores - log_total[..., None]), 0.0).astype(
            jnp.bfloat16
        )
        mixed_rows.append(
            jnp.einsum(
                "hsl,ld->shd", probs, values_all[row_num], preferred_element_type=jnp.float32
            ).astype(jnp.bfloat16)
        )
        lse_rows.append(log_total)
    mixed_heads = jnp.stack(mixed_rows).reshape(tok_count, total_head_width)
    log_totals = jnp.stack(lse_rows)
    outproj_update = dot_plain(mixed_heads, full_out_a).astype(jnp.bfloat16)
    attention_output = dot_plain(mixed_heads, full_out) + dot_plain(outproj_update, full_out_b)
    first_residual = input_f + attention_output
    second_norm_output = norm_apply(first_residual, gain_two).astype(jnp.bfloat16)
    gateup_update = dot_plain(second_norm_output, full_gu_a).astype(jnp.bfloat16)
    gate_f = dot_plain(second_norm_output, full_gate_up[:, :HIDDEN_UNITS]) + dot_plain(
        gateup_update[:, :ADAPTER_RANK], full_gu_b[0]
    )
    up_f = dot_plain(second_norm_output, full_gate_up[:, HIDDEN_UNITS:]) + dot_plain(
        gateup_update[:, ADAPTER_RANK:], full_gu_b[1]
    )
    activation_lowrank = (jax.nn.gelu(gate_f, approximate=True) * up_f).astype(jnp.bfloat16)
    down_update = dot_plain(activation_lowrank, full_down_a).astype(jnp.bfloat16)
    activations = (
        first_residual
        + dot_plain(activation_lowrank, full_down)
        + dot_plain(down_update, full_down_b)
    ).astype(jnp.bfloat16)
    ffn_back = (
        lax.all_gather(shared_gateup_weight, ("seq", "fsdp"), axis=0, tiled=True),
        lax.all_gather(gateup_adapter_a, ("seq", "fsdp"), axis=0, tiled=True),
        lax.all_gather(gateup_adapter_b, ("seq", "fsdp"), axis=1, tiled=True),
        lax.all_gather(shared_down_weight, ("seq", "fsdp"), axis=0, tiled=True),
        lax.all_gather(down_adapter_a, ("seq", "fsdp"), axis=0, tiled=True),
        lax.all_gather(down_adapter_b, ("seq", "fsdp"), axis=0, tiled=True),
    )
    back_gate_up, back_gu_a, back_gu_b, back_down, back_down_a, back_down_b = ffn_back
    lowrank_gradient = cotangent.reshape(tok_count, width)
    grad_float = lowrank_gradient.astype(jnp.float32)
    grad_w_down = dot_transposed_left(activation_lowrank, lowrank_gradient)
    down_update_gradient = dot_right_t(lowrank_gradient, back_down_b).astype(jnp.bfloat16)
    down_adapter_b_gradient = dot_transposed_left(down_update, lowrank_gradient)
    down_adapter_a_gradient = dot_transposed_left(activation_lowrank, down_update_gradient)
    d_act = dot_right_t(lowrank_gradient, back_down) + dot_right_t(
        down_update_gradient, back_down_a
    )
    unused_value, gelu_pull = jax.vjp(
        lambda gate_part, up_part: jax.nn.gelu(gate_part, approximate=True) * up_part, gate_f, up_f
    )
    d_gate, d_up = gelu_pull(d_act)
    d_gu = jnp.concatenate([d_gate, d_up], axis=1).astype(jnp.bfloat16)
    gateup_update_gradient = jnp.concatenate(
        [
            dot_right_t(d_gu[:, :HIDDEN_UNITS], back_gu_b[0]),
            dot_right_t(d_gu[:, HIDDEN_UNITS:], back_gu_b[1]),
        ],
        axis=1,
    ).astype(jnp.bfloat16)
    grad_w_gate_up = dot_transposed_left(second_norm_output, d_gu)
    gateup_adapter_b_gradient = jnp.stack(
        [
            dot_transposed_left(gateup_update[:, :ADAPTER_RANK], d_gu[:, :HIDDEN_UNITS]),
            dot_transposed_left(gateup_update[:, ADAPTER_RANK:], d_gu[:, HIDDEN_UNITS:]),
        ]
    )
    gateup_adapter_a_gradient = dot_transposed_left(second_norm_output, gateup_update_gradient)
    d_norm_two = dot_right_t(d_gu, back_gate_up) + dot_right_t(gateup_update_gradient, back_gu_a)
    unused_norm, norm_pull_two = jax.vjp(norm_apply, first_residual, gain_two)
    d_resid_norm, grad_gain_ffn = norm_pull_two(d_norm_two)
    d_resid = grad_float + d_resid_norm
    ffn_terms = (
        grad_w_gate_up,
        gateup_adapter_a_gradient,
        gateup_adapter_b_gradient,
        grad_w_down,
        down_adapter_a_gradient,
        down_adapter_b_gradient,
        grad_gain_ffn,
    )
    ffn_summed = (
        lax.psum_scatter(ffn_terms[0], ("seq", "fsdp"), scatter_dimension=0, tiled=True),
        lax.psum_scatter(ffn_terms[1], ("seq", "fsdp"), scatter_dimension=0, tiled=True),
        lax.psum_scatter(ffn_terms[2], ("seq", "fsdp"), scatter_dimension=1, tiled=True),
        lax.psum_scatter(ffn_terms[3], ("seq", "fsdp"), scatter_dimension=0, tiled=True),
        lax.psum_scatter(ffn_terms[4], ("seq", "fsdp"), scatter_dimension=0, tiled=True),
        lax.psum_scatter(ffn_terms[5], ("seq", "fsdp"), scatter_dimension=0, tiled=True),
        lax.psum_scatter(ffn_terms[6], ("seq", "fsdp"), scatter_dimension=0, tiled=True),
    )
    (
        grad_w_gate_up,
        gateup_adapter_a_gradient,
        gateup_adapter_b_gradient,
        grad_w_down,
        down_adapter_a_gradient,
        down_adapter_b_gradient,
        grad_gain_ffn,
    ) = ffn_summed
    attn_back = (
        lax.all_gather(shared_qkv_weight, ("seq", "fsdp"), axis=0, tiled=True),
        lax.all_gather(qkv_adapter_a, ("seq", "fsdp"), axis=0, tiled=True),
        lax.all_gather(query_adapter_b, ("seq", "fsdp"), axis=0, tiled=True),
        lax.all_gather(keyvalue_adapter_b, ("seq", "fsdp"), axis=1, tiled=True),
        lax.all_gather(shared_outproj_weight, ("seq", "fsdp"), axis=0, tiled=True),
        lax.all_gather(outproj_adapter_a, ("seq", "fsdp"), axis=0, tiled=True),
        lax.all_gather(outproj_adapter_b, ("seq", "fsdp"), axis=0, tiled=True),
    )
    back_qkv, back_qkv_a, back_q_b, back_kv_b, back_out, back_out_a, back_out_b = attn_back
    attention_gradient = d_resid.astype(jnp.bfloat16)
    outproj_update_gradient = dot_right_t(attention_gradient, back_out_b).astype(jnp.bfloat16)
    d_mixed = (
        dot_right_t(attention_gradient, back_out) + dot_right_t(outproj_update_gradient, back_out_a)
    ).astype(jnp.bfloat16)
    grad_w_out = dot_transposed_left(mixed_heads, attention_gradient)
    outproj_adapter_b_gradient = dot_transposed_left(outproj_update, attention_gradient)
    outproj_adapter_a_gradient = dot_transposed_left(mixed_heads, outproj_update_gradient)
    d_heads = d_mixed.reshape(rows_here, seg_len, QUERY_HEADS, HEAD_SIZE)
    query_grads = []
    delta_rows = []
    key_terms = []
    value_terms = []
    for row_num in range(rows_here):
        row_mask = allowed[row_num][None]
        scores = (
            jnp.einsum(
                "shd,ld->hsl",
                query_low[row_num],
                keys_all[row_num],
                preferred_element_type=jnp.float32,
            )
            * scale
        )
        probs_f = jnp.where(row_mask, jnp.exp(scores - log_totals[row_num][..., None]), 0.0)
        d_probs = jnp.einsum(
            "shd,ld->hsl", d_heads[row_num], values_all[row_num], preferred_element_type=jnp.float32
        )
        delta = jnp.sum(probs_f * d_probs, axis=-1)
        d_scores = (probs_f * (d_probs - delta[..., None])).astype(jnp.bfloat16)
        query_grads.append(
            jnp.einsum(
                "hsl,ld->shd", d_scores, keys_all[row_num], preferred_element_type=jnp.float32
            )
            * scale
        )
        delta_rows.append(delta)
        key_terms.append(
            jnp.einsum(
                "hsl,shd->ld", d_scores, query_low[row_num], preferred_element_type=jnp.float32
            )
            * scale
        )
        value_terms.append(
            jnp.einsum(
                "hsl,shd->ld",
                probs_f.astype(jnp.bfloat16),
                d_heads[row_num],
                preferred_element_type=jnp.float32,
            )
        )
    d_query = jnp.stack(query_grads)
    d_key, d_value = (
        lax.psum_scatter(
            jnp.stack(key_terms).astype(jnp.bfloat16), "seq", scatter_dimension=1, tiled=True
        ).astype(jnp.float32),
        lax.psum_scatter(
            jnp.stack(value_terms).astype(jnp.bfloat16), "seq", scatter_dimension=1, tiled=True
        ).astype(jnp.float32),
    )
    d_query = unrotate(d_query, cosine[:, :, None, :], sine_part[:, :, None, :])
    d_key = unrotate(d_key, cosine, sine_part)
    projection_gradient = jnp.concatenate(
        [
            d_query.reshape(tok_count, total_head_width),
            d_key.reshape(tok_count, HEAD_SIZE),
            d_value.reshape(tok_count, HEAD_SIZE),
        ],
        axis=1,
    ).astype(jnp.bfloat16)
    qkv_update_gradient = jnp.concatenate(
        [
            dot_right_t(projection_gradient[:, :total_head_width], back_q_b),
            dot_right_t(
                projection_gradient[:, total_head_width : total_head_width + HEAD_SIZE],
                back_kv_b[0],
            ),
            dot_right_t(projection_gradient[:, total_head_width + HEAD_SIZE :], back_kv_b[1]),
        ],
        axis=1,
    ).astype(jnp.bfloat16)
    grad_w_qkv = dot_transposed_left(first_norm_output, projection_gradient)
    qkv_adapter_a_gradient = dot_transposed_left(first_norm_output, qkv_update_gradient)
    query_adapter_b_gradient = dot_transposed_left(
        qkv_update[:, :ADAPTER_RANK], projection_gradient[:, :total_head_width]
    )
    keyvalue_adapter_b_gradient = jnp.stack(
        [
            dot_transposed_left(
                qkv_update[:, ADAPTER_RANK : 2 * ADAPTER_RANK],
                projection_gradient[:, total_head_width : total_head_width + HEAD_SIZE],
            ),
            dot_transposed_left(
                qkv_update[:, 2 * ADAPTER_RANK :],
                projection_gradient[:, total_head_width + HEAD_SIZE :],
            ),
        ]
    )
    d_norm_one = dot_right_t(projection_gradient, back_qkv) + dot_right_t(
        qkv_update_gradient, back_qkv_a
    )
    unused_first, norm_pull_one = jax.vjp(norm_apply, input_f, gain_one)
    d_input_norm, grad_gain_attn = norm_pull_one(d_norm_one)
    grad_input = d_resid + d_input_norm
    attn_terms = (
        grad_w_qkv,
        qkv_adapter_a_gradient,
        query_adapter_b_gradient,
        keyvalue_adapter_b_gradient,
        grad_w_out,
        outproj_adapter_a_gradient,
        outproj_adapter_b_gradient,
        grad_gain_attn,
    )
    attn_summed = (
        lax.psum_scatter(attn_terms[0], ("seq", "fsdp"), scatter_dimension=0, tiled=True),
        lax.psum_scatter(attn_terms[1], ("seq", "fsdp"), scatter_dimension=0, tiled=True),
        lax.psum_scatter(attn_terms[2], ("seq", "fsdp"), scatter_dimension=0, tiled=True),
        lax.psum_scatter(attn_terms[3], ("seq", "fsdp"), scatter_dimension=1, tiled=True),
        lax.psum_scatter(attn_terms[4], ("seq", "fsdp"), scatter_dimension=0, tiled=True),
        lax.psum_scatter(attn_terms[5], ("seq", "fsdp"), scatter_dimension=0, tiled=True),
        lax.psum_scatter(attn_terms[6], ("seq", "fsdp"), scatter_dimension=0, tiled=True),
        lax.psum_scatter(attn_terms[7], ("seq", "fsdp"), scatter_dimension=0, tiled=True),
    )
    (
        grad_w_qkv,
        qkv_adapter_a_gradient,
        query_adapter_b_gradient,
        keyvalue_adapter_b_gradient,
        grad_w_out,
        outproj_adapter_a_gradient,
        outproj_adapter_b_gradient,
        grad_gain_attn,
    ) = attn_summed
    return (
        activations.reshape(rows_here, seg_len, width),
        grad_input.reshape(rows_here, seg_len, width),
        grad_w_qkv,
        qkv_adapter_a_gradient,
        query_adapter_b_gradient,
        keyvalue_adapter_b_gradient,
        grad_w_out,
        outproj_adapter_a_gradient,
        outproj_adapter_b_gradient,
        grad_w_gate_up,
        gateup_adapter_a_gradient,
        gateup_adapter_b_gradient,
        grad_w_down,
        down_adapter_a_gradient,
        down_adapter_b_gradient,
        grad_gain_attn,
        grad_gain_ffn,
    )


def solution(mesh):
    placed = (
        P("fsdp", "seq", None),
        P("fsdp", "seq"),
        P("fsdp", "seq", None),
        P(("seq", "fsdp"), None),
        P(("seq", "fsdp"), None),
        P(("seq", "fsdp"), None),
        P(None, ("seq", "fsdp"), None),
        P(("seq", "fsdp"), None),
        P(("seq", "fsdp"), None),
        P(("seq", "fsdp"), None),
        P(("seq", "fsdp"), None),
        P(("seq", "fsdp"), None),
        P(None, ("seq", "fsdp"), None),
        P(("seq", "fsdp"), None),
        P(("seq", "fsdp"), None),
        P(("seq", "fsdp"), None),
        P(("seq", "fsdp")),
        P(("seq", "fsdp")),
    )
    return jax.shard_map(
        shards,
        mesh=mesh,
        in_specs=placed,
        out_specs=(
            P("fsdp", "seq", None),
            P("fsdp", "seq", None),
            P(("seq", "fsdp"), None),
            P(("seq", "fsdp"), None),
            P(("seq", "fsdp"), None),
            P(None, ("seq", "fsdp"), None),
            P(("seq", "fsdp"), None),
            P(("seq", "fsdp"), None),
            P(("seq", "fsdp"), None),
            P(("seq", "fsdp"), None),
            P(("seq", "fsdp"), None),
            P(None, ("seq", "fsdp"), None),
            P(("seq", "fsdp"), None),
            P(("seq", "fsdp"), None),
            P(("seq", "fsdp"), None),
            P(("seq", "fsdp")),
            P(("seq", "fsdp")),
        ),
        check_vma=False,
    )
```

profile of v0, /device:TPU:17, one launch (start us, length us, event | category | flops | bytes accessed | tf_op | source)
XLA Modules:
  0.0 3758.6 jit_solution(14937478995491286118)
XLA Ops:
  16.2 40.1 %all-reduce.17 = (bf16[1152]{0:T(1024)(128)(2,1)S(1)}, bf16[1152]{0:T(1024)(128)(2,1)S(1)}) all-reduce(bf16[1152]{0:T(1024)(128)(2,1)S(1)} %dynamic-update-slice, bf16[1152]{0:T(1024)(128)(2,1)S(1)} %dynamic-update-slice.1), channel_id=1, replica_groups=mesh['seq'=8,'fsdp'=4] {'seq','fsdp'}, use_global_device_ids=true, to_apply=%add | all-reduce | flops 2304 | bytes 9216
  66.4 53.3 %all_gather.71 = bf16[2,256,256]{2,1,0:T(8,128)(2,1)S(1)} all-gather(bf16[2,8,256]{2,1,0:T(8,128)(2,1)} %param.24), channel_id=1, replica_groups=mesh['seq'=8,'fsdp'=4] {'seq','fsdp'}, dimensions={1}, use_global_device_ids=true | all-gather | bytes 270336 | tf_op jit(solution)/shard_map/all_gather | solution.py:105
  121.1 68.3 %all_gather.84 = bf16[256,1152]{1,0:T(8,128)(2,1)S(1)} all-gather(bf16[8,1152]{1,0:T(8,128)(2,1)} %param.33), channel_id=1, replica_groups=mesh['seq'=8,'fsdp'=4] {'seq','fsdp'}, dimensions={0}, use_global_device_ids=true | all-gather | bytes 608256 | tf_op jit(solution)/shard_map/all_gather | solution.py:118
  190.3 67.0 %all_gather.70 = bf16[256,1024]{1,0:T(8,128)(2,1)S(1)} all-gather(bf16[8,1024]{1,0:T(8,128)(2,1)S(1)} %copy-done.96), channel_id=1, replica_groups=mesh['seq'=8,'fsdp'=4] {'seq','fsdp'}, dimensions={0}, use_global_device_ids=true | all-gather | bytes 540672 | tf_op jit(solution)/shard_map/all_gather | solution.py:104
  257.3 77.0 %all_gather.76 = bf16[1024,256]{1,0:T(8,128)(2,1)} all-gather(bf16[32,256]{1,0:T(8,128)(2,1)S(1)} %copy-done.97), channel_id=1, replica_groups=mesh['seq'=8,'fsdp'=4] {'seq','fsdp'}, dimensions={0}, use_global_device_ids=true | all-gather | bytes 540672 | tf_op jit(solution)/shard_map/all_gather | solution.py:107
  334.3 73.2 %all_gather.77 = bf16[256,1152]{1,0:T(8,128)(2,1)} all-gather(bf16[8,1152]{1,0:T(8,128)(2,1)S(1)} %copy-done.91), channel_id=1, replica_groups=mesh['seq'=8,'fsdp'=4] {'seq','fsdp'}, dimensions={0}, use_global_device_ids=true | all-gather | bytes 608256 | tf_op jit(solution)/shard_map/all_gather | solution.py:108
  428.6 34.5 all_gather.74
  466.6 16.9 all_gather.72
  489.4 11.8 fusion.133
  507.4 137.4 %all-gather.26.cloned.1.call-done = bf16[32,36,13824]{2,1,0:T(8,128)(2,1)} async-done(((bf16[1,36,13824]{2,1,0:T(8,128)(2,1)}), bf16[32,36,13824]{2,1,0:T(8,128)(2,1)}) %all-gather.26.cloned.1.call-update) | async-done | bytes 31850512 | tf_op jit(solution)/shard_map/all_gather | solution.py:113
  644.8 29.6 reshape.217
  674.4 9.8 fusion.4
  684.2 10.0 fusion.6
  694.2 24.7 all-gather.16.cloned.1.call-done
  731.5 15.6 fusion.20
  770.4 15.0 reduce-scatter.20.cloned.1.call-done
  786.5 30.7 reduce-scatter.22.cloned.1.call-done
  845.9 11.1 pad_maximum_fusion
  857.1 12.9 fusion.138
  871.0 24.9 fusion.19
  896.0 1993.8 %fusion.2 = f32[48,13824]{1,0:T(8,128)} fusion(f32[1152,13824]{1,0:T(8,128)} %fusion.19), kind=kCustom, calls=%all-reduce-scatter.2 | all-reduce-scatter fusion | flops 21233664 | bytes 66355200
  2907.9 429.5 %fusion.129 = (f32[40,1536]{1,0:T(8,128)S(1)}, f32[40,768]{1,0:T(8,128)S(1)}, f32[40,512]{1,0:T(8,128)S(1)}) fusion(f32[1152,1536]{1,0:T(8,128)} %fusion.62, f32[1152,768]{1,0:T(8,128)} %fusion.86, f32[1152,512]{1,0:T(8,128)} %fusion.85), kind=kCustom, calls=%all-reduce-scatter.4 | all-reduce-scatter fusion | flops 3604481 | bytes 13426688
  3428.1 210.0 %all-reduce.15 = (f32[1152]{0:T(1024)S(1)}, f32[1152]{0:T(1024)S(1)}) all-reduce(f32[1152]{0:T(1024)S(1)} %get-tuple-element.19, f32[1152]{0:T(1024)S(1)} %get-tuple-element.17), channel_id=17, replica_groups=mesh['seq'=8,'fsdp'=4] {'seq','fsdp'}, use_global_device_ids=true, to_apply=%region_27.28.clone | all-reduce | flops 2304 | bytes 18432
  3651.7 96.2 %concatenate.46 = f32[420,13824]{1,0:T(8,128)} concatenate(f32[36,13824]{1,0:T(8,128)} %collective-permute-done.15, f32[48,13824]{1,0:T(8,128)} %collective-permute-done.14, f32[48,13824]{1,0:T(8,128)} %collective-permute-done.13, f32[48,13824]{1,0:T(8,128)} %collective-permute-done.12, f32[48,13824]{1,0:T(8,128)} %collective-permute-done.11, ...), dimensions={0} | concatenate | bytes 46448640
  (441 shorter events, 248.5 us)
Async XLA Ops:
  7.2 400.4 %all-gather.28.cloned.1.call-start = ((), (), s32[]{:S(2)}) async-start(), calls=%async_computation.24 | async-start | bytes 1351680 | tf_op jit(solution)/shard_map/all_gather | solution.py:114
  8.0 402.7 %all-gather.24.cloned.1.call-start = ((), (), s32[]{:S(2)}) async-start(), calls=%async_computation.22 | async-start | bytes 2027520 | tf_op jit(solution)/shard_map/all_gather | solution.py:103
  8.7 407.6 %all-gather.22.cloned.1.call-start = ((), (), s32[]{:S(2)}) async-start(), calls=%async_computation.21 | async-start | bytes 4055040 | tf_op jit(solution)/shard_map/all_gather | solution.py:102
  9.5 475.2 %all-gather.14.cloned.1.call-start = ((), (), s32[]{:S(2)}) async-start(), calls=%async_computation.9 | async-start | bytes 2433024 | tf_op jit(solution)/shard_map/all_gather | solution.py:106
  10.0 479.3 %all-gather.18.cloned.1.call-start = ((), (), s32[]{:S(2)}) async-start(), calls=%async_computation.11 | async-start | bytes 16422912 | tf_op jit(solution)/shard_map/all_gather | solution.py:116
  10.6 490.5 %all-gather.20.cloned.1.call-start = ((), (), s32[]{:S(2)}) async-start(), calls=%async_computation.12 | async-start | bytes 3649536 | tf_op jit(solution)/shard_map/all_gather | solution.py:117
  11.2 633.6 %all-gather.26.cloned.1.call-start = ((), (), s32[]{:S(2)}) async-start(), calls=%async_computation.23 | async-start | bytes 36495360 | tf_op jit(solution)/shard_map/all_gather | solution.py:113
  12.0 707.0 %all-gather.16.cloned.1.call-start = ((), (), s32[]{:S(2)}) async-start(), calls=%async_computation.10 | async-start | bytes 7299072 | tf_op jit(solution)/shard_map/all_gather | solution.py:115
  12.7 772.6 %reduce-scatter.20.cloned.1.call-start = ((), (), s32[]{:S(2)}) async-start(), calls=%async_computation.13 | async-start | bytes 589824 | tf_op jit(solution)/shard_map/reduce_scatter | solution.py:343
  764.8 2881.5 %all-reduce.21.cloned.1.call-start = ((), (), s32[]{:S(2)}) async-start(), calls=%async_computation.26 | async-start | bytes 4718592
  770.3 2980.9 %reduce-scatter.26.cloned.1.call-start = ((), (), s32[]{:S(2)}) async-start(), calls=%async_computation.16 | async-start | bytes 540672 | tf_op jit(solution)/shard_map/reduce_scatter | solution.py:408
  819.4 2931.8 %reduce-scatter.24.cloned.1.call-start = ((), (), s32[]{:S(2)}) async-start(), calls=%async_computation.15 | async-start | bytes 1081344 | tf_op jit(solution)/shard_map/reduce_scatter | solution.py:407
  825.4 2925.8 %reduce-scatter.30.cloned.1.call-start = ((), (), s32[]{:S(2)}) async-start(), calls=%async_computation.18 | async-start | bytes 1081344 | tf_op jit(solution)/shard_map/reduce_scatter | solution.py:410
  827.6 2923.6 %reduce-scatter.28.cloned.1.call-start = ((), (), s32[]{:S(2)}) async-start(), calls=%async_computation.17 | async-start | bytes 4866048 | tf_op jit(solution)/shard_map/reduce_scatter | solution.py:409
  830.6 2920.6 %reduce-scatter.34.cloned.1.call-start = ((), (), s32[]{:S(2)}) async-start(), calls=%async_computation.20 | async-start | bytes 7299072 | tf_op jit(solution)/shard_map/reduce_scatter | solution.py:267
  835.4 2915.9 %reduce-scatter.32.cloned.1.call-start = ((), (), s32[]{:S(2)}) async-start(), calls=%async_computation.19 | async-start | bytes 14598144 | tf_op jit(solution)/shard_map/reduce_scatter | solution.py:265
  857.1 2894.2 %reduce-scatter.36.cloned.1.call-start = ((), (), s32[]{:S(2)}) async-start(), calls=%async_computation.25 | async-start | bytes 32845824
  2893.0 519.0 %collective-permute-start.14 = (f32[48,13824]{1,0:T(8,128)}, f32[48,13824]{1,0:T(8,128)}, u32[]{:S(2)}, u32[]{:S(2)}) collective-permute-start(f32[48,13824]{1,0:T(8,128)} %fusion.2), channel_id=1, source_target_pairs={{0,7},{1,8},{2,9},{3,10},{4,11},{5,12},{6,13},{7,14},{8,15},{9,16}... | collective-permute-start | bytes 7962632
  2894.9 520.0 %collective-permute-start.13 = (f32[48,13824]{1,0:T(8,128)}, f32[48,13824]{1,0:T(8,128)}, u32[]{:S(2)}, u32[]{:S(2)}) collective-permute-start(f32[48,13824]{1,0:T(8,128)} %fusion.2), channel_id=1, source_target_pairs={{0,6},{1,7},{2,8},{3,9},{4,10},{5,11},{6,12},{7,13},{8,14},{9,15},... | collective-permute-start | bytes 7962632
  2896.9 512.8 %collective-permute-start.15 = (f32[36,13824]{1,0:T(8,128)}, f32[36,13824]{1,0:T(8,128)}, u32[]{:S(2)}, u32[]{:S(2)}) collective-permute-start(f32[36,13824]{1,0:T(8,128)} %slice.204), channel_id=1, source_target_pairs={{0,8},{1,9},{2,10},{3,11},{4,12},{5,13},{6,14},{7,15},{8,16},{9,17... | collective-permute-start | bytes 5971976
  3405.8 245.9 %collective-permute-start.12 = (f32[48,13824]{1,0:T(8,128)}, f32[48,13824]{1,0:T(8,128)}, u32[]{:S(2)}, u32[]{:S(2)}) collective-permute-start(f32[48,13824]{1,0:T(8,128)} %fusion.2), channel_id=1, source_target_pairs={{0,5},{1,6},{2,7},{3,8},{4,9},{5,10},{6,11},{7,12},{8,13},{9,14},{... | collective-permute-start | bytes 7962632
  3407.7 243.9 %collective-permute-start.11 = (f32[48,13824]{1,0:T(8,128)}, f32[48,13824]{1,0:T(8,128)}, u32[]{:S(2)}, u32[]{:S(2)}) collective-permute-start(f32[48,13824]{1,0:T(8,128)} %fusion.2), channel_id=1, source_target_pairs={{0,4},{1,5},{2,6},{3,7},{4,8},{5,9},{6,10},{7,11},{8,12},{9,13},{1... | collective-permute-start | bytes 7962632
  3409.7 242.0 %collective-permute-start.10 = (f32[48,13824]{1,0:T(8,128)}, f32[48,13824]{1,0:T(8,128)}, u32[]{:S(2)}, u32[]{:S(2)}) collective-permute-start(f32[48,13824]{1,0:T(8,128)} %fusion.2), channel_id=1, source_target_pairs={{0,3},{1,4},{2,5},{3,6},{4,7},{5,8},{6,9},{7,10},{8,11},{9,12},{10... | collective-permute-start | bytes 7962632
  3412.1 239.6 %collective-permute-start.9 = (f32[48,13824]{1,0:T(8,128)}, f32[48,13824]{1,0:T(8,128)}, u32[]{:S(2)}, u32[]{:S(2)}) collective-permute-start(f32[48,13824]{1,0:T(8,128)} %fusion.2), channel_id=1, source_target_pairs={{0,2},{1,3},{2,4},{3,5},{4,6},{5,7},{6,8},{7,9},{8,10},{9,11},{10,... | collective-permute-start | bytes 7962632
  (128 other events, 8323.5 us)
Sparse Core Ops, SparseCore 0:
  10.9 54.7 all-gather.27
  68.6 55.1 all-gather.23
  126.6 63.2 all-gather.21
  192.6 55.2 all-gather.13
  250.7 118.8 all-gather.17
  372.4 58.6 all-gather.19
  433.9 210.8 all-gather.25
  647.7 71.2 all-gather.15
  761.0 24.2 reduce-scatter.19
  788.1 29.1 reduce-scatter.21
  823.0 145.5 all-reduce.20
  971.3 136.4 reduce-scatter.25
  1110.6 136.7 reduce-scatter.23
  1250.2 133.0 reduce-scatter.29
  1389.2 134.6 reduce-scatter.27
  1530.9 140.8 reduce-scatter.33
  1678.3 201.4 reduce-scatter.31
  1886.6 392.5 reduce-scatter.35
where the time goes:
time: 3770 us; the launch traced here: 3760 us
  blocking collectives  3070 us (81%)
  waiting for transfers between devices  240 us (6%)
  matrix products  179 us (5%)
  local copies, waits for them, and re-layouts  170 us (5%)
  starting transfers between devices  57.6 us (2%)
    unnamed x4, blocking collectives  2670 us
    unnamed x254, local copies, waits for them, and re-layouts  163 us
    all_gather x1, waiting for transfers between devices, shards(): lax.all_gather(shared_gateup_weight, ('seq', 'fsdp'), axis=0, tiled=True)  137 us
    all_gather x1, blocking collectives, shards(): lax.all_gather(outproj_adapter_a, ('seq', 'fsdp'), axis=0, tiled=True)  77 us
  transfers between devices with their start and end apart: 38, of which 11 were waited for; matrix products, arithmetic and copies ran while one was open for 73% of the time, Pallas kernels for 0%

commit v1 on v0

v1 whole, which is shorter than its diff:
```python
import functools
import math

import jax
import jax.numpy as jnp
from jax import lax
from jax.experimental import pallas as pl
from jax.experimental.pallas import tpu as pltpu
from jax.sharding import PartitionSpec as P

HEADS = 4
HEAD = 256
RANK = 256
EPSILON = 1e-06
ROPE_BASE = 10000.0
MASKED = -1e30
MESH = pl.DeviceIdType.MESH
BF = jnp.bfloat16
F32 = jnp.float32


def mm(left, right):
    return jnp.dot(left, right, preferred_element_type=F32)


def mm_tn(left, right):
    return lax.dot_general(left, right, (((0,), (0,)), ((), ())), preferred_element_type=F32)


def mm_nt(left, right):
    return lax.dot_general(left, right, (((1,), (1,)), ((), ())), preferred_element_type=F32)


def greet(peers):
    barrier = pltpu.get_barrier_semaphore()
    for peer in peers:
        pl.semaphore_signal(barrier, inc=1, device_id=peer, device_id_type=MESH)
    pl.semaphore_wait(barrier, len(peers))


def exchange_kernel(axis, size, count, *refs):
    xs, os = refs[:count], refs[count : 2 * count]
    local, send, recv = refs[2 * count :]
    me = lax.axis_index(axis)
    greet([{axis: lax.rem(me + k, size)} for k in range(1, size)])
    copies = []
    for k in range(1, size):
        peer = lax.rem(me + k, size)
        for a in range(count):
            copy = pltpu.make_async_remote_copy(
                src_ref=xs[a].at[peer],
                dst_ref=os[a].at[me],
                send_sem=send.at[a, k],
                recv_sem=recv.at[a, k],
                device_id={axis: peer},
                device_id_type=MESH,
            )
            copy.start()
            copies.append(copy)
    for a in range(count):
        copy = pltpu.make_async_copy(xs[a].at[me], os[a].at[me], local.at[a])
        copy.start()
        copies.append(copy)
    for copy in copies:
        copy.wait()


def exchange(arrays, axis, size, collective_id):
    count = len(arrays)
    any_spec = pl.BlockSpec(memory_space=pl.ANY)
    return pl.pallas_call(
        functools.partial(exchange_kernel, axis, size, count),
        out_shape=[jax.ShapeDtypeStruct(a.shape, a.dtype) for a in arrays],
        in_specs=[any_spec] * count,
        out_specs=[any_spec] * count,
        scratch_shapes=[
            pltpu.SemaphoreType.DMA((count,)),
            pltpu.SemaphoreType.DMA((count, size)),
            pltpu.SemaphoreType.DMA((count, size)),
        ],
        compiler_params=pltpu.CompilerParams(collective_id=collective_id, has_side_effects=True),
    )(*arrays)


def spread_kernel(axis, size, count, *refs):
    xs, os = refs[:count], refs[count : 2 * count]
    local, send, recv = refs[2 * count :]
    me = lax.axis_index(axis)
    greet([{axis: lax.rem(me + k, size)} for k in range(1, size)])
    copies = []
    for k in range(1, size):
        peer = lax.rem(me + k, size)
        for a in range(count):
            copy = pltpu.make_async_remote_copy(
                src_ref=xs[a],
                dst_ref=os[a].at[me],
                send_sem=send.at[a, k],
                recv_sem=recv.at[a, k],
                device_id={axis: peer},
                device_id_type=MESH,
            )
            copy.start()
            copies.append(copy)
    for a in range(count):
        copy = pltpu.make_async_copy(xs[a], os[a].at[me], local.at[a])
        copy.start()
        copies.append(copy)
    for copy in copies:
        copy.wait()


def spread(arrays, axis, size, collective_id):
    count = len(arrays)
    any_spec = pl.BlockSpec(memory_space=pl.ANY)
    return pl.pallas_call(
        functools.partial(spread_kernel, axis, size, count),
        out_shape=[jax.ShapeDtypeStruct((size,) + a.shape, a.dtype) for a in arrays],
        in_specs=[any_spec] * count,
        out_specs=[any_spec] * count,
        scratch_shapes=[
            pltpu.SemaphoreType.DMA((count,)),
            pltpu.SemaphoreType.DMA((count, size)),
            pltpu.SemaphoreType.DMA((count, size)),
        ],
        compiler_params=pltpu.CompilerParams(collective_id=collective_id, has_side_effects=True),
    )(*arrays)


def line_gather_kernel(line, count, *refs):
    xs, os = refs[:count], refs[count : 2 * count]
    local, send, recv = refs[2 * count :]
    s = lax.axis_index("seq")
    base = s // line * line
    n2 = line // 2
    i = s - base
    p, core = i // 2, lax.rem(i, 2)
    sib = s + 1 - 2 * core
    left = base + lax.rem(i + line - 2, line)
    right = base + lax.rem(i + 2, line)
    greet([{"seq": d} for d in ([left, right, sib] if n2 > 2 else [right, sib])])

    def copy(a, blk, src, dst, k):
        return pltpu.make_async_remote_copy(
            src_ref=src,
            dst_ref=os[a].at[blk],
            send_sem=send.at[a, k],
            recv_sem=recv.at[a, blk],
            device_id={"seq": dst},
            device_id_type=MESH,
        )

    for a in range(count):

        @pl.when(p < n2 - 1)
        def _(a=a):
            copy(a, i, xs[a], right, 0).start()

        @pl.when(p > 0)
        def _(a=a):
            copy(a, i, xs[a], left, 1).start()

        copy(a, i, xs[a], sib, 2).start()
        pltpu.make_async_copy(xs[a], os[a].at[i], local.at[a]).start()
    for d in range(1, n2):
        for a in range(count):

            @pl.when(p - d >= 0)
            def _(a=a, d=d):
                blk = i - 2 * d
                copy(a, blk, os[a].at[blk], left, 0).wait_recv()

                @pl.when(p < n2 - 1)
                def _():
                    copy(a, blk, os[a].at[blk], right, 4 * d).start()

                copy(a, blk, os[a].at[blk], sib, 4 * d + 1).start()

            @pl.when(p + d < n2)
            def _(a=a, d=d):
                blk = i + 2 * d
                copy(a, blk, os[a].at[blk], right, 0).wait_recv()

                @pl.when(p > 0)
                def _():
                    copy(a, blk, os[a].at[blk], left, 4 * d + 2).start()

                copy(a, blk, os[a].at[blk], sib, 4 * d + 3).start()

    for a in range(count):
        for q in range(n2):
            blk = 2 * q + 1 - core
            copy(a, blk, os[a].at[blk], sib, 0).wait_recv()

        def sent(k, a=a):
            copy(a, i, xs[a], sib, k).wait_send()

        @pl.when(p < n2 - 1)
        def _():
            sent(0)

        @pl.when(p > 0)
        def _():
            sent(1)

        sent(2)
        for d in range(1, n2):

            @pl.when(p - d >= 0)
            def _(d=d):
                @pl.when(p < n2 - 1)
                def _():
                    sent(4 * d)

                sent(4 * d + 1)

            @pl.when(p + d < n2)
            def _(d=d):
                @pl.when(p > 0)
                def _():
                    sent(4 * d + 2)

                sent(4 * d + 3)

        pltpu.make_async_copy(xs[a], os[a].at[i], local.at[a]).wait()


def line_gather(arrays, line, collective_id):
    count = len(arrays)
    any_spec = pl.BlockSpec(memory_space=pl.ANY)
    return pl.pallas_call(
        functools.partial(line_gather_kernel, line, count),
        out_shape=[jax.ShapeDtypeStruct((line,) + a.shape, a.dtype) for a in arrays],
        in_specs=[any_spec] * count,
        out_specs=[any_spec] * count,
        scratch_shapes=[
            pltpu.SemaphoreType.DMA((count,)),
            pltpu.SemaphoreType.DMA((count, 2 * line)),
            pltpu.SemaphoreType.DMA((count, line)),
        ],
        compiler_params=pltpu.CompilerParams(collective_id=collective_id, has_side_effects=True),
    )(*arrays)


def line_sum_kernel(line, x_ref, o_ref, mine, from_sib, from_left, from_right, send, recv):
    s = lax.axis_index("seq")
    base = s // line * line
    n2 = line // 2
    i = s - base
    p, core = i // 2, lax.rem(i, 2)
    sib = s + 1 - 2 * core
    left = base + lax.rem(i + line - 2, line)
    right = base + lax.rem(i + 2, line)
    greet([{"seq": d} for d in ([left, right, sib] if n2 > 2 else [right, sib])])

    def hand_over(q):
        return pltpu.make_async_remote_copy(
            src_ref=x_ref.at[2 * q + 1 - core],
            dst_ref=from_sib.at[q],
            send_sem=send.at[q],
            recv_sem=recv.at[q],
            device_id={"seq": sib},
            device_id_type=MESH,
        )

    def rightward(q):
        return pltpu.make_async_remote_copy(
            src_ref=mine.at[q],
            dst_ref=from_left.at[q],
            send_sem=send.at[n2 + q],
            recv_sem=recv.at[n2 + q],
            device_id={"seq": right},
            device_id_type=MESH,
        )

    def leftward(q):
        return pltpu.make_async_remote_copy(
            src_ref=mine.at[q],
            dst_ref=from_right.at[q],
            send_sem=send.at[2 * n2 + q],
            recv_sem=recv.at[2 * n2 + q],
            device_id={"seq": left},
            device_id_type=MESH,
        )

    order = [q for k in range(n2) for q in ((n2 - 1 - k, k) if n2 - 1 - k > k else (k,) if n2 - 1 - k == k else ())]
    for q in order:
        hand_over(q).start()

    def add(q, other):
        mine[q] = (mine[q].astype(F32) + other[q].astype(F32)).astype(BF)

    for q in order:
        hand_over(q).wait_recv()
        mine[q] = (x_ref[2 * q + core].astype(F32) + from_sib[q].astype(F32)).astype(BF)

        @pl.when((q > p) & (p == 0))
        def _(q=q):
            rightward(q).start()

        @pl.when((q < p) & (p == n2 - 1))
        def _(q=q):
            leftward(q).start()

    for k in range(n2 - 1):
        q = n2 - 1 - k

        @pl.when((p > 0) & (p < q))
        def _(q=q):
            rightward(q).wait_recv()
            add(q, from_left)
            rightward(q).start()

        q = k

        @pl.when((p < n2 - 1) & (p > q))
        def _(q=q):
            leftward(q).wait_recv()
            add(q, from_right)
            leftward(q).start()

    for q in range(n2):

        @pl.when((p == q) & (p > 0))
        def _(q=q):
            rightward(q).wait_recv()

        @pl.when((p == q) & (p < n2 - 1))
        def _(q=q):
            leftward(q).wait_recv()

        @pl.when(p == q)
        def _(q=q):
            total = mine[q].astype(F32)
            if q > 0:
                total += from_left[q].astype(F32)
            if q < n2 - 1:
                total += from_right[q].astype(F32)
            o_ref[...] = total

    for q in range(n2):
        hand_over(q).wait_send()

        @pl.when(q > p)
        def _(q=q):
            rightward(q).wait_send()

        @pl.when(q < p)
        def _(q=q):
            leftward(q).wait_send()


def line_sum(x, line, collective_id):
    blk = x.shape[1:]
    vmem = pl.BlockSpec(memory_space=pltpu.VMEM)
    n2 = line // 2
    return pl.pallas_call(
        functools.partial(line_sum_kernel, line),
        out_shape=jax.ShapeDtypeStruct(blk, F32),
        in_specs=[vmem],
        out_specs=vmem,
        scratch_shapes=[pltpu.VMEM((n2,) + blk, BF)] * 4
        + [pltpu.SemaphoreType.DMA((3 * n2,)), pltpu.SemaphoreType.DMA((3 * n2,))],
        compiler_params=pltpu.CompilerParams(
            collective_id=collective_id, has_side_effects=True, vmem_limit_bytes=48 << 20
        ),
    )(x)


def norm_apply(hidden, gain):
    return hidden * lax.rsqrt(jnp.mean(hidden * hidden, axis=-1, keepdims=True) + EPSILON) * gain


def rope_tables(positions):
    half = HEAD // 2
    spacing = jnp.exp(-(2.0 * jnp.arange(half).astype(F32) / HEAD) * math.log(ROPE_BASE))
    angle = positions.astype(F32)[..., None] * spacing
    return jnp.cos(angle), jnp.sin(angle)


def rotate(values, cosine, sine):
    half = values.shape[-1] // 2
    a, b = values[..., :half], values[..., half:]
    return jnp.concatenate([a * cosine - b * sine, b * cosine + a * sine], axis=-1)


def unrotate(grads, cosine, sine):
    half = grads.shape[-1] // 2
    a, b = grads[..., :half], grads[..., half:]
    return jnp.concatenate([a * cosine + b * sine, b * cosine - a * sine], axis=-1)


def shards(
    S,
    F,
    layer_input,
    document_numbers,
    cotangent,
    w_qkv,
    qkv_a,
    q_b,
    kv_b,
    w_out,
    out_a,
    out_b,
    w_gu,
    gu_a,
    gu_b,
    w_down,
    down_a,
    down_b,
    gain_a,
    gain_f,
):
    R, seg, width = layer_input.shape
    L = seg * S
    own = R * seg
    G = S // R
    C = G // HEADS
    scale = HEAD**-0.5
    kb = w_qkv.shape[0]
    rb = q_b.shape[0]
    hb = w_down.shape[0]
    ob = w_out.shape[0]
    hidden = w_gu.shape[1] // 2
    hl = hidden // S
    s = lax.axis_index("seq")
    r = s // G
    head = lax.rem(s, G) // C
    chunk = lax.rem(s, C)
    qlen = L // C

    gains = jnp.pad(jnp.stack([gain_a, gain_f], axis=1), ((0, 0), (0, 126)))
    pack1 = jnp.concatenate([w_qkv, qkv_a, gu_a, gains], axis=1)
    pack2 = jnp.concatenate([q_b, kv_b[0], kv_b[1], out_b, down_b], axis=1)
    pack3 = jnp.concatenate([w_out, out_a], axis=1)
    p1, p2, p3 = spread([pack1, pack2, pack3], "fsdp", F, 0)
    ids = jnp.pad(document_numbers[:, None, :], ((0, 0), (0, 7), (0, 128 - seg)))
    p1, p2, p3, xin, cot, ids = line_gather([p1, p2, p3, layer_input, cotangent, ids], S, 1)
    p1 = p1.reshape(width, -1)
    p2 = p2.reshape(RANK, -1)
    p3 = p3.reshape(HEADS, HEAD, -1)
    xrow = lax.dynamic_index_in_dim(xin, r, 1, keepdims=False).reshape(L, width).astype(F32)
    cot = cot.transpose(1, 0, 2, 3).reshape(R * L, width)
    ids = lax.dynamic_index_in_dim(ids[:, :, 0, :seg], r, 1, keepdims=False).reshape(L)

    gw = jnp.concatenate(
        [w_gu[:, :hidden].reshape(kb, S, hl), w_gu[:, hidden:].reshape(kb, S, hl)], axis=2
    ).transpose(1, 0, 2)
    gb = jnp.concatenate([gu_b[0].reshape(rb, S, hl), gu_b[1].reshape(rb, S, hl)], axis=2).transpose(
        1, 0, 2
    )
    gw, gb = exchange([gw, gb], "seq", S, 2)
    dw = jnp.concatenate([w_down, down_a], axis=1)
    gw, gb, dw = spread([gw, gb, dw], "fsdp", F, 3)
    gw = gw.transpose(1, 0, 2, 3).reshape(width, 2 * hl)
    gb = gb.transpose(1, 0, 2, 3).reshape(RANK, 2 * hl)
    dw = dw.reshape(hl, -1)

    q0 = HEADS * HEAD
    wq = lax.dynamic_slice_in_dim(p1, head * HEAD, HEAD, 1)
    w1 = jnp.concatenate([wq, p1[:, q0 : q0 + 2 * HEAD + 3 * RANK]], axis=1)
    at = q0 + 2 * HEAD + 3 * RANK
    f_gu_a = p1[:, at : at + 2 * RANK]
    gain_one = p1[:, at + 2 * RANK].astype(F32)
    gain_two = p1[:, at + 2 * RANK + 1].astype(F32)
    f_q_b = lax.dynamic_slice_in_dim(p2, head * HEAD, HEAD, 1)
    f_k_b = p2[:, q0 : q0 + HEAD]
    f_v_b = p2[:, q0 + HEAD : q0 + 2 * HEAD]
    f_out_b = p2[:, q0 + 2 * HEAD : q0 + 2 * HEAD + width]
    f_down_b = p2[:, q0 + 2 * HEAD + width :]
    wo = lax.dynamic_index_in_dim(p3, head, 0, keepdims=False)

    place = jnp.arange(L, dtype=jnp.int32)
    same = ids[:, None] == ids[None, :]
    before = place[None, :] < place[:, None]
    positions = jnp.sum((same & before).astype(jnp.int32), axis=1)
    allowed = same & (place[None, :] <= place[:, None])
    cosine, sine = rope_tables(positions)
    norm_one = norm_apply(xrow, gain_one).astype(BF)
    pu = mm(norm_one, w1)
    u = pu[:, 3 * HEAD :].astype(BF)
    u_q, u_k, u_v = u[:, :RANK], u[:, RANK : 2 * RANK], u[:, 2 * RANK :]
    query = rotate(pu[:, :HEAD] + mm(u_q, f_q_b), cosine, sine).astype(BF)
    key = rotate(pu[:, HEAD : 2 * HEAD] + mm(u_k, f_k_b), cosine, sine).astype(BF)
    value = (pu[:, 2 * HEAD : 3 * HEAD] + mm(u_v, f_v_b)).astype(BF)
    if C > 1:
        query_c = lax.dynamic_slice_in_dim(query, chunk * qlen, qlen, 0)
        allowed = lax.dynamic_slice_in_dim(allowed, chunk * qlen, qlen, 0)
    else:
        query_c = query
    scores = jnp.where(allowed, mm_nt(query_c, key) * scale, MASKED)
    top = jnp.max(scores, axis=-1, keepdims=True)
    lse = top + jnp.log(jnp.sum(jnp.exp(scores - top), axis=-1, keepdims=True))
    probs = jnp.where(allowed, jnp.exp(scores - lse), 0.0)
    probs_low = probs.astype(BF)
    mixed = mm(probs_low, value).astype(BF)
    part = mm(mixed, wo).astype(BF)
    if C > 1:
        part = lax.dynamic_update_slice_in_dim(jnp.zeros((L, part.shape[1]), BF), part, chunk * qlen, 0)
    attn = line_sum(part.reshape(G, own, -1), G, 4)
    u_out = attn[:, width:].astype(BF)
    mine = lax.rem(s, G) * own
    x_own = lax.dynamic_slice_in_dim(xrow, mine, own, 0)
    resid = x_own + attn[:, :width] + mm(u_out, f_out_b)
    norm_two_own = norm_apply(resid, gain_two).astype(BF)
    (norm_two,) = line_gather([norm_two_own], S, 5)
    norm_two = norm_two.reshape(R * L, width)

    u_gu = mm(norm_two, f_gu_a).astype(BF)
    gu = mm(norm_two, gw)
    gate = gu[:, :hl] + mm(u_gu[:, :RANK], gb[:, :hl])
    up = gu[:, hl:] + mm(u_gu[:, RANK:], gb[:, hl:])
    d_u_down = mm_nt(cot, f_down_b).astype(BF)
    cot_u = jnp.concatenate([cot, d_u_down], axis=1)
    d_act = mm_nt(cot_u, dw)
    inner = math.sqrt(2.0 / math.pi)
    th = jnp.tanh(inner * (gate + 0.044715 * gate * gate * gate))
    gelu = 0.5 * gate * (1.0 + th)
    act = (gelu * up).astype(BF)
    slope = 0.5 * (1.0 + th) + 0.5 * gate * (1.0 - th * th) * inner * (1.0 + 3 * 0.044715 * gate * gate)
    d_gate = (d_act * up * slope).astype(BF)
    d_up = (d_act * gelu).astype(BF)
    d_gu = jnp.concatenate([d_gate, d_up], axis=1)
    d_u_gu = jnp.concatenate(
        [mm_nt(d_gate, gb[:, :hl]), mm_nt(d_up, gb[:, hl:])], axis=1
    ).astype(BF)
    d_norm_two = (mm_nt(d_gu, gw) + mm_nt(d_u_gu, f_gu_a)).astype(BF)
    d_norm_two = line_sum(d_norm_two.reshape(S, own, width), S, 6)
    ffn = mm(act, dw)
    u_down = ffn[:, width:].astype(BF)
    ffn = (ffn[:, :width] + mm(u_down, f_down_b)).astype(BF)
    ffn = line_sum(ffn.reshape(S, own, width), S, 7)
    activations = (resid + ffn).astype(BF)
    g_down = mm_tn(act, cot_u)
    g_down_b = mm_tn(u_down, cot)
    g_gu = mm_tn(norm_two, d_gu)
    g_gu_b = jnp.concatenate([mm_tn(u_gu[:, :RANK], d_gate), mm_tn(u_gu[:, RANK:], d_up)], axis=1)
    g_gu_a = mm_tn(norm_two, d_u_gu)

    def norm_back(G_in, h, g):
        q = lax.rsqrt(jnp.mean(h * h, axis=-1, keepdims=True) + EPSILON)
        gg = G_in * g
        d_gain = jnp.sum(G_in * (h * q), axis=0)
        return d_gain, q * gg - h * (q * q * q) * jnp.mean(gg * h, axis=-1, keepdims=True)

    d_gain_two, back = norm_back(d_norm_two, resid, gain_two)
    cot_own = lax.dynamic_slice_in_dim(cot, s * own, own, 0)
    d_resid = cot_own.astype(F32) + back

    d_attn_own = d_resid.astype(BF)
    (d_attn,) = line_gather([d_attn_own], G, 8)
    d_attn = d_attn.reshape(L, width)
    g_out_b = mm_tn(u_out, d_attn_own)
    if C > 1:
        d_attn = lax.dynamic_slice_in_dim(d_attn, chunk * qlen, qlen, 0)
    d_u_out = mm_nt(d_attn, f_out_b).astype(BF)
    d_attn_u = jnp.concatenate([d_attn, d_u_out], axis=1)
    d_mixed = mm_nt(d_attn_u, wo).astype(BF)
    g_out = mm_tn(mixed, d_attn_u)
    d_probs = mm_nt(d_mixed, value)
    delta = jnp.sum(probs * d_probs, axis=-1, keepdims=True)
    d_scores = (probs * (d_probs - delta)).astype(BF)
    d_query = mm(d_scores, key) * scale
    d_key = mm_tn(d_scores, query_c) * scale
    d_value = mm_tn(probs_low, d_mixed)
    if C > 1:
        d_query = lax.dynamic_update_slice_in_dim(jnp.zeros((L, HEAD), F32), d_query, chunk * qlen, 0)
    dq = unrotate(d_query, cosine, sine).astype(BF)
    dk = unrotate(d_key, cosine, sine).astype(BF)
    dv = d_value.astype(BF)
    d_u = [mm_nt(dq, f_q_b).astype(BF), mm_nt(dk, f_k_b).astype(BF), mm_nt(dv, f_v_b).astype(BF)]
    d_pu = jnp.concatenate([dq, dk, dv] + d_u, axis=1)
    d_norm_one = mm_nt(d_pu, w1).astype(BF)
    d_norm_one = line_sum(d_norm_one.reshape(G, own, width), G, 9)
    g_w1 = mm_tn(norm_one, d_pu)
    g_q_b = mm_tn(u_q, dq)
    g_kv_b = [mm_tn(u_k, dk), mm_tn(u_v, dv)]
    d_gain_one, back_one = norm_back(d_norm_one, x_own, gain_one)
    grad_input = d_resid + back_one

    per = own // seg
    outs = [activations.reshape(per, seg, width), grad_input.reshape(per, seg, width)]
    moved = []
    for o in outs:
        full = jnp.zeros((S,) + o.shape[1:], o.dtype)
        moved.append(lax.dynamic_update_slice_in_dim(full, o, lax.rem(s, G) * per, 0))
    moved = exchange(moved, "seq", S, 10)
    src = s // per
    pick = []
    for m in moved:
        rows = [lax.dynamic_index_in_dim(m, row * G + src, 0, keepdims=False) for row in range(R)]
        pick.append(jnp.stack(rows))
    activations, grad_input = pick

    def split(g, rows):
        return g.astype(BF).reshape(-1, F, rows, g.shape[1]).transpose(1, 0, 2, 3)

    d_gains = jnp.pad(jnp.stack([d_gain_one, d_gain_two], axis=1), ((0, 0), (0, 126)))
    parts = [
        split(g_w1[:, :HEAD], kb),
        split(jnp.concatenate([g_w1[:, HEAD:], g_gu_a, d_gains], axis=1), kb),
        split(g_gu, kb),
        split(g_gu_b, rb),
        split(g_q_b, rb),
        split(jnp.concatenate(g_kv_b + [g_out_b, g_down_b], axis=1), rb),
        split(g_out, ob),
        g_down.astype(BF).reshape(F, 1, hb, -1),
    ]
    parts = exchange(parts, "fsdp", F, 11)
    parts = [jnp.sum(g.astype(F32), axis=0) for g in parts]
    g_down = parts.pop()[0]
    parts = [g.astype(BF) for g in parts]
    per_head = S // HEADS
    g_out = parts[6]
    full = jnp.zeros((S,) + g_out.shape[1:], BF)
    parts[6] = lax.dynamic_update_slice_in_dim(full, g_out, head * per_head, 0)
    t_q, t_1, t_gu, t_gb, t_qb, t_2, t_out = exchange(parts, "seq", S, 12)

    def by_head(t):
        t = t.astype(F32).reshape(R, HEADS, C, t.shape[1], HEAD).sum(axis=(0, 2))
        return t.transpose(1, 0, 2).reshape(t.shape[1], HEADS * HEAD)

    def halves(t):
        t = t.astype(F32).reshape(S, t.shape[1], 2, hl).transpose(2, 1, 0, 3)
        return t.reshape(2, t.shape[1], hidden)

    t_1 = jnp.sum(t_1.astype(F32), axis=0)
    t_2 = jnp.sum(t_2.astype(F32), axis=0)
    grad_w_qkv = jnp.concatenate([by_head(t_q), t_1[:, : 2 * HEAD]], axis=1)
    g_qkv_a = t_1[:, 2 * HEAD : 2 * HEAD + 3 * RANK]
    g_gu_a = t_1[:, 2 * HEAD + 3 * RANK : 2 * HEAD + 5 * RANK]
    d_gain_one = t_1[:, 2 * HEAD + 5 * RANK]
    d_gain_two = t_1[:, 2 * HEAD + 5 * RANK + 1]
    g_gu = halves(t_gu)
    g_out = jnp.sum(t_out.astype(F32), axis=0)
    return (
        activations,
        grad_input,
        grad_w_qkv,
        g_qkv_a,
        by_head(t_qb),
        jnp.stack([t_2[:, :HEAD], t_2[:, HEAD : 2 * HEAD]]),
        g_out[:, :width],
        g_out[:, width:],
        t_2[:, 2 * HEAD : 2 * HEAD + width],
        jnp.concatenate([g_gu[0], g_gu[1]], axis=1),
        g_gu_a,
        halves(t_gb),
        g_down[:, :width],
        g_down[:, width:],
        t_2[:, 2 * HEAD + width :],
        d_gain_one,
        d_gain_two,
    )


def solution(mesh):
    both = P(("seq", "fsdp"), None)
    second = P(None, ("seq", "fsdp"), None)
    tokens = P("fsdp", "seq", None)
    gain = P(("seq", "fsdp"))
    return jax.shard_map(
        functools.partial(shards, mesh.shape["seq"], mesh.shape["fsdp"]),
        mesh=mesh,
        in_specs=(tokens, P("fsdp", "seq"), tokens)
        + (both, both, both, second, both, both, both, both, both, second, both, both, both, gain, gain),
        out_specs=(tokens, tokens)
        + (both, both, both, second, both, both, both, both, both, second, both, both, both, gain, gain),
        check_vma=False,
    )
```

time: 3770 us -> 1040 us (0.28)
  blocking collectives: 3070 us -> 0 us
  Pallas kernels: 0 us -> 753 us
  waiting for transfers between devices: 240 us -> 0 us
  matrix products: 179 us -> 102 us
  starting transfers between devices: 57.6 us -> 0 us
  local copies, waits for them, and re-layouts: 170 us -> 128 us
    unnamed x4 -> x0, blocking collectives: 2670 us -> none
    pallas_call x0 -> x13, Pallas kernels: none -> 753 us  [the longest x4 376 us: exchange(): pl.pallas_call(functools.partial(exchange_kernel, axis, size, count), out...]
    all_gather x8 -> x0, blocking collectives: 399 us -> none  [the longest x1 77 us: shards(): lax.all_gather(outproj_adapter_a, ('seq', 'fsdp'), axis=0, tiled=True)]
    all_gather x8 -> x0, waiting for transfers between devices: 162 us -> none  [the longest x1 137 us: shards(): lax.all_gather(shared_gateup_weight, ('seq', 'fsdp'), axis=0, tiled=True)]
    unnamed x254 -> x173, local copies, waits for them, and re-layouts: 163 us -> 19.6 us
    dot_general x58 -> x42, matrix products: 179 us -> 102 us  [the longest x14 44.4 us: mm(): return jnp.dot(left, right, preferred_element_type=F32)]
    unnamed x22 -> x0, starting transfers between devices: 56.8 us -> none
    reduce_scatter x8 -> x0, waiting for transfers between devices: 45.7 us -> none  [the longest x1 30.7 us: shards(): lax.psum_scatter(jnp.stack(value_terms).astype(jnp.bfloat16), 'seq', scat...]
  transfers between devices with their start and end apart: 38 -> 0, of which waited for: 11 -> 0; matrix products, arithmetic and copies ran while one was open for 73% -> 0% of each run, Pallas kernels for 0% -> 0%
where the time goes in v1:
time: 1040 us
  Pallas kernels  753 us (72%)
  local copies, waits for them, and re-layouts  128 us (12%)
  matrix products  102 us (10%)
  other arithmetic  54 us (5%)
    pallas_call x4, Pallas kernels, exchange(): pl.pallas_call(functools.partial(exchange_kernel, axis, size, count), out...  376 us
    pallas_call x3, Pallas kernels, line_gather(): pl.pallas_call(functools.partial(line_gather_kernel, line, count), out_sh...  174 us
    pallas_call x2, Pallas kernels, spread(): pl.pallas_call(functools.partial(spread_kernel, axis, size, count), out_s...  109 us
    pallas_call x4, Pallas kernels, line_sum(): pl.pallas_call(functools.partial(line_sum_kernel, line), out_shape=jax.Sh...  94.1 us
    dot_general x14, matrix products, mm(): return jnp.dot(left, right, preferred_element_type=F32)  44.4 us
    dot_general x14, matrix products, mm_tn(): lax.dot_general(left, right, (((0,), (0,)), ((), ())), preferred_element_...  33.7 us
    dot_general x14, matrix products, mm_nt(): lax.dot_general(left, right, (((1,), (1,)), ((), ())), preferred_element_...  23.6 us

profile of v1, /device:TPU:17, one launch (start us, length us, event | category | flops | bytes accessed | tf_op | source)
XLA Modules:
  0.0 1038.7 jit_solution(5647310814167484939)
XLA Ops:
  8.3 20.7 %shard_map.305 = (bf16[4,36,2944]{2,1,0:T(8,128)(2,1)}, bf16[4,8,3840]{2,1,0:T(8,128)(2,1)}, bf16[4,32,1408]{2,1,0:T(8,128)(2,1)}) custom-call(bf16[36,2944]{1,0:T(8,128)(2,1)} %fusion.77.refs_0_, bf16[8,3840]{1,0:T(8,128)(2,1)} %copy-done.64, bf16[32,1408]{1,0:T(8,128)(2,1)} %pad_maximum_fusion.33.refs_2_), custom_call_target="tpu_custom_call" | custom-call | tf_op jit(solution)/shard_map/pallas_call | solution.py:115
  30.3 140.3 %shard_map.306 = (bf16[8,4,36,2944]{3,2,1,0:T(8,128)(2,1)}, bf16[8,4,8,3840]{3,2,1,0:T(8,128)(2,1)}, bf16[8,4,32,1408]{3,2,1,0:T(8,128)(2,1)}, bf16[8,2,64,1152]...) custom-call(bf16[4,36,2944]{2,1,0:T(8,128)(2,1)} %get-tuple-element.48.refs_0_, ...), custom_call_target="tpu_custom_call" | custom-call | tf_op jit(solution)/shard_map/pallas_call | solution.py:230
  173.0 9.0 reshape.262
  204.7 16.5 %shard_map.307 = f32[128,1408]{1,0:T(8,128)S(1)} custom-call(bf16[4,128,1408]{2,1,0:T(8,128)(2,1)S(1)} %bitcast.124), custom_call_target="tpu_custom_call" | custom-call | tf_op jit(solution)/shard_map/pallas_call | solution.py:356
  224.3 21.1 %shard_map.308 = bf16[8,128,1152]{2,1,0:T(8,128)(2,1)} custom-call(bf16[128,1152]{1,0:T(8,128)(2,1)} %multiply_convert_fusion.4.refs_0_), custom_call_target="tpu_custom_call" | custom-call | tf_op jit(solution)/shard_map/pallas_call | solution.py:230
  254.7 37.1 %shard_map.309 = (bf16[8,36,1728]{2,1,0:T(8,128)(2,1)}, bf16[8,8,1728]{2,1,0:T(8,128)(2,1)}) custom-call(bf16[8,36,1728]{2,1,0:T(8,128)(2,1)} %maximum_bitcast_fusion.2.refs_0_, bf16[8,8,1728]{2,1,0:T(8,128)(2,1)} %maximum_bitcast_fusion.3.refs_1_), custom_call_target="tpu_custom_call" | custom-call | tf_op jit(solution)/shard_map/pallas_call | solution.py:71
  292.6 87.9 %shard_map.310 = (bf16[4,8,36,1728]{3,2,1,0:T(8,128)(2,1)}, bf16[4,8,8,1728]{3,2,1,0:T(8,128)(2,1)}, bf16[4,216,1408]{2,1,0:T(8,128)(2,1)}) custom-call(bf16[8,36,1728]{2,1,0:T(8,128)(2,1)} %get-tuple-element.56.refs_0_, bf16[8,8,1728]{2,1,0:T(8,128)(2,1)} %get-tuple-element.57.refs_1_, bf16[216,1408]{1,0:T(8,128)(2,1)} %pad_maximum_fusion.17.refs_2_), custom_call_target="tpu_custom_call" | custom-call | tf_op jit(solution)/shard_map/pallas_call | solution.py:115
  385.3 7.7 reshape.269
  393.0 7.3 fusion.119
  409.1 16.1 %fusion.8 = (bf16[1024,864]{0,1:T(8,128)(2,1)S(1)}, bf16[1024,864]{0,1:T(8,128)(2,1)}, bf16[1024,864]{0,1:T(8,128)(2,1)S(1)}) fusion(f32[1024,864]{0,1:T(8,128)S(1)} %fusion.13, f32[1024,864]{0,1:T(8,128)S(1)} %slice_add_fusion, bf16[256,1728]{1,0:T(8,128)(2,1)S(1)} %bitcast.151, bf16[1024,512]{1,0:T(8,128)(2,1)S(1)} %copy-done.56, ...), kind=kOutput, calls=%fused_computation.17 | convolution fusion | flops 475987968 | bytes 16908288 | tf_op jit(solution)/shard_map/dot_general | solution.py:23
  429.6 33.2 %shard_map.311 = f32[128,1152]{1,0:T(8,128)S(1)} custom-call(bf16[8,128,1152]{2,1,0:T(8,128)(2,1)S(1)} %bitcast.125), custom_call_target="tpu_custom_call" | custom-call | tf_op jit(solution)/shard_map/pallas_call | solution.py:356
  465.8 5.0 fusion.11
  473.7 33.9 %shard_map.312 = f32[128,1152]{1,0:T(8,128)S(1)} custom-call(bf16[8,128,1152]{2,1,0:T(8,128)(2,1)S(1)} %bitcast.123), custom_call_target="tpu_custom_call" | custom-call | tf_op jit(solution)/shard_map/pallas_call | solution.py:356
  510.0 12.3 %shard_map.313 = bf16[4,128,1152]{2,1,0:T(8,128)(2,1)} custom-call(bf16[128,1152]{1,0:T(8,128)(2,1)} %get-tuple-element.89.refs_0_), custom_call_target="tpu_custom_call" | custom-call | tf_op jit(solution)/shard_map/pallas_call | solution.py:230
  555.4 9.2 convolution_convert_fusion
  564.6 6.5 copy.209
  571.1 6.9 reshape.280
  578.0 4.9 copy.262
  593.0 10.5 %shard_map.314 = f32[128,1152]{1,0:T(8,128)S(1)} custom-call(bf16[4,128,1152]{2,1,0:T(8,128)(2,1)S(1)} %bitcast.126), custom_call_target="tpu_custom_call" | custom-call | tf_op jit(solution)/shard_map/pallas_call | solution.py:356
  624.7 5.3 concatenate.105
  637.0 172.0 %shard_map.316 = (bf16[4,8,36,256]{3,2,1,0:T(8,128)(2,1)}, bf16[4,8,36,1920]{3,2,1,0:T(8,128)(2,1)}, bf16[4,8,36,1728]{3,2,1,0:T(8,128)(2,1)}, bf16[4,8,8,1728]{...) custom-call(bf16[4,8,36,256]{3,2,1,0:T(8,128)(2,1)} %bitcast.145, ...), custom_call_target="tpu_custom_call" | custom-call | tf_op jit(solution)/shard_map/pallas_call | solution.py:71
  827.8 88.3 %shard_map.317 = (bf16[8,36,256]{2,1,0:T(8,128)(2,1)}, bf16[8,36,1920]{2,1,0:T(8,128)(2,1)}, bf16[8,36,1728]{2,1,0:T(8,128)(2,1)}, bf16[8,8,1728]{2,1,0:T(8,128)...) custom-call(bf16[8,36,256]{2,1,0:T(8,128)(2,1)} %reduce_sum.242.refs_0_, ...), custom_call_target="tpu_custom_call" | custom-call | tf_op jit(solution)/shard_map/pallas_call | solution.py:71
  922.1 7.2 slice_reduce_fusion.1
  955.6 79.1 %shard_map.315 = (bf16[8,64,1152]{2,1,0:T(8,128)(2,1)}, f32[8,64,1152]{2,1,0:T(8,128)}) custom-call(bf16[8,64,1152]{2,1,0:T(8,128)(2,1)} %copy-done.7, f32[8,64,1152]{2,1,0:T(8,128)} %copy-done.4), custom_call_target="tpu_custom_call" | custom-call | tf_op jit(solution)/shard_map/pallas_call | solution.py:71
  (332 shorter events, 198.3 us)
Async XLA Ops:
  172.6 48.5 %copy-start = (f32[8,1,64,1152]{3,2,1,0:T(8,128)}, f32[8,1,64,1152]{3,2,1,0:T(8,128)S(1)}, u32[]{:S(2)}) copy-start(f32[8,1,64,1152]{3,2,1,0:T(8,128)S(1)} %dynamic-slice_convert_fusion) | copy-start | bytes 7077892
  252.0 39.7 %copy-start.50 = (bf16[216,1152]{1,0:T(8,128)(2,1)S(1)}, bf16[216,1152]{1,0:T(8,128)(2,1)}, u32[]{:S(2)}) copy-start(bf16[216,1152]{1,0:T(8,128)(2,1)} %param.31) | copy-start | bytes 1492996
  252.0 39.7 %copy-start.63 = (bf16[216,256]{1,0:T(8,128)(2,1)S(1)}, bf16[216,256]{1,0:T(8,128)(2,1)}, u32[]{:S(2)}) copy-start(bf16[216,256]{1,0:T(8,128)(2,1)} %param.32) | copy-start | bytes 331780
  385.3 7.7 copy-start.2
  393.0 7.3 copy-start.30
  393.0 7.4 copy-start.56
  425.3 39.9 %copy-start.72 = (bf16[1024,864]{0,1:T(8,128)(2,1)}, bf16[1024,864]{0,1:T(8,128)(2,1)S(1)}, u32[]{:S(2)}) copy-start(bf16[1024,864]{0,1:T(8,128)(2,1)S(1)} %get-tuple-element.91) | copy-start | bytes 5308420
  428.8 34.1 %copy-start.65 = (f32[1024,1408]{1,0:T(8,128)}, f32[1024,1408]{1,0:T(8,128)S(1)}, u32[]{:S(2)}) copy-start(f32[1024,1408]{1,0:T(8,128)S(1)} %fusion.120) | copy-start | bytes 17301508
  463.6 7.2 copy-start.37
  465.8 5.0 copy-start.39
  473.7 33.9 %copy-start.6 = (f32[128,1152]{1,0:T(8,128)S(1)}, f32[128,1152]{1,0:T(8,128)}, u32[]{:S(2)}) copy-start(f32[128,1152]{1,0:T(8,128)} %copy-done.5) | copy-start | bytes 1769476
  530.4 5.1 copy-start.76
  534.8 5.4 copy-start.17
  536.8 6.9 copy-start.13
  549.9 5.5 copy-start.3
  583.0 5.4 copy-start.41
  583.0 5.4 copy-start.43
  583.0 6.6 copy-start.29
  583.0 7.7 copy-start.16
  583.0 7.7 copy-start.36
  590.7 12.7 %copy-start.1 = (f32[8,1,64,1152]{3,2,1,0:T(8,128)S(1)}, f32[8,1,64,1152]{3,2,1,0:T(8,128)}, u32[]{:S(2)}) copy-start(f32[8,1,64,1152]{3,2,1,0:T(8,128)} %copy-done) | copy-start | bytes 7077892
  820.8 6.4 copy-start.62
  943.5 6.5 copy-start.66
  943.5 7.1 copy-start.18
  (58 other events, 157.9 us)

commit v2 on v1

v2 whole, which is shorter than its diff:
```python
import functools
import math

import jax
import jax.numpy as jnp
from jax import lax
from jax.experimental import pallas as pl
from jax.experimental.pallas import tpu as pltpu
from jax.sharding import PartitionSpec as P

HEADS = 4
HEAD = 256
RANK = 256
EPSILON = 1e-06
ROPE_BASE = 10000.0
MASKED = -1e30
MESH = pl.DeviceIdType.MESH
BF = jnp.bfloat16
F32 = jnp.float32


def mm(left, right):
    return jnp.dot(left, right, preferred_element_type=F32)


def mm_tn(left, right):
    return lax.dot_general(left, right, (((0,), (0,)), ((), ())), preferred_element_type=F32)


def mm_nt(left, right):
    return lax.dot_general(left, right, (((1,), (1,)), ((), ())), preferred_element_type=F32)


def remote(src, dst, send, recv, peer):
    return pltpu.make_async_remote_copy(
        src_ref=src, dst_ref=dst, send_sem=send, recv_sem=recv, device_id=peer, device_id_type=MESH
    )


class Direct:
    steps = 0

    def __init__(self, x, axis, size, spread=False):
        self.x, self.axis, self.size, self.spread = x, axis, size, spread
        shape = ((size,) if spread else ()) + x.shape
        self.out = jax.ShapeDtypeStruct(shape, x.dtype)
        self.scratch = [
            pltpu.SemaphoreType.DMA,
            pltpu.SemaphoreType.DMA((size,)),
            pltpu.SemaphoreType.DMA((size,)),
        ]

    def bind(self, x_ref, o_ref, local, send, recv):
        me = lax.axis_index(self.axis)
        self.copies = []
        for k in range(1, self.size):
            peer = lax.rem(me + k, self.size)
            src = x_ref if self.spread else x_ref.at[peer]
            self.copies.append(remote(src, o_ref.at[me], send.at[k], recv.at[k], {self.axis: peer}))
        src = x_ref if self.spread else x_ref.at[me]
        self.copies.append(pltpu.make_async_copy(src, o_ref.at[me], local))

    def start(self):
        for copy in self.copies:
            copy.start()

    def finish(self):
        for copy in self.copies:
            copy.wait()


class Post:
    steps = 0

    def __init__(self, x, slots, sends):
        self.slots, self.sends = slots, sends
        self.x = x
        self.out = jax.ShapeDtypeStruct((slots,) + x.shape[1:], x.dtype)
        count = len(sends(0))
        self.scratch = [
            pltpu.SemaphoreType.DMA((count,)),
            pltpu.SemaphoreType.DMA((count,)),
            pltpu.SemaphoreType.DMA((slots,)),
        ]

    def bind(self, x_ref, o_ref, local, send, recv):
        s = lax.axis_index("seq")
        self.s = s
        self.plan = []
        for k, (block, device, slot) in enumerate(self.sends(s)):
            away = remote(x_ref.at[block], o_ref.at[slot], send.at[k], recv.at[slot], {"seq": device})
            here = pltpu.make_async_copy(x_ref.at[block], o_ref.at[slot], recv.at[slot])
            self.plan.append((device, away, here))
        self.arrive = [
            pltpu.make_async_copy(x_ref.at[0], o_ref.at[k], recv.at[k]) for k in range(self.slots)
        ]

    def start(self):
        for device, away, here in self.plan:
            pl.when(device != self.s)(away.start)
            pl.when(device == self.s)(here.start)

    def finish(self):
        for copy in self.arrive:
            copy.wait()
        for device, away, here in self.plan:
            pl.when(device != self.s)(away.wait_send)


class Line:
    def __init__(self, x, line):
        self.x, self.line = x, line
        self.steps = line // 2 - 1
        self.out = jax.ShapeDtypeStruct((line,) + x.shape, x.dtype)
        self.scratch = [
            pltpu.SemaphoreType.DMA,
            pltpu.SemaphoreType.DMA((2 * line,)),
            pltpu.SemaphoreType.DMA((line,)),
        ]

    def bind(self, x_ref, o_ref, local, send, recv):
        self.x_ref, self.o_ref, self.send, self.recv = x_ref, o_ref, send, recv
        line = self.line
        s = lax.axis_index("seq")
        base = s // line * line
        self.n2 = line // 2
        self.i = s - base
        self.p, self.core = self.i // 2, lax.rem(self.i, 2)
        self.sib = s + 1 - 2 * self.core
        self.left = base + lax.rem(self.i + line - 2, line)
        self.right = base + lax.rem(self.i + 2, line)
        self.own = pltpu.make_async_copy(x_ref, o_ref.at[self.i], local)

    def copy(self, blk, src, dst, k):
        return remote(src, self.o_ref.at[blk], self.send.at[k], self.recv.at[blk], {"seq": dst})

    def start(self):
        @pl.when(self.p < self.n2 - 1)
        def _():
            self.copy(self.i, self.x_ref, self.right, 0).start()

        @pl.when(self.p > 0)
        def _():
            self.copy(self.i, self.x_ref, self.left, 1).start()

        self.copy(self.i, self.x_ref, self.sib, 2).start()
        self.own.start()

    def step(self, d):
        p, n2, o = self.p, self.n2, self.o_ref

        @pl.when(p - d >= 0)
        def _():
            blk = self.i - 2 * d
            self.copy(blk, o.at[blk], self.left, 0).wait_recv()

            @pl.when(p < n2 - 1)
            def _():
                self.copy(blk, o.at[blk], self.right, 4 * d).start()

            self.copy(blk, o.at[blk], self.sib, 4 * d + 1).start()

        @pl.when(p + d < n2)
        def _():
            blk = self.i + 2 * d
            self.copy(blk, o.at[blk], self.right, 0).wait_recv()

            @pl.when(p > 0)
            def _():
                self.copy(blk, o.at[blk], self.left, 4 * d + 2).start()

            self.copy(blk, o.at[blk], self.sib, 4 * d + 3).start()

    def finish(self):
        p, n2, o = self.p, self.n2, self.o_ref

        def sent(k):
            self.copy(self.i, self.x_ref, self.sib, k).wait_send()

        for q in range(n2):
            blk = 2 * q + 1 - self.core
            self.copy(blk, o.at[blk], self.sib, 0).wait_recv()

        @pl.when(p < n2 - 1)
        def _():
            sent(0)

        @pl.when(p > 0)
        def _():
            sent(1)

        sent(2)
        for d in range(1, n2):

            @pl.when(p - d >= 0)
            def _():
                @pl.when(p < n2 - 1)
                def _():
                    sent(4 * d)

                sent(4 * d + 1)

            @pl.when(p + d < n2)
            def _():
                @pl.when(p > 0)
                def _():
                    sent(4 * d + 2)

                sent(4 * d + 3)

        self.own.wait()


class LineSum:
    vmem = True

    def __init__(self, x, line):
        self.x, self.line = x, line
        self.n2 = n2 = line // 2
        self.steps = n2 - 1
        blk = x.shape[1:]
        self.out = jax.ShapeDtypeStruct(blk, F32)
        self.scratch = [pltpu.VMEM((n2,) + blk, BF)] * 4 + [
            pltpu.SemaphoreType.DMA((3 * n2,)),
            pltpu.SemaphoreType.DMA((3 * n2,)),
        ]

    def bind(self, x_ref, o_ref, mine, from_sib, from_left, from_right, send, recv):
        self.x_ref, self.o_ref = x_ref, o_ref
        self.mine, self.from_sib, self.from_left, self.from_right = mine, from_sib, from_left, from_right
        line, n2 = self.line, self.n2
        s = lax.axis_index("seq")
        base = s // line * line
        i = s - base
        self.p, self.core = i // 2, lax.rem(i, 2)
        sib = {"seq": s + 1 - 2 * self.core}
        left = {"seq": base + lax.rem(i + line - 2, line)}
        right = {"seq": base + lax.rem(i + 2, line)}
        core = self.core
        self.hand_over = lambda q: remote(
            x_ref.at[2 * q + 1 - core], from_sib.at[q], send.at[q], recv.at[q], sib
        )
        self.rightward = lambda q: remote(
            mine.at[q], from_left.at[q], send.at[n2 + q], recv.at[n2 + q], right
        )
        self.leftward = lambda q: remote(
            mine.at[q], from_right.at[q], send.at[2 * n2 + q], recv.at[2 * n2 + q], left
        )
        order = []
        for k in range((n2 + 1) // 2):
            order += [n2 - 1 - k] + ([k] if k != n2 - 1 - k else [])
        self.order = order

    def start(self):
        for q in self.order:
            self.hand_over(q).start()

    def add(self, q, other):
        self.mine[q] = (self.mine[q].astype(F32) + other[q].astype(F32)).astype(BF)

    def step(self, d):
        p, n2 = self.p, self.n2
        if d == 1:
            for q in self.order:
                self.hand_over(q).wait_recv()
                own = self.x_ref[2 * q + self.core].astype(F32)
                self.mine[q] = (own + self.from_sib[q].astype(F32)).astype(BF)

                @pl.when((q > p) & (p == 0))
                def _():
                    self.rightward(q).start()

                @pl.when((q < p) & (p == n2 - 1))
                def _():
                    self.leftward(q).start()

        q_right = n2 - d

        @pl.when((p > 0) & (p < q_right))
        def _():
            self.rightward(q_right).wait_recv()
            self.add(q_right, self.from_left)
            self.rightward(q_right).start()

        q_left = d - 1

        @pl.when((p < n2 - 1) & (p > q_left))
        def _():
            self.leftward(q_left).wait_recv()
            self.add(q_left, self.from_right)
            self.leftward(q_left).start()

    def finish(self):
        p, n2 = self.p, self.n2
        for q in range(n2):

            @pl.when(p == q)
            def _():
                total = self.mine[q].astype(F32)
                if q > 0:
                    self.rightward(q).wait_recv()
                    total += self.from_left[q].astype(F32)
                if q < n2 - 1:
                    self.leftward(q).wait_recv()
                    total += self.from_right[q].astype(F32)
                self.o_ref[...] = total

        for q in range(n2):
            self.hand_over(q).wait_send()

            @pl.when(q > p)
            def _():
                self.rightward(q).wait_send()

            @pl.when(q < p)
            def _():
                self.leftward(q).wait_send()


def transfer_kernel(ops, axes, *refs):
    count = len(ops)
    rest = list(refs[2 * count :])
    for a, op in enumerate(ops):
        take = len(op.scratch)
        op.bind(refs[a], refs[count + a], *rest[:take])
        rest = rest[take:]
    barrier = pltpu.get_barrier_semaphore()
    for axis, size in axes:
        me = lax.axis_index(axis)
        for k in range(1, size):
            peer = {axis: lax.rem(me + k, size)}
            pl.semaphore_signal(barrier, inc=1, device_id=peer, device_id_type=MESH)
    pl.semaphore_wait(barrier, sum(size - 1 for _, size in axes))
    for op in ops:
        op.start()
    for d in range(1, 1 + max(op.steps for op in ops)):
        for op in ops:
            if d <= op.steps:
                op.step(d)
    for op in ops:
        op.finish()


def transfer(ops, axes, collective_id):
    spaces = [
        pl.BlockSpec(memory_space=pltpu.VMEM if hasattr(op, "vmem") else pl.ANY) for op in ops
    ]
    return pl.pallas_call(
        functools.partial(transfer_kernel, ops, axes),
        out_shape=[op.out for op in ops],
        in_specs=spaces,
        out_specs=spaces,
        scratch_shapes=[entry for op in ops for entry in op.scratch],
        compiler_params=pltpu.CompilerParams(
            collective_id=collective_id, has_side_effects=True, vmem_limit_bytes=48 << 20
        ),
    )(*[op.x for op in ops])


def norm_apply(hidden, gain):
    return hidden * lax.rsqrt(jnp.mean(hidden * hidden, axis=-1, keepdims=True) + EPSILON) * gain


def rope_tables(positions):
    half = HEAD // 2
    spacing = jnp.exp(-(2.0 * jnp.arange(half).astype(F32) / HEAD) * math.log(ROPE_BASE))
    angle = positions.astype(F32)[..., None] * spacing
    return jnp.cos(angle), jnp.sin(angle)


def rotate(values, cosine, sine):
    half = values.shape[-1] // 2
    a, b = values[..., :half], values[..., half:]
    return jnp.concatenate([a * cosine - b * sine, b * cosine + a * sine], axis=-1)


def unrotate(grads, cosine, sine):
    half = grads.shape[-1] // 2
    a, b = grads[..., :half], grads[..., half:]
    return jnp.concatenate([a * cosine + b * sine, b * cosine - a * sine], axis=-1)


def shards(
    S,
    F,
    layer_input,
    document_numbers,
    cotangent,
    w_qkv,
    qkv_a,
    q_b,
    kv_b,
    w_out,
    out_a,
    out_b,
    w_gu,
    gu_a,
    gu_b,
    w_down,
    down_a,
    down_b,
    gain_a,
    gain_f,
):
    R, seg, width = layer_input.shape
    L = seg * S
    own = R * seg
    G = S // R
    C = G // HEADS
    scale = HEAD**-0.5
    kb = w_qkv.shape[0]
    rb = q_b.shape[0]
    hb = w_down.shape[0]
    ob = w_out.shape[0]
    hidden = w_gu.shape[1] // 2
    hl = hidden // S
    s = lax.axis_index("seq")
    r = s // G
    head = lax.rem(s, G) // C
    chunk = lax.rem(s, C)
    qlen = L // C

    on_seq, on_fsdp = ("seq", S), ("fsdp", F)
    per_head = S // HEADS
    gains = jnp.pad(jnp.stack([gain_a, gain_f], axis=1), ((0, 0), (0, 126)))
    pack1 = jnp.concatenate([w_qkv, qkv_a, gains], axis=1)
    pack2 = jnp.concatenate([q_b, kv_b[0], kv_b[1], out_b], axis=1)
    pack3 = jnp.concatenate([w_out, out_a], axis=1)
    gw = jnp.concatenate(
        [
            jnp.concatenate([w_gu[:, :hidden].reshape(kb, S, hl), w_gu[:, hidden:].reshape(kb, S, hl)], axis=2),
            jnp.concatenate([gu_b[0].reshape(rb, S, hl), gu_b[1].reshape(rb, S, hl)], axis=2),
        ],
        axis=0,
    ).transpose(1, 0, 2)
    p1, p2, p3, gw, f_gu_a, f_down_b = transfer(
        [Direct(x, "fsdp", F, True) for x in (pack1, pack2, pack3)]
        + [Direct(gw, "seq", S)]
        + [Direct(x, "fsdp", F, True) for x in (gu_a, down_b)],
        [on_seq, on_fsdp],
        0,
    )
    dw = jnp.concatenate([w_down, down_a], axis=1)
    gw = lax.all_gather(gw, "fsdp", axis=1)
    dw = lax.all_gather(dw, "fsdp", axis=0)
    cot = lax.all_gather(cotangent.reshape(own, width), "seq", axis=0)
    f_gu_a = lax.all_gather(f_gu_a, "seq", axis=0).reshape(width, 2 * RANK)
    f_down_b = lax.all_gather(f_down_b, "seq", axis=0).reshape(RANK, width)
    ids = jnp.pad(document_numbers[:, None, :], ((0, 0), (0, 7), (0, 128 - seg)))

    def to_head(at):
        return [(0, row * G + at // per_head * C + c, lax.rem(at, per_head)) for row in range(R) for c in range(C)]

    p1, p2, xin, ids, wo = transfer(
        [Line(p1, S), Line(p2, S), Line(layer_input, S), Line(ids, S), Post(p3[None], per_head, to_head)],
        [on_seq],
        1,
    )
    p1 = p1.reshape(width, -1)
    p2 = p2.reshape(RANK, -1)
    wo = wo.reshape(HEAD, -1)
    xrow = lax.dynamic_index_in_dim(xin, r, 1, keepdims=False).reshape(L, width).astype(F32)
    cot = cot.reshape(S, R, seg, width).transpose(1, 0, 2, 3).reshape(R * L, width)
    ids = lax.dynamic_index_in_dim(ids[:, :, 0, :seg], r, 1, keepdims=False).reshape(L)
    gb = gw[:, :, kb:].reshape(RANK, 2 * hl)
    gw = gw[:, :, :kb].reshape(width, 2 * hl)
    dw = dw.reshape(hl, -1)

    q0 = HEADS * HEAD
    wq = lax.dynamic_slice_in_dim(p1, head * HEAD, HEAD, 1)
    w1 = jnp.concatenate([wq, p1[:, q0 : q0 + 2 * HEAD + 3 * RANK]], axis=1)
    at = q0 + 2 * HEAD + 3 * RANK
    gain_one = p1[:, at].astype(F32)
    gain_two = p1[:, at + 1].astype(F32)
    f_q_b = lax.dynamic_slice_in_dim(p2, head * HEAD, HEAD, 1)
    f_k_b = p2[:, q0 : q0 + HEAD]
    f_v_b = p2[:, q0 + HEAD : q0 + 2 * HEAD]
    f_out_b = p2[:, q0 + 2 * HEAD : q0 + 2 * HEAD + width]

    place = jnp.arange(L, dtype=jnp.int32)
    same = ids[:, None] == ids[None, :]
    before = place[None, :] < place[:, None]
    positions = jnp.sum((same & before).astype(jnp.int32), axis=1)
    allowed = same & (place[None, :] <= place[:, None])
    cosine, sine = rope_tables(positions)
    norm_one = norm_apply(xrow, gain_one).astype(BF)
    pu = mm(norm_one, w1)
    u = pu[:, 3 * HEAD :].astype(BF)
    u_q, u_k, u_v = u[:, :RANK], u[:, RANK : 2 * RANK], u[:, 2 * RANK :]
    query = rotate(pu[:, :HEAD] + mm(u_q, f_q_b), cosine, sine).astype(BF)
    key = rotate(pu[:, HEAD : 2 * HEAD] + mm(u_k, f_k_b), cosine, sine).astype(BF)
    value = (pu[:, 2 * HEAD : 3 * HEAD] + mm(u_v, f_v_b)).astype(BF)
    if C > 1:
        query_c = lax.dynamic_slice_in_dim(query, chunk * qlen, qlen, 0)
        allowed = lax.dynamic_slice_in_dim(allowed, chunk * qlen, qlen, 0)
    else:
        query_c = query
    scores = jnp.where(allowed, mm_nt(query_c, key) * scale, MASKED)
    top = jnp.max(scores, axis=-1, keepdims=True)
    lse = top + jnp.log(jnp.sum(jnp.exp(scores - top), axis=-1, keepdims=True))
    probs = jnp.where(allowed, jnp.exp(scores - lse), 0.0)
    probs_low = probs.astype(BF)
    mixed = mm(probs_low, value).astype(BF)
    part = mm(mixed, wo).astype(BF)
    if C > 1:
        part = lax.dynamic_update_slice_in_dim(jnp.zeros((L, part.shape[1]), BF), part, chunk * qlen, 0)
    (attn,) = transfer([LineSum(part.reshape(G, own, -1), G)], [on_seq], 4)
    u_out = attn[:, width:].astype(BF)
    mine = lax.rem(s, G) * own
    x_own = lax.dynamic_slice_in_dim(xrow, mine, own, 0)
    resid = x_own + attn[:, :width] + mm(u_out, f_out_b)
    norm_two_own = norm_apply(resid, gain_two).astype(BF)
    (norm_two,) = transfer([Line(norm_two_own, S)], [on_seq], 5)
    norm_two = norm_two.reshape(R * L, width)

    u_gu = mm(norm_two, f_gu_a).astype(BF)
    gu = mm(norm_two, gw)
    gate = gu[:, :hl] + mm(u_gu[:, :RANK], gb[:, :hl])
    up = gu[:, hl:] + mm(u_gu[:, RANK:], gb[:, hl:])
    d_u_down = mm_nt(cot, f_down_b).astype(BF)
    cot_u = jnp.concatenate([cot, d_u_down], axis=1)
    d_act = mm_nt(cot_u, dw)
    inner = math.sqrt(2.0 / math.pi)
    th = jnp.tanh(inner * (gate + 0.044715 * gate * gate * gate))
    gelu = 0.5 * gate * (1.0 + th)
    act = (gelu * up).astype(BF)
    slope = 0.5 * (1.0 + th) + 0.5 * gate * (1.0 - th * th) * inner * (1.0 + 3 * 0.044715 * gate * gate)
    d_gate = (d_act * up * slope).astype(BF)
    d_up = (d_act * gelu).astype(BF)
    d_gu = jnp.concatenate([d_gate, d_up], axis=1)
    d_u_gu = jnp.concatenate(
        [mm_nt(d_gate, gb[:, :hl]), mm_nt(d_up, gb[:, hl:])], axis=1
    ).astype(BF)
    d_norm_two = (mm_nt(d_gu, gw) + mm_nt(d_u_gu, f_gu_a)).astype(BF)
    (d_norm_two,) = transfer([LineSum(d_norm_two.reshape(S, own, width), S)], [on_seq], 6)
    ffn = mm(act, dw)
    u_down = ffn[:, width:].astype(BF)
    ffn = (ffn[:, :width] + mm(u_down, f_down_b)).astype(BF)
    (ffn,) = transfer([LineSum(ffn.reshape(S, own, width), S)], [on_seq], 7)
    activations = (resid + ffn).astype(BF)
    g_down = mm_tn(act, cot_u)
    g_down_b = mm_tn(u_down, cot)
    g_gu = mm_tn(norm_two, d_gu)
    g_gu_b = jnp.concatenate([mm_tn(u_gu[:, :RANK], d_gate), mm_tn(u_gu[:, RANK:], d_up)], axis=1)
    g_gu_a = mm_tn(norm_two, d_u_gu)

    def split(g, rows):
        return g.astype(BF).reshape(-1, F, rows, g.shape[1]).transpose(1, 0, 2, 3)

    def scatter(g, axes):
        return lax.psum_scatter(g, axes, scatter_dimension=0, tiled=True)[0]

    g_gu = scatter(jnp.concatenate([split(g_gu, kb), split(g_gu_b, rb)], axis=2), "fsdp")
    g_down = scatter(g_down.astype(BF).reshape(F, hb, -1), "fsdp").astype(F32)
    g_gu_a = scatter(g_gu_a.astype(BF).reshape(S * F, kb, -1), ("seq", "fsdp")).astype(F32)
    g_down_b = scatter(g_down_b.astype(BF).reshape(S * F, rb, -1), ("seq", "fsdp")).astype(F32)

    def norm_back(G_in, h, g):
        q = lax.rsqrt(jnp.mean(h * h, axis=-1, keepdims=True) + EPSILON)
        gg = G_in * g
        d_gain = jnp.sum(G_in * (h * q), axis=0)
        return d_gain, q * gg - h * (q * q * q) * jnp.mean(gg * h, axis=-1, keepdims=True)

    d_gain_two, back = norm_back(d_norm_two, resid, gain_two)
    cot_own = lax.dynamic_slice_in_dim(cot, s * own, own, 0)
    d_resid = cot_own.astype(F32) + back

    d_attn_own = d_resid.astype(BF)
    (d_attn,) = transfer([Line(d_attn_own, G)], [on_seq], 8)
    d_attn = d_attn.reshape(L, width)
    g_out_b = mm_tn(u_out, d_attn_own)
    if C > 1:
        d_attn = lax.dynamic_slice_in_dim(d_attn, chunk * qlen, qlen, 0)
    d_u_out = mm_nt(d_attn, f_out_b).astype(BF)
    d_attn_u = jnp.concatenate([d_attn, d_u_out], axis=1)
    d_mixed = mm_nt(d_attn_u, wo).astype(BF)
    g_out = mm_tn(mixed, d_attn_u)
    d_probs = mm_nt(d_mixed, value)
    delta = jnp.sum(probs * d_probs, axis=-1, keepdims=True)
    d_scores = (probs * (d_probs - delta)).astype(BF)
    d_query = mm(d_scores, key) * scale
    d_key = mm_tn(d_scores, query_c) * scale
    d_value = mm_tn(probs_low, d_mixed)
    if C > 1:
        d_query = lax.dynamic_update_slice_in_dim(jnp.zeros((L, HEAD), F32), d_query, chunk * qlen, 0)
    dq = unrotate(d_query, cosine, sine).astype(BF)
    dk = unrotate(d_key, cosine, sine).astype(BF)
    dv = d_value.astype(BF)
    d_u = [mm_nt(dq, f_q_b).astype(BF), mm_nt(dk, f_k_b).astype(BF), mm_nt(dv, f_v_b).astype(BF)]
    d_pu = jnp.concatenate([dq, dk, dv] + d_u, axis=1)
    d_norm_one = mm_nt(d_pu, w1).astype(BF)
    (d_norm_one,) = transfer([LineSum(d_norm_one.reshape(G, own, width), G)], [on_seq], 9)
    g_w1 = mm_tn(norm_one, d_pu)
    g_q_b = mm_tn(u_q, dq)
    g_kv_b = [mm_tn(u_k, dk), mm_tn(u_v, dv)]
    d_gain_one, back_one = norm_back(d_norm_one, x_own, gain_one)
    grad_input = d_resid + back_one

    d_gains = jnp.pad(jnp.stack([d_gain_one, d_gain_two], axis=1), ((0, 0), (0, 126)))
    t_1 = jnp.concatenate([g_w1[:, HEAD:], d_gains], axis=1).astype(BF).reshape(S, F, kb, -1)
    t_2 = jnp.concatenate(g_kv_b + [g_out_b], axis=1).astype(BF).reshape(S, F, rb, -1)
    t_1, t_2, t_q, t_qb, t_out = transfer(
        [LineSum(t_1, S), LineSum(t_2, S)]
        + [Direct(x, "fsdp", F) for x in (split(g_w1[:, :HEAD], kb), split(g_q_b, rb), split(g_out, ob))],
        [on_seq, on_fsdp],
        10,
    )

    def total(t):
        return jnp.sum(t.astype(F32), axis=0)

    per = own // seg

    def to_rows(at):
        return [(j, lax.rem(at, G) * per + j, at // G) for j in range(per)]

    def to_out(at):
        return [
            (j, lax.rem(at, G) // C * per_head + j, at // G * C + lax.rem(at, C)) for j in range(per_head)
        ]

    t_1, t_2, t_q, t_qb, t_gu, t_out, activations, grad_input = transfer(
        [Direct(t.astype(BF), "fsdp", F) for t in (t_1, t_2)]
        + [Direct(t.astype(BF), "seq", S) for t in (total(t_q), total(t_qb), g_gu)]
        + [Post(total(t_out).astype(BF), R * C, to_out)]
        + [Post(t.reshape(per, seg, width), R, to_rows) for t in (activations, grad_input)],
        [on_seq, on_fsdp],
        11,
    )

    def by_head(t):
        t = t.astype(F32).reshape(R, HEADS, C, t.shape[1], HEAD).sum(axis=(0, 2))
        return t.transpose(1, 0, 2).reshape(t.shape[1], HEADS * HEAD)

    def halves(t):
        t = t.astype(F32).reshape(S, t.shape[1], 2, hl).transpose(2, 1, 0, 3)
        return t.reshape(2, t.shape[1], hidden)

    t_1, t_2, g_out = total(t_1), total(t_2), total(t_out)
    grad_w_qkv = jnp.concatenate([by_head(t_q), t_1[:, : 2 * HEAD]], axis=1)
    g_qkv_a = t_1[:, 2 * HEAD : 2 * HEAD + 3 * RANK]
    d_gain_one = t_1[:, 2 * HEAD + 3 * RANK]
    d_gain_two = t_1[:, 2 * HEAD + 3 * RANK + 1]
    g_gu_b = halves(t_gu[:, kb:])
    g_gu = halves(t_gu[:, :kb])
    return (
        activations,
        grad_input,
        grad_w_qkv,
        g_qkv_a,
        by_head(t_qb),
        jnp.stack([t_2[:, :HEAD], t_2[:, HEAD : 2 * HEAD]]),
        g_out[:, :width],
        g_out[:, width:],
        t_2[:, 2 * HEAD :],
        jnp.concatenate([g_gu[0], g_gu[1]], axis=1),
        g_gu_a,
        g_gu_b,
        g_down[:, :width],
        g_down[:, width:],
        g_down_b,
        d_gain_one,
        d_gain_two,
    )


def solution(mesh):
    both = P(("seq", "fsdp"), None)
    second = P(None, ("seq", "fsdp"), None)
    tokens = P("fsdp", "seq", None)
    gain = P(("seq", "fsdp"))
    return jax.shard_map(
        functools.partial(shards, mesh.shape["seq"], mesh.shape["fsdp"]),
        mesh=mesh,
        in_specs=(tokens, P("fsdp", "seq"), tokens)
        + (both, both, both, second, both, both, both, both, both, second, both, both, both, gain, gain),
        out_specs=(tokens, tokens)
        + (both, both, both, second, both, both, both, both, both, second, both, both, both, gain, gain),
        check_vma=False,
    )
```

time: 1040 us -> 774 us (0.74); the launches traced: 1040 us -> 761 us
  Pallas kernels: 753 us -> 411 us
  waiting for transfers between devices: 0 us -> 48.1 us
  other arithmetic: 54 us -> 33 us
  blocking collectives: 0 us -> 18.2 us
  between operations: 2.34 us -> 16.4 us
    pallas_call x13 -> x10, Pallas kernels: 753 us -> 411 us  [transfer(): pl.pallas_call(functools.partial(transfer_kernel, ops, axes), out_shape=[...]
    unnamed x0 -> x11, waiting for transfers between devices: none -> 48.1 us
    all_gather x0 -> x1, blocking collectives: none -> 18.2 us  [shards(): f_down_b = lax.all_gather(f_down_b, 'seq', axis=0).reshape(RANK, width)]
    reduce_sum x13 -> x8, other arithmetic: 19.7 us -> 3.83 us  [the longest x2 2.55 us: norm_back(): jnp.mean(gg * h, axis=-1, keepdims=True)]
    dot_general x14, matrix products: 23.6 us -> 34.9 us  [mm_nt(): lax.dot_general(left, right, (((1,), (1,)), ((), ())), preferred_element_...]
    unnamed x173 -> x211, local copies, waits for them, and re-layouts: 19.6 us -> 25.5 us
  transfers between devices with their start and end apart: 0 -> 8, of which waited for: 0 -> 1; matrix products, arithmetic and copies ran while one was open for 0% -> 22% of each run, Pallas kernels for 0% -> 42%
where the time goes in v2:
time: 774 us; the launch traced here: 761 us
  Pallas kernels  411 us (53%)
  local copies, waits for them, and re-layouts  126 us (16%)
  matrix products  108 us (14%)
  waiting for transfers between devices  48.1 us (6%)
  other arithmetic  33 us (4%)
  blocking collectives  18.2 us (2%)
  between operations  16.4 us (2%)
    pallas_call x10, Pallas kernels, transfer(): pl.pallas_call(functools.partial(transfer_kernel, ops, axes), out_shape=[...  411 us
    unnamed x11, waiting for transfers between devices  48.1 us
    dot_general x14, matrix products, mm(): return jnp.dot(left, right, preferred_element_type=F32)  40.7 us
    dot_general x14, matrix products, mm_nt(): lax.dot_general(left, right, (((1,), (1,)), ((), ())), preferred_element_...  34.9 us
    dot_general x14, matrix products, mm_tn(): lax.dot_general(left, right, (((0,), (0,)), ((), ())), preferred_element_...  32.5 us
    unnamed x211, local copies, waits for them, and re-layouts  25.5 us
    all_gather x1, blocking collectives, shards(): f_down_b = lax.all_gather(f_down_b, 'seq', axis=0).reshape(RANK, width)  18.2 us
  transfers between devices with their start and end apart: 8, of which 1 were waited for; matrix products, arithmetic and copies ran while one was open for 22% of the time, Pallas kernels for 42%

profile of v2, /device:TPU:17, one launch (start us, length us, event | category | flops | bytes accessed | tf_op | source)
XLA Modules:
  0.0 761.1 jit_solution(11330885311170530043)
XLA Ops:
  12.0 32.3 %shard_map.305 = (bf16[4,36,2432]{2,1,0:T(8,128)(2,1)S(1)}, bf16[4,8,2688]{2,1,0:T(8,128)(2,1)S(1)}, bf16[4,32,1408]{2,1,0:T(8,128)(2,1)S(1)}, bf16[8,44,1728]{2...) custom-call(bf16[36,2432]{1,0:T(8,128)(2,1)S(1)} %fusion.74.refs_0_, ...), custom_call_target="tpu_custom_call" | custom-call | tf_op jit(solution)/shard_map/pallas_call | solution.py:348
  50.8 121.4 %shard_map.306 = (bf16[8,4,36,2432]{3,2,1,0:T(8,128)(2,1)}, bf16[8,4,8,2688]{3,2,1,0:T(8,128)(2,1)S(1)}, bf16[8,2,64,1152]{3,2,1,0:T(8,128)(2,1)S(1)}, s32[8,2,8...) custom-call(bf16[4,36,2432]{2,1,0:T(8,128)(2,1)S(1)} %get-tuple-element.41.refs_0_, bf16[4,8,2688]{2,1,0:T(8,128)(2,1)S(1)} %copy-done.8, ...), custom_call_target="tpu_custom_call" | custom-call | tf_op jit(solution)/shard_map/pallas_call | solution.py:348
  175.3 8.1 %reshape.279 = bf16[1152,2432]{1,0:T(8,128)(2,1)} reshape(bf16[8,4,36,2432]{3,2,1,0:T(8,128)(2,1)} %get-tuple-element.45) | data formatting | bytes 11206656 | tf_op jit(solution)/shard_map/reshape | solution.py:459
  200.5 18.1 %shard_map.307 = f32[128,1408]{1,0:T(8,128)S(1)} custom-call(bf16[4,128,1408]{2,1,0:T(8,128)(2,1)S(1)} %bitcast.131), custom_call_target="tpu_custom_call" | custom-call | tf_op jit(solution)/shard_map/pallas_call | solution.py:348
  221.4 22.6 %shard_map.308 = bf16[8,128,1152]{2,1,0:T(8,128)(2,1)S(1)} custom-call(bf16[128,1152]{1,0:T(8,128)(2,1)S(1)} %multiply_convert_fusion.4.refs_0_), custom_call_target="tpu_custom_call" | custom-call | tf_op jit(solution)/shard_map/pallas_call | solution.py:348
  244.0 18.2 %all-gather = bf16[32,8,1152]{2,1,0:T(8,128)(2,1)S(1)} all-gather(bf16[4,8,1152]{2,1,0:T(8,128)(2,1)S(1)} %copy-done.11), channel_id=2, replica_groups=mesh['seq'=8,'fsdp'=4] {'seq'}, dimensions={0}, use_global_device_ids=true | all-gather | bytes 663552 | tf_op jit(solution)/shard_map/all_gather | solution.py:448
  273.9 7.3 fusion.12
  288.8 7.3 reshape.288
  296.1 7.2 fusion.105
  305.9 15.9 %multiply_convert_fusion = (bf16[1024,864]{0,1:T(8,128)(2,1)S(1)}, bf16[1024,864]{0,1:T(8,128)(2,1)}, bf16[1024,864]{0,1:T(8,128)(2,1)}) fusion(f32[1024,864]{0,1:T(8,128)S(1)} %slice_add_fusion, f32[1024,864]{0,1:T(8,128)S(1)} %copy-done.100, bf16[256,1728]{1,0:T(8,128)(2,1)S(1)} %bitcast.177, bf16[1024,512]{1,0:T(8,128)(2,1)S(1)} %copy-done.58, ...), kind=kOutput, calls=%fused_computation.21 | convolution fusion | flops 475987968 | bytes 16908288 | tf_op jit(solution)/shard_map/dot_general | solution.py:23
  339.2 6.7 convolution_convert_fusion.2
  351.4 33.5 %shard_map.313 = f32[128,1152]{1,0:T(8,128)S(1)} custom-call(bf16[8,128,1152]{2,1,0:T(8,128)(2,1)S(1)} %bitcast.138), custom_call_target="tpu_custom_call" | custom-call | tf_op jit(solution)/shard_map/pallas_call | solution.py:348
  384.9 7.7 %convolution_convert_fusion = bf16[1152,1728]{0,1:T(8,128)(2,1)} fusion(bf16[1024,1152]{1,0:T(8,128)(2,1)S(1)} %bitcast.137, bf16[1024,864]{0,1:T(8,128)(2,1)S(1)} %copy-done.97, bf16[1024,864]{0,1:T(8,128)(2,1)S(1)} %copy-done.94), kind=kOutput, calls=%fused_computation | convolution fusion | flops 4085932032 | bytes 9879552 | tf_op jit(solution)/shard_map/dot_general | solution.py:27
  392.6 6.5 copy.203
  399.1 7.4 reshape.297
  419.8 9.9 %fusion.10 = f32[1024,1152]{1,0:T(8,128)} fusion(bf16[1152,1728]{1,0:T(8,128)(2,1)} %reshape.288, bf16[1024,864]{0,1:T(8,128)(2,1)} %get-tuple-element.79, bf16[1024,864]{0,1:T(8,128)(2,1)S(1)} %copy-done.95), kind=kOutput, calls=%fused_computation.36 | convolution fusion | flops 4083941376 | bytes 12238848 | tf_op jit(solution)/shard_map/dot_general | solution.py:31
  435.3 36.4 %shard_map.309 = f32[128,1152]{1,0:T(8,128)S(1)} custom-call(bf16[8,128,1152]{2,1,0:T(8,128)(2,1)S(1)} %bitcast.130), custom_call_target="tpu_custom_call" | custom-call | tf_op jit(solution)/shard_map/pallas_call | solution.py:348
  474.5 14.1 %shard_map.310 = bf16[4,128,1152]{2,1,0:T(8,128)(2,1)S(1)} custom-call(bf16[128,1152]{1,0:T(8,128)(2,1)S(1)} %get-tuple-element.75.refs_0_), custom_call_target="tpu_custom_call" | custom-call | tf_op jit(solution)/shard_map/pallas_call | solution.py:348
  515.7 12.0 %shard_map.311 = f32[128,1152]{1,0:T(8,128)S(1)} custom-call(bf16[4,128,1152]{2,1,0:T(8,128)(2,1)S(1)} %bitcast.144), custom_call_target="tpu_custom_call" | custom-call | tf_op jit(solution)/shard_map/pallas_call | solution.py:348
  529.9 5.3 concatenate.112
  544.6 58.7 %shard_map.312 = (f32[4,36,1408]{2,1,0:T(8,128)S(1)}, f32[4,8,1664]{2,1,0:T(8,128)S(1)}, bf16[4,8,36,256]{3,2,1,0:T(8,128)(2,1)S(1)}, bf16[4,8,8,256]{3,2,1,0:T(8,128)(2,1)S(1)}, bf16[4,2,32,1408]{3,2,1,0:T(8,128)(2,1)S(1)}) custom-call(bf16[8,4,36,1408]{3,2,1,0:T(8,128)(2,1)} %pad_maximum_fusion.1.refs_0_, ...), custom_call_target="tpu_custom_call" | custom-call | tf_op jit(solution)/shard_map/pallas_call | solution.py:348
  612.3 47.3 %reduce-scatter.13.cloned.1.call-done = bf16[1,8,44,1728]{3,1,2,0:T(8,128)(2,1)} async-done(((bf16[4,8,44,1728]{3,1,2,0:T(8,128)(2,1)}), bf16[1,8,44,1728]{3,1,2,0:T(8,128)(2,1)}) %reduce-scatter.13.cloned.1.call-update) | async-done | bytes 1216528
  662.2 61.4 %shard_map.314 = (bf16[4,36,1408]{2,1,0:T(8,128)(2,1)S(1)}, bf16[4,8,1664]{2,1,0:T(8,128)(2,1)S(1)}, bf16[8,36,256]{2,1,0:T(8,128)(2,1)S(1)}, bf16[8,8,256]{2,1,...) custom-call(bf16[4,36,1408]{2,1,0:T(8,128)(2,1)S(1)} %convert_elemen, ...), custom_call_target="tpu_custom_call" | custom-call | tf_op jit(solution)/shard_map/pallas_call | solution.py:348
  734.7 7.0 slice_reduce_fusion.1
  (387 shorter events, 172.3 us)
Async XLA Ops:
  7.2 255.0 %all-gather.15.cloned.1.call-start = ((), (), s32[]{:S(2)}) async-start(), calls=%async_computation.8 | async-start | bytes 1474560 | tf_op jit(solution)/shard_map/all_gather | solution.py:447
  11.4 35.0 %copy-start.51 = (bf16[216,1152]{1,0:T(8,128)(2,1)S(1)}, bf16[216,1152]{1,0:T(8,128)(2,1)}, u32[]{:S(2)}) copy-start(bf16[216,1152]{1,0:T(8,128)(2,1)} %param.31) | copy-start | bytes 1492996
  11.4 35.0 %copy-start.67 = (bf16[216,256]{1,0:T(8,128)(2,1)S(1)}, bf16[216,256]{1,0:T(8,128)(2,1)}, u32[]{:S(2)}) copy-start(bf16[216,256]{1,0:T(8,128)(2,1)} %param.32) | copy-start | bytes 331780
  45.6 223.3 %all-gather.9.cloned.1.call-start = ((), (), s32[]{:S(2)}) async-start(), calls=%async_computation.4 | async-start | bytes 2654208 | tf_op jit(solution)/shard_map/all_gather | solution.py:446
  46.4 227.5 %all-gather.11.cloned.1.call-start = ((), (), s32[]{:S(2)}) async-start(), calls=%async_computation.6 | async-start | bytes 3041280 | tf_op jit(solution)/shard_map/all_gather | solution.py:445
  47.4 233.9 %all-gather.13.cloned.1.call-start = ((), (), s32[]{:S(2)}) async-start(), calls=%async_computation.7 | async-start | bytes 6307840 | tf_op jit(solution)/shard_map/all_gather | solution.py:444
  48.8 557.8 %reduce-scatter.17.cloned.1.call-start = ((), (), s32[]{:S(2)}) async-start(), calls=%async_computation.11 | async-start | bytes 608256
  188.2 10.9 %copy-start.70 = (s32[512]{0:T(512)}, s32[512]{0:T(512)S(1)}, u32[]{:S(2)}) copy-start(s32[512]{0:T(512)S(1)} %eq.15) | copy-start | bytes 6148
  188.4 8.2 %copy-start.72 = (f32[512]{0:T(512)}, f32[512]{0:T(512)S(1)}, u32[]{:S(2)}) copy-start(f32[512]{0:T(512)S(1)} %convert_element_type.208) | copy-start | bytes 6148
  188.5 8.2 %copy-start.83 = (f32[128]{0:T(128)}, f32[128]{0:T(128)S(1)}, u32[]{:S(2)}) copy-start(f32[128]{0:T(128)S(1)} %multiply_exponential_fusion) | copy-start | bytes 1540
  218.6 25.4 %copy-start.11 = (bf16[4,8,1152]{2,1,0:T(8,128)(2,1)S(1)}, bf16[4,8,1152]{2,1,0:T(8,128)(2,1)}, u32[]{:S(2)}) copy-start(bf16[4,8,1152]{2,1,0:T(8,128)(2,1)} %copy-done.10) | copy-start | bytes 221188
  305.9 15.9 %copy-start.91 = (bf16[864,1408]{1,0:T(8,128)(2,1)S(1)}, bf16[864,1408]{1,0:T(8,128)(2,1)}, u32[]{:S(2)}) copy-start(bf16[864,1408]{1,0:T(8,128)(2,1)} %all-gather.11.cloned.1.call-done) | copy-start | bytes 7299076
  329.5 278.5 %reduce-scatter.11.cloned.1.call-start = ((), (), s32[]{:S(2)}) async-start(), calls=%async_computation.5 | async-start | bytes 1351680 | tf_op jit(solution)/shard_map/reduce_scatter | solution.py:551
  339.1 270.3 %reduce-scatter.15.cloned.1.call-start = ((), (), s32[]{:S(2)}) async-start(), calls=%async_computation.10 | async-start | bytes 3041280
  345.9 313.7 %reduce-scatter.13.cloned.1.call-start = ((), (), s32[]{:S(2)}) async-start(), calls=%async_computation.9 | async-start | bytes 6307840
  347.7 37.2 %copy-start.97 = (bf16[1024,864]{0,1:T(8,128)(2,1)S(1)}, bf16[1024,864]{0,1:T(8,128)(2,1)}, u32[]{:S(2)}) copy-start(bf16[1024,864]{0,1:T(8,128)(2,1)} %get-tuple-element.79) | copy-start | bytes 5308420
  351.4 33.5 %copy-start.94 = (bf16[1024,864]{0,1:T(8,128)(2,1)S(1)}, bf16[1024,864]{0,1:T(8,128)(2,1)}, u32[]{:S(2)}) copy-start(bf16[1024,864]{0,1:T(8,128)(2,1)} %get-tuple-element.78) | copy-start | bytes 5308420
  435.2 36.5 %copy-start.82 = (f32[128]{0:T(128)S(1)}, f32[128]{0:T(128)}, u32[]{:S(2)}) copy-start(f32[128]{0:T(128)} %copy-done.81) | copy-start | bytes 1540
  435.2 37.2 %copy-start.90 = (f32[128]{0:T(128)S(1)}, f32[128]{0:T(128)}, u32[]{:S(2)}) copy-start(f32[128]{0:T(128)} %get-tuple-element.103) | copy-start | bytes 1540
  474.5 15.9 %copy-start.5 = (bf16[2,4,32,1408]{3,2,1,0:T(8,128)(2,1)S(1)}, bf16[2,4,32,1408]{3,2,1,0:T(8,128)(2,1)}, u32[]{:S(2)}) copy-start(bf16[2,4,32,1408]{3,2,1,0:T(8,128)(2,1)} %copy-done.3) | copy-start | bytes 2162692
  493.2 8.7 %copy-start.22 = (f32[512,512]{0,1:T(8,128)S(1)}, f32[512,512]{0,1:T(8,128)}, u32[]{:S(2)}) copy-start(f32[512,512]{0,1:T(8,128)} %copy-done.20) | copy-start | bytes 3145732
  495.5 9.3 %copy-start.46 = (bf16[512,128]{1,0:T(8,128)(2,1)}, bf16[512,128]{1,0:T(8,128)(2,1)S(1)}, u32[]{:S(2)}) copy-start(bf16[512,128]{1,0:T(8,128)(2,1)S(1)} %get-tuple-element.83) | copy-start | bytes 393220
  513.5 14.3 %copy-start.53 = (bf16[512,256]{1,0:T(8,128)(2,1)S(1)}, bf16[512,256]{1,0:T(8,128)(2,1)}, u32[]{:S(2)}) copy-start(bf16[512,256]{1,0:T(8,128)(2,1)} %copy-done.52) | copy-start | bytes 786436
  513.5 14.3 %copy-start.55 = (bf16[512,256]{1,0:T(8,128)(2,1)S(1)}, bf16[512,256]{1,0:T(8,128)(2,1)}, u32[]{:S(2)}) copy-start(bf16[512,256]{1,0:T(8,128)(2,1)} %copy-done.54) | copy-start | bytes 786436
  (87 other events, 202.4 us)
Sparse Core Ops, SparseCore 0:
  45.8 36.0 all-gather.14
  83.4 44.6 all-gather.8
  130.6 41.1 all-gather.10
  174.0 59.7 all-gather.12
  329.6 85.2 reduce-scatter.16
  417.1 121.2 reduce-scatter.10
  541.5 54.9 reduce-scatter.14
  599.8 59.7 reduce-scatter.12

commit v3 on v2

--- a/solution.py
+++ b/solution.py
@@ -220,14 +220,13 @@
         self.steps = n2 - 1
         blk = x.shape[1:]
         self.out = jax.ShapeDtypeStruct(blk, F32)
-        self.scratch = [pltpu.VMEM((n2,) + blk, BF)] * 4 + [
+        self.scratch = [pltpu.VMEM((n2,) + blk, BF), pltpu.VMEM((n2 + 1,) + blk, BF)] + [
             pltpu.SemaphoreType.DMA((3 * n2,)),
             pltpu.SemaphoreType.DMA((3 * n2,)),
         ]
 
-    def bind(self, x_ref, o_ref, mine, from_sib, from_left, from_right, send, recv):
-        self.x_ref, self.o_ref = x_ref, o_ref
-        self.mine, self.from_sib, self.from_left, self.from_right = mine, from_sib, from_left, from_right
+    def bind(self, x_ref, o_ref, mine, came, send, recv):
+        self.x_ref, self.o_ref, self.mine, self.came = x_ref, o_ref, mine, came
         line, n2 = self.line, self.n2
         s = lax.axis_index("seq")
         base = s // line * line
@@ -238,13 +237,13 @@
         right = {"seq": base + lax.rem(i + 2, line)}
         core = self.core
         self.hand_over = lambda q: remote(
-            x_ref.at[2 * q + 1 - core], from_sib.at[q], send.at[q], recv.at[q], sib
+            x_ref.at[2 * q + 1 - core], mine.at[q], send.at[q], recv.at[q], sib
         )
         self.rightward = lambda q: remote(
-            mine.at[q], from_left.at[q], send.at[n2 + q], recv.at[n2 + q], right
+            mine.at[q], came.at[q + 1], send.at[n2 + q], recv.at[n2 + q], right
         )
         self.leftward = lambda q: remote(
-            mine.at[q], from_right.at[q], send.at[2 * n2 + q], recv.at[2 * n2 + q], left
+            mine.at[q], came.at[q], send.at[2 * n2 + q], recv.at[2 * n2 + q], left
         )
         order = []
         for k in range((n2 + 1) // 2):
@@ -256,7 +255,7 @@
             self.hand_over(q).start()
 
     def add(self, q, other):
-        self.mine[q] = (self.mine[q].astype(F32) + other[q].astype(F32)).astype(BF)
+        self.mine[q] = (self.mine[q].astype(F32) + self.came[other].astype(F32)).astype(BF)
 
     def step(self, d):
         p, n2 = self.p, self.n2
@@ -264,7 +263,7 @@
             for q in self.order:
                 self.hand_over(q).wait_recv()
                 own = self.x_ref[2 * q + self.core].astype(F32)
-                self.mine[q] = (own + self.from_sib[q].astype(F32)).astype(BF)
+                self.mine[q] = (own + self.mine[q].astype(F32)).astype(BF)
 
                 @pl.when((q > p) & (p == 0))
                 def _():
@@ -279,7 +278,7 @@
         @pl.when((p > 0) & (p < q_right))
         def _():
             self.rightward(q_right).wait_recv()
-            self.add(q_right, self.from_left)
+            self.add(q_right, q_right + 1)
             self.rightward(q_right).start()
 
         q_left = d - 1
@@ -287,7 +286,7 @@
         @pl.when((p < n2 - 1) & (p > q_left))
         def _():
             self.leftward(q_left).wait_recv()
-            self.add(q_left, self.from_right)
+            self.add(q_left, q_left)
             self.leftward(q_left).start()
 
     def finish(self):
@@ -299,10 +298,10 @@
                 total = self.mine[q].astype(F32)
                 if q > 0:
                     self.rightward(q).wait_recv()
-                    total += self.from_left[q].astype(F32)
+                    total += self.came[q + 1].astype(F32)
                 if q < n2 - 1:
                     self.leftward(q).wait_recv()
-                    total += self.from_right[q].astype(F32)
+                    total += self.came[q].astype(F32)
                 self.o_ref[...] = total
 
         for q in range(n2):
@@ -355,6 +354,535 @@
             collective_id=collective_id, has_side_effects=True, vmem_limit_bytes=48 << 20
         ),
     )(*[op.x for op in ops])
+
+
+def meet(axes):
+    barrier = pltpu.get_barrier_semaphore()
+    for axis, size in axes:
+        me = lax.axis_index(axis)
+        for k in range(1, size):
+            peer = {axis: lax.rem(me + k, size)}
+            pl.semaphore_signal(barrier, inc=1, device_id=peer, device_id_type=MESH)
+    pl.semaphore_wait(barrier, sum(size - 1 for _, size in axes))
+
+
+def ffn_kernel(
+    dims,
+    ops,
+    n2_own,
+    gw_in,
+    dw_in,
+    cot_in,
+    gu_a_in,
+    down_b,
+    dn_sum,
+    ffn_part,
+    g_gw,
+    g_down,
+    g_gu_a,
+    g_down_b,
+    n2,
+    gw,
+    gb,
+    dw,
+    cot_u,
+    gu_a,
+    u_gu,
+    act,
+    d_gu,
+    d_u_gu,
+    u_down,
+    dn,
+    stage,
+    stage_sem,
+    cot_sem,
+    *sems,
+):
+    S, F, R, seg, kb, rb, hb, hl, hp = dims
+    own = R * seg
+    width = n2_own.shape[1]
+    tokens = S * own
+    G = S // R
+    gather, scatter = ops
+    take = len(gather.scratch)
+    gather.bind(n2_own, n2, *sems[:take])
+    scatter.bind(dn, dn_sum, *sems[take:])
+    meet([("seq", S)])
+    gather.start()
+
+    def fetch(s):
+        return pltpu.make_async_copy(gw_in.at[s], stage.at[s % 2], stage_sem.at[s % 2])
+
+    fetch(0).start()
+    moves = []
+    for j in range(S):
+        row, i = j // G, j % G
+        for e in range(R):
+            at = j * own + e * seg
+            src = cot_in.at[i * R + e, pl.ds(row * seg, seg), :]
+            dst = cot_u.at[pl.ds(at, seg), pl.ds(0, width)]
+            moves.append(pltpu.make_async_copy(src, dst, cot_sem.at[len(moves)]))
+            moves[-1].start()
+
+    for s in range(S):
+        if s + 1 < S:
+            fetch(s + 1).start()
+        fetch(s).wait()
+        for f in range(F):
+            b = s * F + f
+            gw[b * kb : b * kb + kb, :] = stage[s % 2, f, 0:kb, :]
+            gb[b * rb : b * rb + rb, :] = stage[s % 2, f, kb : kb + rb, :]
+            gu_a[b * kb : b * kb + kb, :] = gu_a_in[s, f]
+        if s + 1 <= gather.steps:
+            gather.step(s + 1)
+    for f in range(F):
+        dw[f * hb : f * hb + hb, :] = dw_in[f]
+    if hp > hl:
+        dw[hl:hp, :] = jnp.zeros((hp - hl, dw.shape[1]), BF)
+    for move in moves:
+        move.wait()
+    tile = 256
+    tiles = tokens // tile
+
+    @pl.loop(0, tiles)
+    def _(t):
+        rows = pl.ds(pl.multiple_of(t * tile, tile), tile)
+        cot_u[rows, width:] = mm_nt(cot_u[rows, :width], down_b[...]).astype(BF)
+
+    gather.finish()
+    inner = math.sqrt(2.0 / math.pi)
+    per_tile = tile // own
+
+    @pl.loop(0, tiles)
+    def _(t):
+        rows = pl.ds(pl.multiple_of(t * tile, tile), tile)
+        n = n2[pl.ds(t * per_tile, per_tile)].reshape(tile, width)
+        u = mm(n, gu_a[...]).astype(BF)
+        u_gu[rows, :] = u
+        d_act = mm_nt(cot_u[rows, :], dw[...])
+        gate = mm(n, gw[:, :hp]) + mm(u[:, :RANK], gb[:, :hp])
+        up = mm(n, gw[:, hp:]) + mm(u[:, RANK:], gb[:, hp:])
+        square = gate * gate
+        th = jnp.tanh(inner * gate * (1.0 + 0.044715 * square))
+        half = 0.5 * (1.0 + th)
+        gelu = gate * half
+        act[rows, :] = (gelu * up).astype(BF)
+        slope = half + 0.5 * gate * (1.0 - th * th) * (inner * (1.0 + 3 * 0.044715 * square))
+        d_gate = (d_act * up * slope).astype(BF)
+        d_up = (d_act * gelu).astype(BF)
+        d_gu[rows, :hp] = d_gate
+        d_gu[rows, hp:] = d_up
+        d_u_gu[rows, :RANK] = mm_nt(d_gate, gb[:, :hp]).astype(BF)
+        d_u_gu[rows, RANK:] = mm_nt(d_up, gb[:, hp:]).astype(BF)
+        out = mm_nt(d_gu[rows, :], gw[...]) + mm_nt(d_u_gu[rows, :], gu_a[...])
+        dn[pl.ds(t * per_tile, per_tile)] = out.astype(BF).reshape(per_tile, own, width)
+
+    scatter.start()
+
+    @pl.loop(0, tiles)
+    def _(t):
+        rows = pl.ds(pl.multiple_of(t * tile, tile), tile)
+        out = mm(act[rows, :], dw[...])
+        low = out[:, width:].astype(BF)
+        u_down[rows, :] = low
+        out = out[:, :width] + mm(low, down_b[...])
+        ffn_part[pl.ds(t * per_tile, per_tile)] = out.astype(BF).reshape(per_tile, own, width)
+
+    scatter.step(1)
+    for half in range(2):
+        cols = slice(half * hp, half * hp + hp)
+        out = mm_tn(u_gu[:, half * RANK : half * RANK + RANK], d_gu[:, cols]).astype(BF)
+        for b in range(S * F):
+            g_gw[b % F, b // F, kb : kb + rb, cols] = out[b * rb : b * rb + rb, :]
+    if scatter.steps >= 2:
+        scatter.step(2)
+    g_down_b[...] = mm_tn(u_down[...], cot_u[:, :width]).astype(BF)
+    step = 128
+    n_all = n2[...].reshape(tokens, width)
+
+    @pl.loop(0, cot_u.shape[1] // step)
+    def _(t):
+        cols = pl.ds(pl.multiple_of(t * step, step), step)
+        out = mm_tn(act[...], cot_u[:, cols]).astype(BF)
+        for f in range(F):
+            g_down[f, :, cols] = out[f * hb : f * hb + hb, :]
+
+    for d in range(3, scatter.steps + 1):
+        scatter.step(d)
+    step = 256
+
+    @pl.loop(0, 2 * hp // step)
+    def _(t):
+        cols = pl.ds(pl.multiple_of(t * step, step), step)
+        out = mm_tn(n2[...].reshape(tokens, width), d_gu[:, cols]).astype(BF)
+        for b in range(S * F):
+            g_gw[b % F, b // F, 0:kb, cols] = out[b * kb : b * kb + kb, :]
+
+    scatter.finish()
+    out = mm_tn(n2[...].reshape(tokens, width), d_u_gu[...]).astype(BF)
+    for b in range(S * F):
+        g_gu_a[b // F, b % F] = out[b * kb : b * kb + kb, :]
+
+
+def feed_forward(n2_own, gw, dw, cot, gu_a, down_b, dims, collective_id):
+    S, F, R, seg, kb, rb, hb, hl, hp = dims
+    own, width = n2_own.shape
+    tokens = S * own
+    gather = Line(n2_own, S)
+    scatter = LineSum(jax.ShapeDtypeStruct((S, own, width), BF), S)
+    vmem = pl.BlockSpec(memory_space=pltpu.VMEM)
+    away = pl.BlockSpec(memory_space=pl.ANY)
+    low = functools.partial(jax.ShapeDtypeStruct, dtype=BF)
+    lora = width + RANK
+    return pl.pallas_call(
+        functools.partial(ffn_kernel, dims, (gather, scatter)),
+        out_shape=[
+            jax.ShapeDtypeStruct((own, width), F32),
+            low((S, own, width)),
+            low((F, S, kb + rb, 2 * hp)),
+            low((F, hb, lora)),
+            low((S, F, kb, 2 * RANK)),
+            low((RANK, width)),
+        ],
+        in_specs=[vmem, away, vmem, away, vmem, vmem],
+        out_specs=[vmem] * 6,
+        scratch_shapes=[
+            pltpu.VMEM(shape, BF)
+            for shape in (
+                (S, own, width),
+                (width, 2 * hp),
+                (RANK, 2 * hp),
+                (hp, lora),
+                (tokens, lora),
+                (width, 2 * RANK),
+                (tokens, 2 * RANK),
+                (tokens, hp),
+                (tokens, 2 * hp),
+                (tokens, 2 * RANK),
+                (tokens, RANK),
+                (S, own, width),
+                (2, F, kb + rb, 2 * hp),
+            )
+        ]
+        + [pltpu.SemaphoreType.DMA((2,)), pltpu.SemaphoreType.DMA((S * R,))]
+        + gather.scratch
+        + scatter.scratch,
+        compiler_params=pltpu.CompilerParams(
+            collective_id=collective_id, has_side_effects=True, vmem_limit_bytes=62 << 20
+        ),
+    )(n2_own, gw, dw, cot, gu_a, down_b)
+
+
+class Bag:
+    pass
+
+
+def norm_back(G_in, h, g):
+    q = lax.rsqrt(jnp.mean(h * h, axis=-1, keepdims=True) + EPSILON)
+    gg = G_in * g
+    d_gain = jnp.sum(G_in * (h * q), axis=0, keepdims=True)
+    return d_gain, q * gg - h * (q * q * q) * jnp.mean(gg * h, axis=-1, keepdims=True)
+
+
+def back_kernel(dims, names, ops, *refs):
+    S, F, R, seg, L, kb, rb, hb, ob = dims
+    v = Bag()
+    for name, ref in zip(names, refs):
+        setattr(v, name, ref)
+    rest = list(refs[len(names) :])
+    bound = Bag()
+    for name, (op, src, dst) in ops.items():
+        take = len(op.scratch)
+        op.bind(getattr(v, src), getattr(v, dst), *rest[:take])
+        setattr(bound, name, op)
+        rest = rest[take:]
+    t = bound
+    own = R * seg
+    G = S // R
+    C = G // HEADS
+    qlen = L // C
+    width = v.resid.shape[1]
+    scale = HEAD**-0.5
+    s = lax.axis_index("seq")
+    chunk = lax.rem(s, C)
+    meet([("seq", S), ("fsdp", F)])
+    t.gw.start()
+    t.down.start()
+
+    gain_two, back = norm_back(v.d_n2[...], v.resid[...], v.gains[1:2, :])
+    d_resid = v.cot_own[...].astype(F32) + back
+    v.d_resid[...] = d_resid
+    v.d_attn_own[...] = d_resid.astype(BF)
+    t.d_attn.start()
+    early = [t.ffn, t.gu_a, t.down_b] if "ffn" in ops else [t.gu_a, t.down_b]
+    for op in early:
+        op.start()
+    for d in range(1, t.d_attn.steps + 1):
+        t.d_attn.step(d)
+    t.d_attn.finish()
+
+    blocks = qlen // own
+    first = chunk * blocks
+    v.da[:, :width] = v.d_attn[pl.ds(first, blocks)].reshape(qlen, width)
+    v.da[:, width:] = mm_nt(v.da[:, :width], v.out_b[...]).astype(BF)
+    v.d_mixed[...] = mm_nt(v.da[...], v.wo[...]).astype(BF)
+
+    @pl.loop(0, qlen // 128)
+    def _(i):
+        rows = pl.ds(pl.multiple_of(i * 128, 128), 128)
+        p = v.probs[rows, :]
+        d_probs = mm_nt(v.d_mixed[rows, :], v.value[...])
+        delta = jnp.sum(p * d_probs, axis=-1, keepdims=True)
+        v.d_scores[rows, :] = (p * (d_probs - delta)).astype(BF)
+        v.probs_low[rows, :] = p.astype(BF)
+
+    def unrot(g, rows):
+        half = HEAD // 2
+        cosine, sine = v.cosine[rows, :], v.sine[rows, :]
+        a, b = g[:, :half], g[:, half:]
+        return (a * cosine + b * sine).astype(BF), (b * cosine - a * sine).astype(BF)
+
+    half = HEAD // 2
+    mine = pl.ds(pl.multiple_of(chunk * qlen, own), qlen)
+    if C > 1:
+        v.d_pu[:, :HEAD] = jnp.zeros((L, HEAD), BF)
+    v.d_pu[mine, :half], v.d_pu[mine, half:HEAD] = unrot(mm(v.d_scores[...], v.key[...]) * scale, mine)
+    every = pl.ds(0, L)
+    v.d_pu[:, HEAD : HEAD + half], v.d_pu[:, HEAD + half : 2 * HEAD] = unrot(
+        mm_tn(v.d_scores[...], v.query[...]) * scale, every
+    )
+    v.d_pu[:, 2 * HEAD : 3 * HEAD] = mm_tn(v.probs_low[...], v.d_mixed[...]).astype(BF)
+    for k in range(3):
+        v.d_pu[:, 3 * HEAD + k * RANK : 3 * HEAD + (k + 1) * RANK] = mm_nt(
+            v.d_pu[:, k * HEAD : (k + 1) * HEAD], v.up_b[k]
+        ).astype(BF)
+
+    @pl.loop(0, L // 256)
+    def _(i):
+        rows = pl.ds(pl.multiple_of(i * 256, 256), 256)
+        out = mm_nt(v.d_pu[rows, :], v.w1[...]).astype(BF)
+        v.d_attn[pl.ds(i * (256 // own), 256 // own)] = out.reshape(256 // own, own, width)
+
+    t.d_n1.start()
+    for op in early:
+        op.step(1)
+
+    out = mm_tn(v.mixed[...], v.da[...]).astype(BF)
+    for j in range(HEAD // ob):
+        v.t_out[j % F, j // F] = out[j * ob : j * ob + ob, :]
+    t.out.start()
+    out = mm_tn(v.norm_one[...], v.d_pu[:, :HEAD]).astype(BF)
+    for b in range(S * F):
+        v.t_q[b % F, b // F] = out[b * kb : b * kb + kb, :]
+    t.q.start()
+    out = mm_tn(v.u[:, :RANK], v.d_pu[:, :HEAD]).astype(BF)
+    for b in range(S * F):
+        v.t_qb[b % F, b // F] = out[b * rb : b * rb + rb, :]
+    t.qb.start()
+    t.d_n1.step(1)
+
+    @pl.loop(0, v.t_1.shape[3] // 256)
+    def _(i):
+        cols = pl.ds(pl.multiple_of(i * 256, 256), 256)
+        src = pl.ds(pl.multiple_of(i * 256 + 256, 256), 256)
+        out = mm_tn(v.norm_one[...], v.d_pu[:, src]).astype(BF)
+        for b in range(S * F):
+            v.t_1[b // F, b % F, :, cols] = out[b * kb : b * kb + kb, :]
+
+    t.one.start()
+    for d in range(2, t.d_n1.steps + 1):
+        t.d_n1.step(d)
+    for k in range(2):
+        out = mm_tn(
+            v.u[:, (k + 1) * RANK : (k + 2) * RANK], v.d_pu[:, (k + 1) * HEAD : (k + 2) * HEAD]
+        ).astype(BF)
+        for b in range(S * F):
+            v.t_2[b // F, b % F, :, k * HEAD : (k + 1) * HEAD] = out[b * rb : b * rb + rb, :]
+    out = mm_tn(v.u_out[...], v.d_attn_own[...]).astype(BF)
+    for b in range(S * F):
+        v.t_2[b // F, b % F, :, 2 * HEAD :] = out[b * rb : b * rb + rb, :]
+    t.two.start()
+
+    t.d_n1.finish()
+    gain_one, back = norm_back(v.d_n1_sum[...], v.x_own[...].astype(F32), v.gains[0:1, :])
+    grad_input = v.d_resid[...] + back
+    for j in range(R):
+        v.grad_rows[j] = grad_input[j * seg : j * seg + seg, :]
+    t.grad_input.start()
+    both = jnp.concatenate([gain_one, gain_two, jnp.zeros((126, width), F32)], axis=0)
+    both = jnp.transpose(both)
+    for b in range(S * F):
+        v.t_3[b // F, b % F] = both[b * kb : b * kb + kb, :].astype(BF)
+    t.three.start()
+    for d in range(2, t.gu_a.steps + 1):
+        for op in early:
+            op.step(d)
+    late = [t.one, t.two, t.three]
+    for op in late:
+        op.step(1)
+    for op in early:
+        op.finish()
+    activations = (v.resid[...] + v.ffn_sum[...]).astype(BF)
+    for j in range(R):
+        v.act_rows[j] = activations[j * seg : j * seg + seg, :]
+    t.activations.start()
+
+    def total(ref, at):
+        out = ref[(0,) + at].astype(F32)
+        for f in range(1, F):
+            out += ref[(f,) + at].astype(F32)
+        return out
+
+    for name in ("q", "qb", "out"):
+        getattr(t, name).finish()
+        got, put = getattr(v, "r_" + name), getattr(v, "s_" + name)
+        for k in range(put.shape[0]):
+            put[k] = total(got, (k,)).astype(BF)
+        getattr(t, name + "_home").start()
+    for d in range(2, t.one.steps + 1):
+        for op in late:
+            op.step(d)
+    t.gw.finish()
+
+    @pl.loop(0, S)
+    def _(k):
+        v.s_gw[k] = total(v.r_gw, (k,)).astype(BF)
+
+    t.gw_home.start()
+    for op in late:
+        op.finish()
+    for name in ("one", "two", "three", "gu_a", "down_b"):
+        getattr(v, "s_" + name)[...] = getattr(v, "f_" + name)[...].astype(BF)
+        getattr(t, name + "_home").start()
+    t.down.finish()
+    v.g_down[...] = total(v.r_down, ())
+    for name in ("grad_input", "activations", "q_home", "qb_home", "out_home", "gw_home"):
+        getattr(t, name).finish()
+    for name in ("one", "two", "three", "gu_a", "down_b"):
+        getattr(t, name + "_home").finish()
+
+
+def backward(given, dims, collective_id):
+    S, F, R, seg, L, kb, rb, hb, ob = dims
+    own = R * seg
+    G = S // R
+    C = G // HEADS
+    qlen = L // C
+    width = given["resid"].shape[1]
+    per_head = S // HEADS
+    hp2 = given["g_gw"].shape[3]
+    lora = width + RANK
+    one = 2 * HEAD + 3 * RANK
+    two = 2 * HEAD + width
+    low = functools.partial(jax.ShapeDtypeStruct, dtype=BF)
+    full = functools.partial(jax.ShapeDtypeStruct, dtype=F32)
+
+    def to_rows(at):
+        return [(j, lax.rem(at, G) * R + j, at // G) for j in range(R)]
+
+    def to_out(at):
+        return [
+            (j, lax.rem(at, G) // C * per_head + j, at // G * C + lax.rem(at, C)) for j in range(per_head)
+        ]
+
+    outs = {
+        "act_home": low((R, seg, width)),
+        "grad_home": full((R, seg, width)),
+        "o_q": low((S, kb, HEAD)),
+        "o_qb": low((S, rb, HEAD)),
+        "o_out": low((R * C, ob, lora)),
+        "o_gw": low((S, kb + rb, hp2)),
+        "o_one": low((F, kb, one)),
+        "o_two": low((F, rb, two)),
+        "o_three": low((F, kb, 128)),
+        "o_gu_a": low((F, kb, 2 * RANK)),
+        "o_down_b": low((F, rb, width)),
+        "g_down": full((hb, lora)),
+    }
+    scratch = {
+        "d_resid": full((own, width)),
+        "d_attn_own": low((own, width)),
+        "d_attn": low((G, own, width)),
+        "da": low((qlen, lora)),
+        "d_mixed": low((qlen, HEAD)),
+        "d_scores": low((qlen, L)),
+        "probs_low": low((qlen, L)),
+        "d_pu": low((L, 3 * HEAD + 3 * RANK)),
+        "d_n1_sum": full((own, width)),
+        "grad_rows": full((R, seg, width)),
+        "act_rows": low((R, seg, width)),
+        "ffn_sum": full((own, width)),
+        "t_out": low((F, per_head, ob, lora)),
+        "t_q": low((F, S, kb, HEAD)),
+        "t_qb": low((F, S, rb, HEAD)),
+        "t_1": low((S, F, kb, one)),
+        "t_2": low((S, F, rb, two)),
+        "t_3": low((S, F, kb, 128)),
+        "r_out": low((F, per_head, ob, lora)),
+        "r_q": low((F, S, kb, HEAD)),
+        "r_qb": low((F, S, rb, HEAD)),
+        "r_gw": low((F, S, kb + rb, hp2)),
+        "r_down": low((F, hb, lora)),
+        "s_out": low((per_head, ob, lora)),
+        "s_q": low((S, kb, HEAD)),
+        "s_qb": low((S, rb, HEAD)),
+        "s_gw": low((S, kb + rb, hp2)),
+    }
+    for name, rows, cols in (
+        ("one", kb, one),
+        ("two", rb, two),
+        ("three", kb, 128),
+        ("gu_a", kb, 2 * RANK),
+        ("down_b", rb, width),
+    ):
+        scratch["f_" + name] = full((F, rows, cols))
+        scratch["s_" + name] = low((F, rows, cols))
+    if "ffn_sum" in given:
+        scratch.pop("ffn_sum")
+    arrays = {**given, **outs, **scratch}
+
+    def op(kind, src, dst, *more):
+        return kind(arrays[src], *more), src, dst
+
+    ops = {
+        "gw": op(Direct, "g_gw", "r_gw", "fsdp", F),
+        "down": op(Direct, "g_dw", "r_down", "fsdp", F),
+        "d_attn": op(Line, "d_attn_own", "d_attn", G),
+        "gu_a": op(LineSum, "g_gu_a", "f_gu_a", S),
+        "down_b": op(LineSum, "g_down_b", "f_down_b", S),
+        "d_n1": op(LineSum, "d_attn", "d_n1_sum", G),
+        "out": op(Direct, "t_out", "r_out", "fsdp", F),
+        "q": op(Direct, "t_q", "r_q", "fsdp", F),
+        "qb": op(Direct, "t_qb", "r_qb", "fsdp", F),
+        "one": op(LineSum, "t_1", "f_one", S),
+        "two": op(LineSum, "t_2", "f_two", S),
+        "three": op(LineSum, "t_3", "f_three", S),
+        "grad_input": op(Post, "grad_rows", "grad_home", R, to_rows),
+        "activations": op(Post, "act_rows", "act_home", R, to_rows),
+        "q_home": op(Direct, "s_q", "o_q", "seq", S),
+        "qb_home": op(Direct, "s_qb", "o_qb", "seq", S),
+        "out_home": op(Post, "s_out", "o_out", R * C, to_out),
+        "gw_home": op(Direct, "s_gw", "o_gw", "seq", S),
+    }
+    if "ffn_part" in given:
+        ops["ffn"] = op(LineSum, "ffn_part", "ffn_sum", S)
+    for name in ("one", "two", "three", "gu_a", "down_b"):
+        ops[name + "_home"] = op(Direct, "s_" + name, "o_" + name, "fsdp", F)
+    vmem = pl.BlockSpec(memory_space=pltpu.VMEM)
+    away = pl.BlockSpec(memory_space=pl.ANY)
+    names = list(given) + list(outs) + list(scratch)
+    result = pl.pallas_call(
+        functools.partial(back_kernel, dims, names, ops),
+        out_shape=list(outs.values()),
+        in_specs=[away if name in ("g_gw", "g_dw") else vmem for name in given],
+        out_specs=[vmem if name == "g_down" else away for name in outs],
+        scratch_shapes=[pltpu.VMEM(a.shape, a.dtype) for a in scratch.values()]
+        + [entry for kind, _, _ in ops.values() for entry in kind.scratch],
+        compiler_params=pltpu.CompilerParams(
+            collective_id=collective_id, has_side_effects=True, vmem_limit_bytes=62 << 20
+        ),
+    )(*given.values())
+    return dict(zip(outs, result))
 
 
 def norm_apply(hidden, gain):
@@ -414,6 +942,7 @@
     ob = w_out.shape[0]
     hidden = w_gu.shape[1] // 2
     hl = hidden // S
+    hp = (hl + 127) // 128 * 128
     s = lax.axis_index("seq")
     r = s // G
     head = lax.rem(s, G) // C
@@ -426,13 +955,12 @@
     pack1 = jnp.concatenate([w_qkv, qkv_a, gains], axis=1)
     pack2 = jnp.concatenate([q_b, kv_b[0], kv_b[1], out_b], axis=1)
     pack3 = jnp.concatenate([w_out, out_a], axis=1)
-    gw = jnp.concatenate(
-        [
-            jnp.concatenate([w_gu[:, :hidden].reshape(kb, S, hl), w_gu[:, hidden:].reshape(kb, S, hl)], axis=2),
-            jnp.concatenate([gu_b[0].reshape(rb, S, hl), gu_b[1].reshape(rb, S, hl)], axis=2),
-        ],
-        axis=0,
-    ).transpose(1, 0, 2)
+
+    def shares(w):
+        w = w.reshape(w.shape[0], 2, S, hl).transpose(2, 0, 1, 3)
+        return jnp.pad(w, ((0, 0), (0, 0), (0, 0), (0, hp - hl))).reshape(S, w.shape[1], 2 * hp)
+
+    gw = shares(jnp.concatenate([w_gu, jnp.concatenate([gu_b[0], gu_b[1]], axis=1)], axis=0))
     p1, p2, p3, gw, f_gu_a, f_down_b = transfer(
         [Direct(x, "fsdp", F, True) for x in (pack1, pack2, pack3)]
         + [Direct(gw, "seq", S)]
@@ -444,7 +972,7 @@
     gw = lax.all_gather(gw, "fsdp", axis=1)
     dw = lax.all_gather(dw, "fsdp", axis=0)
     cot = lax.all_gather(cotangent.reshape(own, width), "seq", axis=0)
-    f_gu_a = lax.all_gather(f_gu_a, "seq", axis=0).reshape(width, 2 * RANK)
+    f_gu_a = lax.all_gather(f_gu_a, "seq", axis=0)
     f_down_b = lax.all_gather(f_down_b, "seq", axis=0).reshape(RANK, width)
     ids = jnp.pad(document_numbers[:, None, :], ((0, 0), (0, 7), (0, 128 - seg)))
 
@@ -460,12 +988,7 @@
     p2 = p2.reshape(RANK, -1)
     wo = wo.reshape(HEAD, -1)
     xrow = lax.dynamic_index_in_dim(xin, r, 1, keepdims=False).reshape(L, width).astype(F32)
-    cot = cot.reshape(S, R, seg, width).transpose(1, 0, 2, 3).reshape(R * L, width)
     ids = lax.dynamic_index_in_dim(ids[:, :, 0, :seg], r, 1, keepdims=False).reshape(L)
-    gb = gw[:, :, kb:].reshape(RANK, 2 * hl)
-    gw = gw[:, :, :kb].reshape(width, 2 * hl)
-    dw = dw.reshape(hl, -1)
-
     q0 = HEADS * HEAD
     wq = lax.dynamic_slice_in_dim(p1, head * HEAD, HEAD, 1)
     w1 = jnp.concatenate([wq, p1[:, q0 : q0 + 2 * HEAD + 3 * RANK]], axis=1)
@@ -510,157 +1033,81 @@
     x_own = lax.dynamic_slice_in_dim(xrow, mine, own, 0)
     resid = x_own + attn[:, :width] + mm(u_out, f_out_b)
     norm_two_own = norm_apply(resid, gain_two).astype(BF)
-    (norm_two,) = transfer([Line(norm_two_own, S)], [on_seq], 5)
-    norm_two = norm_two.reshape(R * L, width)
-
-    u_gu = mm(norm_two, f_gu_a).astype(BF)
-    gu = mm(norm_two, gw)
-    gate = gu[:, :hl] + mm(u_gu[:, :RANK], gb[:, :hl])
-    up = gu[:, hl:] + mm(u_gu[:, RANK:], gb[:, hl:])
-    d_u_down = mm_nt(cot, f_down_b).astype(BF)
-    cot_u = jnp.concatenate([cot, d_u_down], axis=1)
-    d_act = mm_nt(cot_u, dw)
-    inner = math.sqrt(2.0 / math.pi)
-    th = jnp.tanh(inner * (gate + 0.044715 * gate * gate * gate))
-    gelu = 0.5 * gate * (1.0 + th)
-    act = (gelu * up).astype(BF)
-    slope = 0.5 * (1.0 + th) + 0.5 * gate * (1.0 - th * th) * inner * (1.0 + 3 * 0.044715 * gate * gate)
-    d_gate = (d_act * up * slope).astype(BF)
-    d_up = (d_act * gelu).astype(BF)
-    d_gu = jnp.concatenate([d_gate, d_up], axis=1)
-    d_u_gu = jnp.concatenate(
-        [mm_nt(d_gate, gb[:, :hl]), mm_nt(d_up, gb[:, hl:])], axis=1
-    ).astype(BF)
-    d_norm_two = (mm_nt(d_gu, gw) + mm_nt(d_u_gu, f_gu_a)).astype(BF)
-    (d_norm_two,) = transfer([LineSum(d_norm_two.reshape(S, own, width), S)], [on_seq], 6)
-    ffn = mm(act, dw)
-    u_down = ffn[:, width:].astype(BF)
-    ffn = (ffn[:, :width] + mm(u_down, f_down_b)).astype(BF)
-    (ffn,) = transfer([LineSum(ffn.reshape(S, own, width), S)], [on_seq], 7)
-    activations = (resid + ffn).astype(BF)
-    g_down = mm_tn(act, cot_u)
-    g_down_b = mm_tn(u_down, cot)
-    g_gu = mm_tn(norm_two, d_gu)
-    g_gu_b = jnp.concatenate([mm_tn(u_gu[:, :RANK], d_gate), mm_tn(u_gu[:, RANK:], d_up)], axis=1)
-    g_gu_a = mm_tn(norm_two, d_u_gu)
-
-    def split(g, rows):
-        return g.astype(BF).reshape(-1, F, rows, g.shape[1]).transpose(1, 0, 2, 3)
-
-    def scatter(g, axes):
-        return lax.psum_scatter(g, axes, scatter_dimension=0, tiled=True)[0]
-
-    g_gu = scatter(jnp.concatenate([split(g_gu, kb), split(g_gu_b, rb)], axis=2), "fsdp")
-    g_down = scatter(g_down.astype(BF).reshape(F, hb, -1), "fsdp").astype(F32)
-    g_gu_a = scatter(g_gu_a.astype(BF).reshape(S * F, kb, -1), ("seq", "fsdp")).astype(F32)
-    g_down_b = scatter(g_down_b.astype(BF).reshape(S * F, rb, -1), ("seq", "fsdp")).astype(F32)
-
-    def norm_back(G_in, h, g):
-        q = lax.rsqrt(jnp.mean(h * h, axis=-1, keepdims=True) + EPSILON)
-        gg = G_in * g
-        d_gain = jnp.sum(G_in * (h * q), axis=0)
-        return d_gain, q * gg - h * (q * q * q) * jnp.mean(gg * h, axis=-1, keepdims=True)
-
-    d_gain_two, back = norm_back(d_norm_two, resid, gain_two)
-    cot_own = lax.dynamic_slice_in_dim(cot, s * own, own, 0)
-    d_resid = cot_own.astype(F32) + back
-
-    d_attn_own = d_resid.astype(BF)
-    (d_attn,) = transfer([Line(d_attn_own, G)], [on_seq], 8)
-    d_attn = d_attn.reshape(L, width)
-    g_out_b = mm_tn(u_out, d_attn_own)
-    if C > 1:
-        d_attn = lax.dynamic_slice_in_dim(d_attn, chunk * qlen, qlen, 0)
-    d_u_out = mm_nt(d_attn, f_out_b).astype(BF)
-    d_attn_u = jnp.concatenate([d_attn, d_u_out], axis=1)
-    d_mixed = mm_nt(d_attn_u, wo).astype(BF)
-    g_out = mm_tn(mixed, d_attn_u)
-    d_probs = mm_nt(d_mixed, value)
-    delta = jnp.sum(probs * d_probs, axis=-1, keepdims=True)
-    d_scores = (probs * (d_probs - delta)).astype(BF)
-    d_query = mm(d_scores, key) * scale
-    d_key = mm_tn(d_scores, query_c) * scale
-    d_value = mm_tn(probs_low, d_mixed)
-    if C > 1:
-        d_query = lax.dynamic_update_slice_in_dim(jnp.zeros((L, HEAD), F32), d_query, chunk * qlen, 0)
-    dq = unrotate(d_query, cosine, sine).astype(BF)
-    dk = unrotate(d_key, cosine, sine).astype(BF)
-    dv = d_value.astype(BF)
-    d_u = [mm_nt(dq, f_q_b).astype(BF), mm_nt(dk, f_k_b).astype(BF), mm_nt(dv, f_v_b).astype(BF)]
-    d_pu = jnp.concatenate([dq, dk, dv] + d_u, axis=1)
-    d_norm_one = mm_nt(d_pu, w1).astype(BF)
-    (d_norm_one,) = transfer([LineSum(d_norm_one.reshape(G, own, width), G)], [on_seq], 9)
-    g_w1 = mm_tn(norm_one, d_pu)
-    g_q_b = mm_tn(u_q, dq)
-    g_kv_b = [mm_tn(u_k, dk), mm_tn(u_v, dv)]
-    d_gain_one, back_one = norm_back(d_norm_one, x_own, gain_one)
-    grad_input = d_resid + back_one
-
-    d_gains = jnp.pad(jnp.stack([d_gain_one, d_gain_two], axis=1), ((0, 0), (0, 126)))
-    t_1 = jnp.concatenate([g_w1[:, HEAD:], d_gains], axis=1).astype(BF).reshape(S, F, kb, -1)
-    t_2 = jnp.concatenate(g_kv_b + [g_out_b], axis=1).astype(BF).reshape(S, F, rb, -1)
-    t_1, t_2, t_q, t_qb, t_out = transfer(
-        [LineSum(t_1, S), LineSum(t_2, S)]
-        + [Direct(x, "fsdp", F) for x in (split(g_w1[:, :HEAD], kb), split(g_q_b, rb), split(g_out, ob))],
-        [on_seq, on_fsdp],
-        10,
+
+    dims = (S, F, R, seg, kb, rb, hb, hl, hp)
+    d_norm_two, ffn, g_gu, g_down, g_gu_a, g_down_b = feed_forward(
+        norm_two_own, gw, dw, cot, f_gu_a, f_down_b, dims, 5
+    )
+    cot_own = lax.dynamic_slice_in_dim(cot, lax.rem(s, G) * R, R, 0).reshape(R, R, seg, width)
+    cot_own = lax.dynamic_index_in_dim(cot_own, r, 1, keepdims=False).reshape(own, width)
+
+    ffn = {"ffn_part": ffn}
+    if S * own > 1024:
+        ffn = {"ffn_sum": transfer([LineSum(ffn["ffn_part"], S)], [on_seq], 7)[0]}
+    got = backward(
+        dict(
+            d_n2=d_norm_two,
+            resid=resid,
+            gains=jnp.pad(jnp.stack([gain_one, gain_two]), ((0, 6), (0, 0))),
+            cot_own=cot_own,
+            x_own=x_own.astype(BF),
+            out_b=f_out_b,
+            wo=wo,
+            w1=w1,
+            up_b=jnp.stack([f_q_b, f_k_b, f_v_b]),
+            norm_one=norm_one,
+            u=u,
+            u_out=u_out,
+            query=query_c,
+            key=key,
+            value=value,
+            cosine=cosine,
+            sine=sine,
+            probs=probs,
+            mixed=mixed,
+            **ffn,
+            g_gw=g_gu,
+            g_dw=g_down,
+            g_gu_a=g_gu_a,
+            g_down_b=g_down_b.reshape(S, F, rb, width),
+        ),
+        (S, F, R, seg, L, kb, rb, hb, ob),
+        8,
     )
 
     def total(t):
         return jnp.sum(t.astype(F32), axis=0)
-
-    per = own // seg
-
-    def to_rows(at):
-        return [(j, lax.rem(at, G) * per + j, at // G) for j in range(per)]
-
-    def to_out(at):
-        return [
-            (j, lax.rem(at, G) // C * per_head + j, at // G * C + lax.rem(at, C)) for j in range(per_head)
-        ]
-
-    t_1, t_2, t_q, t_qb, t_gu, t_out, activations, grad_input = transfer(
-        [Direct(t.astype(BF), "fsdp", F) for t in (t_1, t_2)]
-        + [Direct(t.astype(BF), "seq", S) for t in (total(t_q), total(t_qb), g_gu)]
-        + [Post(total(t_out).astype(BF), R * C, to_out)]
-        + [Post(t.reshape(per, seg, width), R, to_rows) for t in (activations, grad_input)],
-        [on_seq, on_fsdp],
-        11,
-    )
 
     def by_head(t):
         t = t.astype(F32).reshape(R, HEADS, C, t.shape[1], HEAD).sum(axis=(0, 2))
         return t.transpose(1, 0, 2).reshape(t.shape[1], HEADS * HEAD)
 
     def halves(t):
-        t = t.astype(F32).reshape(S, t.shape[1], 2, hl).transpose(2, 1, 0, 3)
-        return t.reshape(2, t.shape[1], hidden)
-
-    t_1, t_2, g_out = total(t_1), total(t_2), total(t_out)
-    grad_w_qkv = jnp.concatenate([by_head(t_q), t_1[:, : 2 * HEAD]], axis=1)
-    g_qkv_a = t_1[:, 2 * HEAD : 2 * HEAD + 3 * RANK]
-    d_gain_one = t_1[:, 2 * HEAD + 3 * RANK]
-    d_gain_two = t_1[:, 2 * HEAD + 3 * RANK + 1]
-    g_gu_b = halves(t_gu[:, kb:])
-    g_gu = halves(t_gu[:, :kb])
+        rows = t.shape[1]
+        t = t.astype(F32).reshape(S, rows, 2, hp)[..., :hl].transpose(2, 1, 0, 3)
+        return t.reshape(2, rows, hidden)
+
+    t_1, t_2, t_3, g_out = (total(got[name]) for name in ("o_one", "o_two", "o_three", "o_out"))
+    g_gu = halves(got["o_gw"][:, :kb])
+    g_down = got["g_down"]
     return (
-        activations,
-        grad_input,
-        grad_w_qkv,
-        g_qkv_a,
-        by_head(t_qb),
+        got["act_home"],
+        got["grad_home"],
+        jnp.concatenate([by_head(got["o_q"]), t_1[:, : 2 * HEAD]], axis=1),
+        t_1[:, 2 * HEAD :],
+        by_head(got["o_qb"]),
         jnp.stack([t_2[:, :HEAD], t_2[:, HEAD : 2 * HEAD]]),
         g_out[:, :width],
         g_out[:, width:],
         t_2[:, 2 * HEAD :],
         jnp.concatenate([g_gu[0], g_gu[1]], axis=1),
-        g_gu_a,
-        g_gu_b,
+        total(got["o_gu_a"]),
+        halves(got["o_gw"][:, kb:]),
         g_down[:, :width],
         g_down[:, width:],
-        g_down_b,
-        d_gain_one,
-        d_gain_two,
+        total(got["o_down_b"]),
+        t_3[:, 0],
+        t_3[:, 1],
     )
 
 

time: 774 us -> 583 us (0.75)
  matrix products: 108 us -> 7.87 us
  local copies, waits for them, and re-layouts: 126 us -> 56.2 us
  waiting for transfers between devices: 48.1 us -> 1.4 us
  Pallas kernels: 411 us -> 452 us
  other arithmetic: 33 us -> 25.1 us
    pallas_call x0 -> x2, Pallas kernels: none -> 282 us  [the longest x1 186 us: backward(): pl.pallas_call(functools.partial(back_kernel, dims, names, ops), out_shap...]
    pallas_call x10 -> x3, Pallas kernels: 411 us -> 170 us  [transfer(): pl.pallas_call(functools.partial(transfer_kernel, ops, axes), out_shape=[...]
    unnamed x11 -> x4, waiting for transfers between devices: 48.1 us -> 1.39 us
    dot_general x14 -> x1, matrix products: 34.9 us -> 0.46 us  [mm_nt(): lax.dot_general(left, right, (((1,), (1,)), ((), ())), preferred_element_...]
    dot_general x14 -> x7, matrix products: 40.7 us -> 7.41 us  [mm(): return jnp.dot(left, right, preferred_element_type=F32)]
    dot_general x14 -> x0, matrix products: 32.5 us -> none  [mm_tn(): lax.dot_general(left, right, (((0,), (0,)), ((), ())), preferred_element_...]
    unnamed x211 -> x94, local copies, waits for them, and re-layouts: 25.5 us -> 5.77 us
    reshape x15 -> x7, local copies, waits for them, and re-layouts: 24.1 us -> 5.41 us  [the longest x2 2.87 us: shares(): w = w.reshape(w.shape[0], 2, S, hl).transpose(2, 0, 1, 3)]
  transfers between devices with their start and end apart: 8 -> 4, of which waited for: 1 -> 0; matrix products, arithmetic and copies ran while one was open for 22% -> 11% of each run, Pallas kernels for 42% -> 30%
where the time goes in v3:
time: 583 us; the launch traced here: 573 us
  Pallas kernels  452 us (78%)
  local copies, waits for them, and re-layouts  56.2 us (10%)
  other arithmetic  25.1 us (4%)
  blocking collectives  15.4 us (3%)
  between operations  15 us (3%)
  matrix products  7.87 us (1%)
    pallas_call x1, Pallas kernels, backward(): pl.pallas_call(functools.partial(back_kernel, dims, names, ops), out_shap...  186 us
    pallas_call x3, Pallas kernels, transfer(): pl.pallas_call(functools.partial(transfer_kernel, ops, axes), out_shape=[...  170 us
    pallas_call x1, Pallas kernels, feed_forward(): pl.pallas_call(functools.partial(ffn_kernel, dims, (gather, scatter)), ou...  95.7 us
    all_gather x1, blocking collectives, shards(): f_down_b = lax.all_gather(f_down_b, 'seq', axis=0).reshape(RANK, width)  15.4 us
  transfers between devices with their start and end apart: 4, of which 0 were waited for; matrix products, arithmetic and copies ran while one was open for 11% of the time, Pallas kernels for 30%

profile of v3, /device:TPU:17, one launch (start us, length us, event | category | flops | bytes accessed | tf_op | source)
XLA Modules:
  0.0 573.2 jit_solution(5067531048226156932)
XLA Ops:
  11.1 1.9 reshape.191
  16.8 51.6 %shard_map.305 = (bf16[4,36,2432]{2,1,0:T(8,128)(2,1)S(1)}, bf16[4,8,2688]{2,1,0:T(8,128)(2,1)S(1)}, bf16[4,32,1408]{2,1,0:T(8,128)(2,1)S(1)}, bf16[8,44,1792]{2...) custom-call(bf16[36,2432]{1,0:T(8,128)(2,1)S(1)} %fusion.23.refs_0_, ...), custom_call_target="tpu_custom_call" | custom-call | tf_op jit(solution)/shard_map/pallas_call | solution.py:347
  69.0 1.4 copy.75
  73.2 101.4 %shard_map.306 = (bf16[8,4,36,2432]{3,2,1,0:T(8,128)(2,1)}, bf16[8,4,8,2688]{3,2,1,0:T(8,128)(2,1)S(1)}, bf16[8,2,64,1152]{3,2,1,0:T(8,128)(2,1)S(1)}, s32[8,2,8...) custom-call(bf16[4,36,2432]{2,1,0:T(8,128)(2,1)S(1)} %get-tuple-element.46.refs_0_, ...), custom_call_target="tpu_custom_call" | custom-call | tf_op jit(solution)/shard_map/pallas_call | solution.py:347
  174.9 1.6 dynamic-slice_convert_fusion
  176.6 7.9 %reshape.193 = bf16[1152,2432]{1,0:T(8,128)(2,1)} reshape(bf16[8,4,36,2432]{3,2,1,0:T(8,128)(2,1)} %get-tuple-element.51) | data formatting | bytes 11206656 | tf_op jit(solution)/shard_map/reshape | solution.py:987
  184.5 1.4 convert_reduce_fusion.2
  185.9 3.7 slice.174
  190.9 2.1 multiply_convert_fusion.refs_9_
  193.1 2.2 fusion.34
  199.5 1.9 fusion.13
  203.9 1.6 slice_reduce_fusion.3
  206.3 2.1 slice.190.refs_10_
  210.2 17.4 %shard_map.307 = f32[128,1408]{1,0:T(8,128)S(1)} custom-call(bf16[4,128,1408]{2,1,0:T(8,128)(2,1)S(1)} %bitcast.64), custom_call_target="tpu_custom_call" | custom-call | tf_op jit(solution)/shard_map/pallas_call | solution.py:347
  229.9 1.6 multiply_reduce_fusion.1
  232.2 1.8 dynamic-slice_convert_fusion.1.refs_4_
  234.1 15.4 %all-gather.3 = bf16[32,8,1152]{2,1,0:T(8,128)(2,1)} all-gather(bf16[4,8,1152]{2,1,0:T(8,128)(2,1)S(1)} %copy-done.3), channel_id=5, replica_groups=mesh['seq'=8,'fsdp'=4] {'seq'}, dimensions={0}, use_global_device_ids=true | all-gather | bytes 663552 | tf_op jit(solution)/shard_map/all_gather | solution.py:976
  250.3 2.0 pad_maximum_fusion.refs_7_
  254.2 5.9 %copy.76.gw_in = bf16[8,4,44,1792]{3,2,1,0:T(8,128)(2,1)} copy(bf16[8,4,44,1792]{3,0,2,1:T(8,128)(2,1)} %bitcast.76) | data formatting | bytes 10092544 | tf_op jit(solution)/shard_map/all_gather | solution.py:972
  260.1 95.7 %shard_map.308 = (f32[128,1152]{1,0:T(8,128)}, bf16[8,128,1152]{2,1,0:T(8,128)(2,1)}, bf16[4,8,44,1792]{3,2,1,0:T(8,128)(2,1)}, bf16[4,216,1408]{2,1,0:T(8,128)(...) custom-call(bf16[128,1152]{1,0:T(8,128)(2,1)} %multiply_convert_fusion.1.n2_own, ...), custom_call_target="tpu_custom_call" | custom-call | tf_op jit(solution)/shard_map/pallas_call | solution.py:537
  355.8 185.9 %shard_map.309 = (bf16[2,64,1152]{2,1,0:T(8,128)(2,1)}, f32[2,64,1152]{2,1,0:T(8,128)}, bf16[8,36,256]{2,1,0:T(8,128)(2,1)}, bf16[8,8,256]{2,1,0:T(8,128)(2,1)},...) custom-call(f32[128,1152]{1,0:T(8,128)} %get-tuple-element.57.refs_0, ...), custom_call_target="tpu_custom_call" | custom-call | tf_op jit(solution)/shard_map/pallas_call | solution.py:874
  547.5 1.6 slice.170
  555.4 5.7 slice_reduce_fusion.1
  563.2 1.5 pad_maximum_fusion.1
  (180 shorter events, 42.8 us)
Async XLA Ops:
  7.2 245.2 %all-gather.9.cloned.1.call-start = ((), (), s32[]{:S(2)}) async-start(), calls=%async_computation | async-start | bytes 2654208 | tf_op jit(solution)/shard_map/all_gather | solution.py:974
  7.9 246.3 %all-gather.11.cloned.1.call-start = ((), (), s32[]{:S(2)}) async-start(), calls=%async_computation.1 | async-start | bytes 6307840 | tf_op jit(solution)/shard_map/all_gather | solution.py:972
  70.5 189.6 %all-gather.15.cloned.1.call-start = ((), (), s32[]{:S(2)}) async-start(), calls=%async_computation.3 | async-start | bytes 1474560 | tf_op jit(solution)/shard_map/all_gather | solution.py:975
  71.2 188.9 %all-gather.13.cloned.1.call-start = ((), (), s32[]{:S(2)}) async-start(), calls=%async_computation.2 | async-start | bytes 3041280 | tf_op jit(solution)/shard_map/all_gather | solution.py:973
  174.6 34.9 %copy-start = (bf16[2,4,32,1408]{3,2,1,0:T(8,128)(2,1)}, bf16[2,4,32,1408]{3,2,1,0:T(8,128)(2,1)S(1)}, u32[]{:S(2)}) copy-start(bf16[2,4,32,1408]{3,2,1,0:T(8,128)(2,1)S(1)} %get-tuple-element.53) | copy-start | bytes 2162692
  189.6 3.4 copy-start.6
  190.9 4.4 copy-start.13
  203.6 4.8 copy-start.8
  203.9 6.3 %copy-start.11 = (bf16[512,256]{1,0:T(8,128)(2,1)}, bf16[512,256]{1,0:T(8,128)(2,1)S(1)}, u32[]{:S(2)}) copy-start(bf16[512,256]{1,0:T(8,128)(2,1)S(1)} %convolution_convert_fusion.1.refs_18_) | copy-start | bytes 786436
  210.1 18.9 %copy-start.22 = (bf16[512,128]{1,0:T(8,128)(2,1)S(1)}, bf16[512,128]{1,0:T(8,128)(2,1)}, u32[]{:S(2)}) copy-start(bf16[512,128]{1,0:T(8,128)(2,1)} %copy-done.21) | copy-start | bytes 393220
  210.2 18.9 %copy-start.24 = (bf16[512,128]{1,0:T(8,128)(2,1)S(1)}, bf16[512,128]{1,0:T(8,128)(2,1)}, u32[]{:S(2)}) copy-start(bf16[512,128]{1,0:T(8,128)(2,1)} %copy-done.23) | copy-start | bytes 393220
  210.2 18.9 %copy-start.26 = (bf16[512,128]{1,0:T(8,128)(2,1)S(1)}, bf16[512,128]{1,0:T(8,128)(2,1)}, u32[]{:S(2)}) copy-start(bf16[512,128]{1,0:T(8,128)(2,1)} %copy-done.25) | copy-start | bytes 393220
  228.2 3.3 copy-start.38
  228.2 3.3 copy-start.39
  228.2 5.8 %copy-start.3 = (bf16[4,8,1152]{2,1,0:T(8,128)(2,1)S(1)}, bf16[4,8,1152]{2,1,0:T(8,128)(2,1)}, u32[]{:S(2)}) copy-start(bf16[4,8,1152]{2,1,0:T(8,128)(2,1)} %copy-done.2) | copy-start | bytes 221188
  229.9 20.4 %copy-start.7 = (bf16[1152,1280]{1,0:T(8,128)(2,1)S(1)}, bf16[1152,1280]{1,0:T(8,128)(2,1)}, u32[]{:S(2)}) copy-start(bf16[1152,1280]{1,0:T(8,128)(2,1)} %slice.174) | copy-start | bytes 8847364
  229.9 20.4 %copy-start.14 = (bf16[1152,256]{1,0:T(8,128)(2,1)S(1)}, bf16[1152,256]{1,0:T(8,128)(2,1)}, u32[]{:S(2)}) copy-start(bf16[1152,256]{1,0:T(8,128)(2,1)} %copy-done.13) | copy-start | bytes 1769476
  231.5 20.9 %copy-start.9 = (f32[128,1152]{1,0:T(8,128)}, f32[128,1152]{1,0:T(8,128)S(1)}, u32[]{:S(2)}) copy-start(f32[128,1152]{1,0:T(8,128)S(1)} %get-tuple-element.107.refs_1_) | copy-start | bytes 1769476
  541.7 7.4 %copy-start.17 = (f32[216,1408]{1,0:T(8,128)S(1)}, f32[216,1408]{1,0:T(8,128)}, u32[]{:S(2)}) copy-start(f32[216,1408]{1,0:T(8,128)} %get-tuple-element.72) | copy-start | bytes 3649540
  541.7 8.5 %copy-start.16 = (bf16[8,44,1792]{2,1,0:T(8,128)(2,1)S(1)}, bf16[8,44,1792]{2,1,0:T(8,128)(2,1)}, u32[]{:S(2)}) copy-start(bf16[8,44,1792]{2,1,0:T(8,128)(2,1)} %get-tuple-element.70) | copy-start | bytes 3784708
  546.8 3.6 copy-start.18
  549.1 2.6 copy-start.34
  549.1 3.2 copy-start.30
  549.1 3.8 copy-start.29
  (26 other events, 36.3 us)
Sparse Core Ops, SparseCore 0:
  9.7 52.7 all-gather.8
  70.6 60.8 all-gather.10
  133.1 25.8 all-gather.14
  160.7 39.7 all-gather.12

commit v4 on v3

v4 whole, which is shorter than its diff:
```python
import functools
import math

import jax
import jax.numpy as jnp
from jax import lax
from jax.experimental import pallas as pl
from jax.experimental.pallas import tpu as pltpu
from jax.sharding import PartitionSpec as P

HEADS = 4
HEAD = 256
RANK = 256
EPSILON = 1e-06
ROPE_BASE = 10000.0
MASKED = -1e30
FFN = "ffn"
ROWS = tuple("abcdefgh")
MESH = pl.DeviceIdType.MESH
BF = jnp.bfloat16
F32 = jnp.float32


def mm(left, right):
    return jnp.dot(left, right, preferred_element_type=F32)


def mm_tn(left, right):
    return lax.dot_general(left, right, (((0,), (0,)), ((), ())), preferred_element_type=F32)


def mm_nt(left, right):
    return lax.dot_general(left, right, (((1,), (1,)), ((), ())), preferred_element_type=F32)


def remote(src, dst, send, recv, peer):
    return pltpu.make_async_remote_copy(
        src_ref=src, dst_ref=dst, send_sem=send, recv_sem=recv, device_id=peer, device_id_type=MESH
    )


class Bag:
    def __init__(self, entries=()):
        self.__dict__.update(entries)


class Slot(jax.ShapeDtypeStruct):
    pass


def named(*groups):
    slots = {}
    for group in groups:
        for name, a in group.items():
            slots[name] = Slot(a.shape, a.dtype)
    return slots


def unpack(slots, ops, refs):
    refs = list(refs)
    where = {id(slot): ref for slot, ref in zip(slots.values(), refs)}
    v = Bag(zip(slots, refs))
    rest = refs[len(slots) :]
    bound = Bag()
    for name, (op, src, dst) in ops.items():
        take = len(op.scratch)
        src, dst = (
            where[id(x[0])].at[x[1]] if isinstance(x, tuple) else where[id(x)] for x in (src, dst)
        )
        op.bind(src, dst, *rest[:take])
        setattr(bound, name, op)
        rest = rest[take:]
    return v, bound


class Direct:
    steps = 0

    def relay(self):
        pass

    def __init__(self, x, axis, size, spread=False):
        self.x, self.axis, self.size, self.spread = x, axis, size, spread
        shape = ((size,) if spread else ()) + x.shape
        self.out = jax.ShapeDtypeStruct(shape, x.dtype)
        self.scratch = [
            pltpu.SemaphoreType.DMA,
            pltpu.SemaphoreType.DMA((size,)),
            pltpu.SemaphoreType.DMA((size,)),
        ]

    def bind(self, x_ref, o_ref, local, send, recv):
        me = lax.axis_index(self.axis)
        self.copies = []
        for k in range(1, self.size):
            peer = lax.rem(me + k, self.size)
            src = x_ref if self.spread else x_ref.at[peer]
            self.copies.append(remote(src, o_ref.at[me], send.at[k], recv.at[k], {self.axis: peer}))
        src = x_ref if self.spread else x_ref.at[me]
        self.copies.append(pltpu.make_async_copy(src, o_ref.at[me], local))

    def start(self):
        for copy in self.copies:
            copy.start()

    def finish(self):
        for copy in self.copies:
            copy.wait()


class Square:
    steps = 0

    def __init__(self, x, dim):
        self.x = x
        size = x.shape[dim]
        half = size // 2 if dim == 0 else size // 256 * 128
        first = (slice(None),) * dim
        self.cut = (first + (pl.ds(0, half),), first + (pl.ds(half, size - half),))
        self.out = jax.ShapeDtypeStruct((4,) + x.shape, x.dtype)
        self.scratch = [
            pltpu.SemaphoreType.DMA,
            pltpu.SemaphoreType.DMA((3, 2)),
            pltpu.SemaphoreType.DMA((3, 2)),
        ]

    def bind(self, x_ref, o_ref, local, send, recv):
        me = lax.axis_index("fsdp")
        near_x, near_y, far = me + 1 - 2 * lax.rem(me, 2), lax.rem(me + 2, 4), 3 - me
        cut = self.cut

        def move(src, owner, part, way, peer):
            dst = o_ref.at[owner].at[cut[part]]
            src = dst if src is None else src.at[cut[part]]
            return remote(src, dst, send.at[way, part], recv.at[way, part], {"fsdp": peer})

        self.to_x = [move(x_ref, me, part, 0, near_x) for part in range(2)]
        self.to_y = [move(x_ref, me, part, 1, near_y) for part in range(2)]
        self.from_x = [move(None, near_x, part, 0, near_x) for part in range(2)]
        self.from_y = [move(None, near_y, part, 1, near_y) for part in range(2)]
        self.on_y = move(None, near_x, 0, 2, near_y)
        self.on_x = move(None, near_y, 1, 2, near_x)
        self.from_far = [move(None, far, part, 2, near_x) for part in range(2)]
        self.own = pltpu.make_async_copy(x_ref, o_ref.at[me], local)

    def start(self):
        self.to_x[0].start()
        self.to_y[1].start()
        self.to_x[1].start()
        self.to_y[0].start()
        self.own.start()

    def relay(self):
        self.from_x[0].wait_recv()
        self.on_y.start()
        self.from_y[1].wait_recv()
        self.on_x.start()

    def finish(self):
        self.from_x[1].wait_recv()
        self.from_y[0].wait_recv()
        for part in range(2):
            self.from_far[part].wait_recv()
            self.to_x[part].wait_send()
            self.to_y[part].wait_send()
        self.on_y.wait_send()
        self.on_x.wait_send()
        self.own.wait()


class Post:
    steps = 0

    def __init__(self, x, slots, sends):
        self.slots, self.sends = slots, sends
        self.x = x
        count = len(sends(0))
        self.scratch = [
            pltpu.SemaphoreType.DMA((count,)),
            pltpu.SemaphoreType.DMA((count,)),
            pltpu.SemaphoreType.DMA((slots,)),
        ]

    def bind(self, x_ref, o_ref, local, send, recv):
        s = lax.axis_index("seq")
        self.s = s
        self.plan = []
        for k, (block, device, slot) in enumerate(self.sends(s)):
            src = x_ref if block is None else x_ref.at[block]
            away = remote(src, o_ref.at[slot], send.at[k], recv.at[slot], {"seq": device})
            here = pltpu.make_async_copy(src, o_ref.at[slot], recv.at[slot])
            self.plan.append((device, away, here))
        self.arrive = [
            pltpu.make_async_copy(o_ref.at[k], o_ref.at[k], recv.at[k]) for k in range(self.slots)
        ]

    def start(self):
        for device, away, here in self.plan:
            pl.when(device != self.s)(away.start)
            pl.when(device == self.s)(here.start)

    def finish(self):
        for copy in self.arrive:
            copy.wait()
        for device, away, here in self.plan:
            pl.when(device != self.s)(away.wait_send)


class Line:
    def __init__(self, x, line, span=None):
        self.x, self.line = x, line
        self.lo, self.hi = span or (0, line // 2)
        self.steps = line // 2 - 1
        self.out = jax.ShapeDtypeStruct((line,) + x.shape, x.dtype)
        self.scratch = [
            pltpu.SemaphoreType.DMA,
            pltpu.SemaphoreType.DMA((2 * line,)),
            pltpu.SemaphoreType.DMA((line,)),
        ]

    def bind(self, x_ref, o_ref, local, send, recv):
        self.x_ref, self.o_ref, self.send, self.recv = x_ref, o_ref, send, recv
        line = self.line
        s = lax.axis_index("seq")
        base = s // line * line
        self.n2 = line // 2
        self.i = s - base
        self.p, self.core = self.i // 2, lax.rem(self.i, 2)
        self.sib = s + 1 - 2 * self.core
        self.left = base + lax.rem(self.i + line - 2, line)
        self.right = base + lax.rem(self.i + 2, line)
        self.own = pltpu.make_async_copy(x_ref, o_ref.at[self.i], local)
        self.inside = (self.p >= self.lo) & (self.p < self.hi)

    def copy(self, blk, src, dst, k):
        return remote(src, self.o_ref.at[blk], self.send.at[k], self.recv.at[blk], {"seq": dst})

    def start(self):
        @pl.when(self.p + 1 < self.hi)
        def _():
            self.copy(self.i, self.x_ref, self.right, 0).start()

        @pl.when(self.p > self.lo)
        def _():
            self.copy(self.i, self.x_ref, self.left, 1).start()

        @pl.when(self.inside)
        def _():
            self.copy(self.i, self.x_ref, self.sib, 2).start()

        self.own.start()

    def step(self, d):
        p, n2, o = self.p, self.n2, self.o_ref

        @pl.when((p - d >= 0) & (p < self.hi))
        def _():
            blk = self.i - 2 * d
            self.copy(blk, o.at[blk], self.left, 0).wait_recv()

            @pl.when(p + 1 < self.hi)
            def _():
                self.copy(blk, o.at[blk], self.right, 4 * d).start()

            @pl.when(self.inside)
            def _():
                self.copy(blk, o.at[blk], self.sib, 4 * d + 1).start()

        @pl.when((p + d < n2) & (p >= self.lo))
        def _():
            blk = self.i + 2 * d
            self.copy(blk, o.at[blk], self.right, 0).wait_recv()

            @pl.when(p > self.lo)
            def _():
                self.copy(blk, o.at[blk], self.left, 4 * d + 2).start()

            @pl.when(self.inside)
            def _():
                self.copy(blk, o.at[blk], self.sib, 4 * d + 3).start()

    def finish(self):
        p, n2, o = self.p, self.n2, self.o_ref

        def sent(k, sure):
            @pl.when(sure)
            def _():
                self.copy(self.i, self.x_ref, self.sib, k).wait_send()

        @pl.when(self.inside)
        def _():
            for q in range(n2):
                blk = 2 * q + 1 - self.core
                self.copy(blk, o.at[blk], self.sib, 0).wait_recv()

        sent(0, p + 1 < self.hi)
        sent(1, p > self.lo)
        sent(2, self.inside)
        for d in range(1, n2):
            sent(4 * d, (p - d >= 0) & (p + 1 < self.hi))
            sent(4 * d + 1, (p - d >= 0) & self.inside)
            sent(4 * d + 2, (p + d < n2) & (p > self.lo))
            sent(4 * d + 3, (p + d < n2) & self.inside)
        self.own.wait()


class Grid:
    def __init__(self, x, S, F):
        self.x, self.S, self.F = x, S, F
        self.n2 = n2 = S // 2
        self.steps = n2 - 1
        self.out = jax.ShapeDtypeStruct((S, F) + x.shape, x.dtype)
        self.scratch = [
            pltpu.SemaphoreType.DMA,
            pltpu.SemaphoreType.DMA((2, n2)),
            pltpu.SemaphoreType.DMA((n2, F)),
            pltpu.SemaphoreType.DMA((n2, F)),
            pltpu.SemaphoreType.DMA((S, F)),
        ]

    def bind(self, x_ref, o_ref, local, z_send, f_send, s_send, recv):
        self.x_ref, self.o_ref, self.recv = x_ref, o_ref, recv
        self.z_send, self.f_send, self.s_send = z_send, f_send, s_send
        s, self.f = lax.axis_index("seq"), lax.axis_index("fsdp")
        self.p, self.core = s // 2, lax.rem(s, 2)
        self.s = s
        self.sib = {"seq": s + 1 - 2 * self.core}
        self.left = {"seq": lax.rem(s + self.S - 2, self.S)}
        self.right = {"seq": lax.rem(s + 2, self.S)}
        self.own = pltpu.make_async_copy(x_ref, o_ref.at[s, self.f], local)
        self.square = self.F == 4
        self.near = (1, 2) if self.square else range(1, self.F)

    def place(self, k):
        f = self.f
        if self.square:
            return (f, f + 1 - 2 * lax.rem(f, 2), lax.rem(f + 2, 4), 3 - f)[k]
        return lax.rem(f + self.F - k, self.F)

    def peer(self, k):
        return {"fsdp": self.place(k) if self.square else lax.rem(self.f + k, self.F)}

    def copy(self, q, f, send, peer):
        blk = 2 * q + self.core
        dst = self.o_ref.at[blk, f]
        return remote(dst, dst, send, self.recv.at[blk, f], peer)

    def first(self, send, peer):
        return remote(self.x_ref, self.o_ref.at[self.s, self.f], send, self.recv.at[self.s, self.f], peer)

    def start(self):
        p, n2 = self.p, self.n2

        @pl.when(p < n2 - 1)
        def _():
            self.first(self.z_send.at[0, p], self.right).start()

        @pl.when(p > 0)
        def _():
            self.first(self.z_send.at[1, p], self.left).start()

        for k in self.near:
            self.first(self.f_send.at[p, k], self.peer(k)).start()
        self.first(self.s_send.at[p, 0], self.sib).start()
        self.own.start()

    def pass_on(self, q):
        for k in self.near:
            self.copy(q, self.f, self.f_send.at[q, k], self.peer(k)).start()
        self.copy(q, self.f, self.s_send.at[q, 0], self.sib).start()

    def arrived(self, q, f):
        self.copy(q, f, self.s_send.at[q, 0], self.sib).wait_recv()

    def step(self, d):
        p, n2 = self.p, self.n2

        @pl.when(p - d >= 0)
        def _():
            self.arrived(p - d, self.f)

            @pl.when(p < n2 - 1)
            def _():
                self.copy(p - d, self.f, self.z_send.at[0, p - d], self.right).start()

            self.pass_on(p - d)

        @pl.when(p + d < n2)
        def _():
            self.arrived(p + d, self.f)

            @pl.when(p > 0)
            def _():
                self.copy(p + d, self.f, self.z_send.at[1, p + d], self.left).start()

            self.pass_on(p + d)

    def relay(self, k):
        f = self.place(k)
        for q in range(self.n2):
            self.arrived(q, f)
            self.copy(q, f, self.s_send.at[q, k], self.sib).start()
            if self.square and ((k == 1 and q < self.n2 // 2) or (k == 2 and q >= self.n2 // 2)):
                self.copy(q, f, self.f_send.at[q, 3], self.peer(3 - k)).start()

    def finish(self):
        p, n2 = self.p, self.n2
        for q in range(n2):
            for k in range(self.F):
                f = self.place(k)
                blk = 2 * q + 1 - self.core
                dst = self.o_ref.at[blk, f]
                remote(dst, dst, self.s_send.at[q, k], self.recv.at[blk, f], self.sib).wait_recv()
        for q in range(n2):

            @pl.when((q <= p) & (p < n2 - 1))
            def _():
                self.first(self.z_send.at[0, q], self.right).wait_send()

            @pl.when((q >= p) & (p > 0))
            def _():
                self.first(self.z_send.at[1, q], self.left).wait_send()

            for k in range(self.F):
                self.first(self.s_send.at[q, k], self.sib).wait_send()
                if k:
                    self.first(self.f_send.at[q, k], self.sib).wait_send()
        self.own.wait()


class LineSum:
    vmem = True

    def __init__(self, x, line):
        self.x, self.line = x, line
        self.n2 = n2 = line // 2
        self.steps = n2 - 1
        blk = x.shape[1:]
        self.out = jax.ShapeDtypeStruct(blk, F32)
        self.scratch = [pltpu.VMEM((n2,) + blk, BF), pltpu.VMEM((n2 + 1,) + blk, BF)] + [
            pltpu.SemaphoreType.DMA((3 * n2,)),
            pltpu.SemaphoreType.DMA((3 * n2,)),
        ]

    def bind(self, x_ref, o_ref, mine, came, send, recv):
        self.x_ref, self.o_ref, self.mine, self.came = x_ref, o_ref, mine, came
        line, n2 = self.line, self.n2
        s = lax.axis_index("seq")
        base = s // line * line
        i = s - base
        self.p, self.core = i // 2, lax.rem(i, 2)
        sib = {"seq": s + 1 - 2 * self.core}
        left = {"seq": base + lax.rem(i + line - 2, line)}
        right = {"seq": base + lax.rem(i + 2, line)}
        core = self.core
        self.hand_over = lambda q: remote(
            x_ref.at[2 * q + 1 - core], mine.at[q], send.at[q], recv.at[q], sib
        )
        self.rightward = lambda q: remote(
            mine.at[q], came.at[q + 1], send.at[n2 + q], recv.at[n2 + q], right
        )
        self.leftward = lambda q: remote(
            mine.at[q], came.at[q], send.at[2 * n2 + q], recv.at[2 * n2 + q], left
        )
        order = []
        for k in range((n2 + 1) // 2):
            order += [n2 - 1 - k] + ([k] if k != n2 - 1 - k else [])
        self.order = order

    def start(self):
        for q in self.order:
            self.hand_over(q).start()

    def add(self, q, other):
        self.mine[q] = (self.mine[q].astype(F32) + self.came[other].astype(F32)).astype(BF)

    def step(self, d):
        p, n2 = self.p, self.n2
        if d == 1:
            for q in self.order:
                self.hand_over(q).wait_recv()
                own = self.x_ref[2 * q + self.core].astype(F32)
                self.mine[q] = (own + self.mine[q].astype(F32)).astype(BF)

                @pl.when((q > p) & (p == 0))
                def _():
                    self.rightward(q).start()

                @pl.when((q < p) & (p == n2 - 1))
                def _():
                    self.leftward(q).start()

        q_right = n2 - d

        @pl.when((p > 0) & (p < q_right))
        def _():
            self.rightward(q_right).wait_recv()
            self.add(q_right, q_right + 1)
            self.rightward(q_right).start()

        q_left = d - 1

        @pl.when((p < n2 - 1) & (p > q_left))
        def _():
            self.leftward(q_left).wait_recv()
            self.add(q_left, q_left)
            self.leftward(q_left).start()

    def finish(self):
        p, n2 = self.p, self.n2
        for q in range(n2):

            @pl.when(p == q)
            def _():
                total = self.mine[q].astype(F32)
                if q > 0:
                    self.rightward(q).wait_recv()
                    total += self.came[q + 1].astype(F32)
                if q < n2 - 1:
                    self.leftward(q).wait_recv()
                    total += self.came[q].astype(F32)
                self.o_ref[...] = total

        for q in range(n2):
            self.hand_over(q).wait_send()

            @pl.when(q > p)
            def _():
                self.rightward(q).wait_send()

            @pl.when(q < p)
            def _():
                self.leftward(q).wait_send()


def transfer_kernel(ops, axes, *refs):
    count = len(ops)
    rest = list(refs[2 * count :])
    for a, op in enumerate(ops):
        take = len(op.scratch)
        op.bind(refs[a], refs[count + a], *rest[:take])
        rest = rest[take:]
    barrier = pltpu.get_barrier_semaphore()
    for axis, size in axes:
        me = lax.axis_index(axis)
        for k in range(1, size):
            peer = {axis: lax.rem(me + k, size)}
            pl.semaphore_signal(barrier, inc=1, device_id=peer, device_id_type=MESH)
    pl.semaphore_wait(barrier, sum(size - 1 for _, size in axes))
    for op in ops:
        op.start()
    for d in range(1, 1 + max(op.steps for op in ops)):
        for op in ops:
            if d <= op.steps:
                op.step(d)
    for op in ops:
        op.finish()


def transfer(ops, axes, collective_id):
    spaces = [
        pl.BlockSpec(memory_space=pltpu.VMEM if hasattr(op, "vmem") else pl.ANY) for op in ops
    ]
    return pl.pallas_call(
        functools.partial(transfer_kernel, ops, axes),
        out_shape=[op.out for op in ops],
        in_specs=spaces,
        out_specs=spaces,
        scratch_shapes=[entry for op in ops for entry in op.scratch],
        compiler_params=pltpu.CompilerParams(
            collective_id=collective_id, has_side_effects=True, vmem_limit_bytes=48 << 20
        ),
    )(*[op.x for op in ops])


def meet(axes):
    barrier = pltpu.get_barrier_semaphore()
    for axis, size in axes:
        me = lax.axis_index(axis)
        for k in range(1, size):
            peer = {axis: lax.rem(me + k, size)}
            pl.semaphore_signal(barrier, inc=1, device_id=peer, device_id_type=MESH)
    pl.semaphore_wait(barrier, sum(size - 1 for _, size in axes))


def ffn_kernel(dims, slots, ops, *refs):
    S, F, R, seg, kb, rb, hb, hl, hp = dims
    v, t = unpack(slots, ops, refs[2:])
    stage_sem, cot_sem = refs[:2]
    own = R * seg
    width = v.n2_own.shape[1]
    tokens = S * own
    G = S // R
    gather, scatter = t.n2, t.d_n2
    early = [t.gu_a, t.down_b, t.ffn] if hasattr(t, FFN) else []
    n2, gw, gb, dw, cot_u, gu_a, down_b = v.n2, v.w, v.gb, v.w_down, v.cot_u, v.w_gu_a, v.down_b
    u_gu, act, d_gu, d_u_gu = v.u_gu, v.act, v.d_gu, v.d_u_gu
    meet([("seq", S), ("fsdp", F)])
    gather.start()

    def fetch(s):
        return pltpu.make_async_copy(v.gw.at[:, s], v.stage.at[s % 2], stage_sem.at[s % 2])

    fetch(0).start()
    moves = []
    for j in range(S):
        row, i = j // G, j % G
        for e in range(R):
            at = j * own + e * seg
            src = v.cot.at[i * R + e, row]
            dst = cot_u.at[pl.ds(at, seg), pl.ds(0, width)]
            moves.append(pltpu.make_async_copy(src, dst, cot_sem.at[len(moves)]))
            moves[-1].start()

    for s in range(S):
        if s + 1 < S:
            fetch(s + 1).start()
        fetch(s).wait()
        for f in range(F):
            b = s * F + f
            gw[b * kb : b * kb + kb, :] = v.stage[s % 2, f, 0:kb, :]
            gb[b * rb : b * rb + rb, :] = v.stage[s % 2, f, kb : kb + rb, :]
            gu_a[b * kb : b * kb + kb, :] = v.gu_a[s, f]
        if s + 1 <= gather.steps:
            gather.step(s + 1)
    for move in moves:
        move.wait()
    tile = 256
    tiles = tokens // tile

    @pl.loop(0, tiles)
    def _(k):
        rows = pl.ds(pl.multiple_of(k * tile, tile), tile)
        cot_u[rows, width:] = mm_nt(cot_u[rows, :width], down_b[...]).astype(BF)

    for f in range(F):
        dw[f * hb : f * hb + hb, :] = v.dw[f]
    if hp > hl:
        dw[hl:hp, :] = jnp.zeros((hp - hl, dw.shape[1]), BF)
    gather.finish()
    inner = math.sqrt(2.0 / math.pi)
    per_tile = tile // own

    @pl.loop(0, tiles)
    def _(k):
        rows = pl.ds(pl.multiple_of(k * tile, tile), tile)
        n = n2[pl.ds(k * per_tile, per_tile)].reshape(tile, width)
        u = mm(n, gu_a[...]).astype(BF)
        u_gu[rows, :] = u
        d_act = mm_nt(cot_u[rows, :], dw[...])
        gate = mm(n, gw[:, :hp]) + mm(u[:, :RANK], gb[:, :hp])
        up = mm(n, gw[:, hp:]) + mm(u[:, RANK:], gb[:, hp:])
        square = gate * gate
        th = jnp.tanh(inner * gate * (1.0 + 0.044715 * square))
        half = 0.5 * (1.0 + th)
        gelu = gate * half
        act[rows, :] = (gelu * up).astype(BF)
        slope = half + 0.5 * gate * (1.0 - th * th) * (inner * (1.0 + 3 * 0.044715 * square))
        d_gate = (d_act * up * slope).astype(BF)
        d_up = (d_act * gelu).astype(BF)
        d_gu[rows, :hp] = d_gate
        d_gu[rows, hp:] = d_up
        d_u_gu[rows, :RANK] = mm_nt(d_gate, gb[:, :hp]).astype(BF)
        d_u_gu[rows, RANK:] = mm_nt(d_up, gb[:, hp:]).astype(BF)
        out = mm_nt(d_gu[rows, :], gw[...]) + mm_nt(d_u_gu[rows, :], gu_a[...])
        v.dn[pl.ds(k * per_tile, per_tile)] = out.astype(BF).reshape(per_tile, own, width)

    scatter.start()

    def gate_or_up(half, part, move):
        base = half * hp
        out = mm_tn(u_gu[:, half * RANK : half * RANK + RANK], d_gu[:, base : base + hp]).astype(BF)
        for b in range(S * F):
            part[b % F, b // F, kb : kb + rb, :] = out[b * rb : b * rb + rb, :]

        def columns(src, dst):
            out = mm_tn(n2[...].reshape(tokens, width), d_gu[:, src]).astype(BF)
            for b in range(S * F):
                part[b % F, b // F, 0:kb, dst] = out[b * kb : b * kb + kb, :]

        @pl.loop(0, hp // 256)
        def _(k):
            at = pl.multiple_of(k * 256, 128)
            columns(pl.ds(pl.multiple_of(base + at, 128), 256), pl.ds(at, 256))

        left = hp % 256
        if left:
            columns(slice(base + hp - left, base + hp), slice(hp - left, hp))
        move.start()

    gate_or_up(0, v.part_gate, t.gate)
    scatter.step(1)
    gate_or_up(1, v.part_up, t.up)
    if scatter.steps >= 2:
        scatter.step(2)

    @pl.loop(0, tiles)
    def _(k):
        rows = pl.ds(pl.multiple_of(k * tile, tile), tile)
        out = mm(act[rows, :], dw[...])
        low = out[:, width:].astype(BF)
        v.u_down[rows, :] = low
        out = out[:, :width] + mm(low, down_b[...])
        v.ffn_part[pl.ds(k * per_tile, per_tile)] = out.astype(BF).reshape(per_tile, own, width)

    for d in range(3, scatter.steps + 1):
        scatter.step(d)
    for op in early[2:]:
        op.start()
    scatter.finish()
    out = mm_tn(v.u_down[...], cot_u[:, :width]).astype(BF)
    for b in range(S * F):
        v.g_down_b[b // F, b % F] = out[b * rb : b * rb + rb, :]
    out = mm_tn(n2[...].reshape(tokens, width), d_u_gu[...]).astype(BF)
    for b in range(S * F):
        v.g_gu_a[b // F, b % F] = out[b * kb : b * kb + kb, :]
    for op in early[:2]:
        op.start()
    for op in early[2:] + early[:2]:
        op.step(1)
    step = 128

    @pl.loop(0, cot_u.shape[1] // step)
    def _(k):
        cols = pl.ds(pl.multiple_of(k * step, step), step)
        out = mm_tn(act[...], cot_u[:, cols]).astype(BF)
        for f in range(F):
            v.part_down[f, :, cols] = out[f * hb : f * hb + hb, :]

    for op in early:
        for d in range(2, op.steps + 1):
            op.step(d)
    for op in early:
        op.finish()

    for move, came, put in ((t.gate, v.came_gate, v.sum_gate), (t.up, v.came_up, v.sum_up)):

        def load(s):
            return pltpu.make_async_copy(
                came.at[:, s], v.stage.at[s % 2].at[:, :, pl.ds(0, hp)], stage_sem.at[s % 2]
            )

        move.finish()
        load(0).start()
        for s in range(S):
            if s + 1 < S:
                load(s + 1).start()
            load(s).wait()
            total = v.stage[s % 2, 0, :, :hp].astype(F32)
            for f in range(1, F):
                total += v.stage[s % 2, f, :, :hp].astype(F32)
            put[s] = total.astype(BF)


def over_fsdp(ref, at, F):
    out = ref[(0,) + at].astype(F32)
    for f in range(1, F):
        out += ref[(f,) + at].astype(F32)
    return out


def feed_forward(given, dims, apart, collective_id):
    S, F, R, seg, kb, rb, hb, hl, hp = dims
    g = Bag(given)
    own, width = g.n2_own.shape
    tokens = S * own
    low = functools.partial(jax.ShapeDtypeStruct, dtype=BF)
    full = functools.partial(jax.ShapeDtypeStruct, dtype=F32)
    lora = width + RANK
    outs = dict(
        dn_sum=full((own, width)),
        part_down=low((F, hb, lora)),
        sum_gate=low((S, kb + rb, hp)),
        sum_up=low((S, kb + rb, hp)),
        came_gate=low((F, S, kb + rb, hp)),
        came_up=low((F, S, kb + rb, hp)),
    )
    scratch = dict(
        n2=low((S, own, width)),
        w=low((width, 2 * hp)),
        gb=low((RANK, 2 * hp)),
        w_down=low((hp, lora)),
        cot_u=low((tokens, lora)),
        w_gu_a=low((width, 2 * RANK)),
        u_gu=low((tokens, 2 * RANK)),
        act=low((tokens, hp)),
        d_gu=low((tokens, 2 * hp)),
        d_u_gu=low((tokens, 2 * RANK)),
        u_down=low((tokens, RANK)),
        dn=low((S, own, width)),
        stage=low((2, F, kb + rb, 2 * hp)),
        part_gate=low((F, S, kb + rb, hp)),
        part_up=low((F, S, kb + rb, hp)),
    )
    parts = dict(
        ffn_part=low((S, own, width)),
        g_gu_a=low((S, F, kb, 2 * RANK)),
        g_down_b=low((S, F, rb, width)),
    )
    if apart:
        outs.update(parts)
    else:
        scratch.update(parts)
        outs.update(
            ffn_sum=full((own, width)),
            f_gu_a=full((F, kb, 2 * RANK)),
            f_down_b=full((F, rb, width)),
        )
    slots = named(given, outs, scratch)
    a = Bag(slots)

    def op(kind, src, dst, *more):
        return kind(src, *more), src, dst

    ops = dict(
        n2=op(Line, a.n2_own, a.n2, S),
        d_n2=op(LineSum, a.dn, a.dn_sum, S),
        gate=op(Direct, a.part_gate, a.came_gate, "fsdp", F),
        up=op(Direct, a.part_up, a.came_up, "fsdp", F),
    )
    if not apart:
        ops.update(
            ffn=op(LineSum, a.ffn_part, a.ffn_sum, S),
            gu_a=op(LineSum, a.g_gu_a, a.f_gu_a, S),
            down_b=op(LineSum, a.g_down_b, a.f_down_b, S),
        )
    vmem = pl.BlockSpec(memory_space=pltpu.VMEM)
    away = pl.BlockSpec(memory_space=pl.ANY)
    far = [id(x) for x in (a.gw, a.cot, a.came_gate, a.came_up)]

    def kernel(*refs):
        count = len(slots)
        ffn_kernel(dims, slots, ops, *refs[count : count + 2], *refs[:count], *refs[count + 2 :])

    result = pl.pallas_call(
        kernel,
        out_shape=list(outs.values()),
        in_specs=[away if id(slots[name]) in far else vmem for name in given],
        out_specs=[away if id(slots[name]) in far else vmem for name in outs],
        scratch_shapes=[pltpu.VMEM(x.shape, x.dtype) for x in scratch.values()]
        + [pltpu.SemaphoreType.DMA((2,)), pltpu.SemaphoreType.DMA((S * R,))]
        + [entry for kind, _, _ in ops.values() for entry in kind.scratch],
        compiler_params=pltpu.CompilerParams(
            collective_id=collective_id, has_side_effects=True, vmem_limit_bytes=62 << 20
        ),
    )(*given.values())
    return Bag(zip(outs, result))


def front_kernel(dims, slots, ops, *refs):
    S, F, R, seg, kb, rb, ob = dims
    v, t = unpack(slots, ops, refs)
    own = R * seg
    L = S * seg
    G = S // R
    C = G // HEADS
    qlen = L // C
    width = v.x.shape[2]
    scale = HEAD**-0.5
    s = lax.axis_index("seq")
    r = s // G
    head = lax.rem(s, G) // C
    chunk = lax.rem(s, C)
    meet([("seq", S), ("fsdp", F)])

    n_qkv, n_a, n_q = v.w_qkv.shape[1], v.qkv_a.shape[1], v.q_b.shape[1]
    v.p1[:, :n_qkv] = v.w_qkv[...]
    v.p1[:, n_qkv : n_qkv + n_a] = v.qkv_a[...]
    v.p1[:, n_qkv + n_a :] = v.gain_pair[...]
    t.one.start()
    v.p2[:, :n_q] = v.q_b[...]
    v.p2[:, n_q : n_q + HEAD] = v.kv_b[0]
    v.p2[:, n_q + HEAD : n_q + 2 * HEAD] = v.kv_b[1]
    v.p2[:, n_q + 2 * HEAD :] = v.add_out_b[...]
    t.two.start()
    rows_in = [getattr(t, ROWS[j]) for j in range(R)]
    for op in rows_in:
        op.start()
    t.ids.start()
    first = [t.one, t.two, t.ids] + rows_in
    v.p3[:, :width] = v.w_out[...]
    v.p3[:, width:] = v.out_a[...]
    t.three.start()
    hidden = v.w_gu.shape[1] // 2
    hl = hidden // S
    hp = v.gws.shape[2] // 2
    for half in range(2):
        for j in range(S):
            at = half * hidden + j * hl
            v.gws[j, 0:kb, half * hp : half * hp + hl] = v.w_gu[:, at : at + hl]
            v.gws[j, kb:, half * hp : half * hp + hl] = v.gu_b[half, :, j * hl : j * hl + hl]
            if hp > hl:
                v.gws[j, :, half * hp + hl : half * hp + hp] = jnp.zeros((kb + rb, hp - hl), BF)
    t.gw.start()
    v.dws[:, :width] = v.w_down[...]
    v.dws[:, width:] = v.down_a[...]
    later = [t.gu_a, t.down_b]
    for op in later:
        op.start()
    for d in range(1, t.one.steps + 1):
        for op in first:
            op.step(d)
    t.cot.start()
    t.three.finish()
    t.wo.start()
    t.ids.finish()

    for j in range(S):
        ids = jnp.where(r == 0, v.ids_all[j, 0:1, :], v.ids_all[j, 1:2, :])
        for row in range(2, R):
            ids = jnp.where(r == row, v.ids_all[j, row : row + 1, :], ids)
        v.id_row[:, j * seg : j * seg + seg] = ids.astype(F32)
    id_row = v.id_row[...]
    v.id_cols[...] = jnp.transpose(jnp.broadcast_to(id_row, (128, L)))
    lane = lax.broadcasted_iota(jnp.int32, (128, HEAD // 2), 1).astype(F32)
    spacing = jnp.exp(lane * (-2.0 / HEAD * math.log(ROPE_BASE)))
    places = lax.broadcasted_iota(jnp.int32, (128, L), 1)
    steps = lax.broadcasted_iota(jnp.int32, (128, L), 0)

    @pl.loop(0, L // 128)
    def _(i):
        rows = pl.ds(pl.multiple_of(i * 128, 128), 128)
        before = (v.id_cols[rows, 0:1] == id_row) & (places < steps + i * 128)
        position = jnp.sum(jnp.where(before, 1.0, 0.0), axis=1, keepdims=True)
        angle = position * spacing
        v.cosine[rows, :] = jnp.cos(angle)
        v.sine[rows, :] = jnp.sin(angle)

    for k in range(1, F):
        for op in (t.one, t.two):
            op.relay(k)
    t.dw.start()
    for d in range(1, t.gu_a.steps + 1):
        for op in later:
            op.step(d)
    t.gw.finish()
    t.gw_all.start()
    for op in (t.one, t.two):
        op.finish()
    for op in rows_in:
        op.finish()

    q_cols = pl.ds(pl.multiple_of(head * HEAD, HEAD), HEAD)
    rest_of = HEADS * HEAD
    wide = 2 * HEAD + 3 * RANK
    for j in range(S):
        for f in range(F):
            at = (j * F + f) * kb
            v.w1[at : at + kb, :HEAD] = v.p1_all[j, f, :, q_cols]
            v.w1[at : at + kb, HEAD:] = v.p1_all[j, f, :, rest_of : rest_of + wide]
            v.gain_cols[at : at + kb, :] = v.p1_all[j, f, :, rest_of + wide :].astype(F32)
            at = (j * F + f) * rb
            v.up_b[0, at : at + rb, :] = v.p2_all[j, f, :, q_cols]
            v.up_b[1, at : at + rb, :] = v.p2_all[j, f, :, rest_of : rest_of + HEAD]
            v.up_b[2, at : at + rb, :] = v.p2_all[j, f, :, rest_of + HEAD : rest_of + 2 * HEAD]
            v.out_b[at : at + rb, :] = v.p2_all[j, f, :, rest_of + 2 * HEAD :]
    v.gains[...] = jnp.transpose(v.gain_cols[...])[0:8, :]

    def norm(h, g):
        return (h * lax.rsqrt(jnp.mean(h * h, axis=-1, keepdims=True) + EPSILON) * g).astype(BF)

    for j in range(S):
        v.norm_one[j * seg : j * seg + seg, :] = norm(v.x_all[r, j].astype(F32), v.gains[0:1, :])
    mine = lax.rem(s, G) * R
    for e in range(R):
        v.x_own[e * seg : e * seg + seg, :] = v.x_all[r, mine + e]

    half = HEAD // 2

    @pl.loop(0, L // 256)
    def _(i):
        rows = pl.ds(pl.multiple_of(i * 256, 256), 256)
        pu = mm(v.norm_one[rows, :], v.w1[...])
        u = pu[:, 3 * HEAD :].astype(BF)
        v.u[rows, :] = u
        cosine, sine = v.cosine[rows, :], v.sine[rows, :]
        for k, ref in ((0, v.q_all), (1, v.key)):
            out = pu[:, k * HEAD : (k + 1) * HEAD] + mm(u[:, k * RANK : (k + 1) * RANK], v.up_b[k])
            a, b = out[:, :half], out[:, half:]
            ref[rows, :half] = (a * cosine - b * sine).astype(BF)
            ref[rows, half:] = (b * cosine + a * sine).astype(BF)
        out = pu[:, 2 * HEAD : 3 * HEAD] + mm(u[:, 2 * RANK :], v.up_b[2])
        v.value[rows, :] = out.astype(BF)

    t.cot.step(1)
    for k in range(1, F):
        for op in later:
            op.relay(k)
    t.wo.finish()
    for j in range(S // HEADS):
        for f in range(F):
            at = (j * F + f) * ob
            v.wo[at : at + ob, :] = v.wo_in[j, f]
    from_row = pl.multiple_of(chunk * qlen, own)
    v.query[...] = v.q_all[pl.ds(from_row, qlen), :]
    if C > 1:
        v.part[...] = jnp.zeros(v.part.shape, BF)

    @pl.loop(0, qlen // 128)
    def _(i):
        rows = pl.ds(pl.multiple_of(i * 128, 128), 128)
        here = pl.multiple_of(from_row + i * 128, own)
        allowed = (v.id_cols[pl.ds(here, 128), 0:1] == id_row) & (places <= steps + here)
        scores = jnp.where(allowed, mm_nt(v.query[rows, :], v.key[...]) * scale, MASKED)
        top = jnp.max(scores, axis=-1, keepdims=True)
        lse = top + jnp.log(jnp.sum(jnp.exp(scores - top), axis=-1, keepdims=True))
        probs = jnp.where(allowed, jnp.exp(scores - lse), 0.0)
        v.probs[rows, :] = probs
        mixed = mm(probs.astype(BF), v.value[...]).astype(BF)
        v.mixed[rows, :] = mixed
        out = mm(mixed, v.wo[...]).astype(BF)
        v.part[pl.ds(here // own, 128 // own)] = out.reshape(128 // own, own, out.shape[1])

    t.attn.start()
    t.gw_all.relay()
    t.dw.relay()
    for d in range(1, t.attn.steps + 1):
        t.attn.step(d)
    t.attn.finish()
    u_out = v.attn[:, width:].astype(BF)
    v.u_out[...] = u_out
    resid = v.x_own[...].astype(F32) + v.attn[:, :width] + mm(u_out, v.out_b[...])
    v.resid[...] = resid
    v.n2_own[...] = norm(resid, v.gains[1:2, :])

    for d in range(2, t.cot.steps + 1):
        t.cot.step(d)
    for op in later + [t.cot, t.gw_all, t.dw]:
        op.finish()


def forward(given, dims, collective_id):
    S, F, R, seg, kb, rb, ob = dims
    own = R * seg
    L = S * seg
    G = S // R
    C = G // HEADS
    qlen = L // C
    width = given["x"].shape[2]
    per_head = S // HEADS
    lora = width + RANK
    low = functools.partial(jax.ShapeDtypeStruct, dtype=BF)
    full = functools.partial(jax.ShapeDtypeStruct, dtype=F32)

    g = Bag(given)
    wide = g.w_qkv.shape[1] + g.qkv_a.shape[1] + 128
    thin = g.q_b.shape[1] + 2 * HEAD + width
    hb = g.w_down.shape[0]
    hp = (g.w_gu.shape[1] // 2 // S + 127) // 128 * 128

    def like(array, *lead):
        return jax.ShapeDtypeStruct(lead + array.shape, array.dtype)

    outs = dict(
        w1=low((width, 3 * HEAD + 3 * RANK)),
        norm_one=low((L, width)),
        u=low((L, 3 * RANK)),
        query=low((qlen, HEAD)),
        key=low((L, HEAD)),
        value=low((L, HEAD)),
        cosine=full((L, HEAD // 2)),
        sine=full((L, HEAD // 2)),
        probs=full((qlen, L)),
        mixed=low((qlen, HEAD)),
        u_out=low((own, RANK)),
        resid=full((own, width)),
        n2_own=low((own, width)),
        x_own=low((own, width)),
        gains=full((8, width)),
        out_b=low((RANK, width)),
        wo=low((HEAD, lora)),
        up_b=low((3, RANK, HEAD)),
        gw_all=low((F, S, kb + rb, 2 * hp)),
        dw_all=low((F, hb, lora)),
        cot_all=like(g.cot, S),
        gu_a_all=like(g.gu_a, S, F),
        down_b_all=like(g.down_b, S, F),
        gw_mid=low((S, kb + rb, 2 * hp)),
    )
    scratch = dict(
        p1=low((kb, wide)),
        p2=low((rb, thin)),
        p3=low((ob, lora)),
        gws=low((S, kb + rb, 2 * hp)),
        dws=low((hb, lora)),
        p1_all=low((S, F, kb, wide)),
        p2_all=low((S, F, rb, thin)),
        x_all=low((R, S, seg, width)),
        ids_all=like(g.ids, S),
        p3_all=low((F, ob, lora)),
        wo_in=low((per_head, F, ob, lora)),
        id_row=full((1, L)),
        id_cols=full((L, 128)),
        gain_cols=full((width, 128)),
        q_all=low((L, HEAD)),
        part=low((G, own, lora)),
        attn=full((own, lora)),
    )
    slots = named(given, outs, scratch)
    a = Bag(slots)

    far = [id(x) for x in (a.gw_all, a.dw_all, a.cot_all, a.gu_a_all, a.down_b_all, a.gw_mid)]
    far += [id(x) for x in (a.x, a.ids, a.cot, a.gu_a, a.down_b)]

    def to_head(at):
        return [
            (None, row * G + at // per_head * C + c, lax.rem(at, per_head))
            for row in range(R)
            for c in range(C)
        ]

    def op(kind, src, dst, *more):
        return kind(src, *more), src, dst

    ops = dict(
        one=op(Grid, a.p1, a.p1_all, S, F),
        two=op(Grid, a.p2, a.p2_all, S, F),
        ids=op(Line, a.ids, a.ids_all, S),
        three=op(Direct, a.p3, a.p3_all, "fsdp", F, True),
        wo=op(Post, a.p3_all, a.wo_in, per_head, to_head),
        gw=op(Direct, a.gws, a.gw_mid, "seq", S),
        dw=op(Square, a.dws, a.dw_all, 1) if F == 4 else op(Direct, a.dws, a.dw_all, "fsdp", F, True),
        gw_all=op(Square, a.gw_mid, a.gw_all, 0) if F == 4 else op(Direct, a.gw_mid, a.gw_all, "fsdp", F, True),
        cot=op(Line, a.cot, a.cot_all, S),
        gu_a=op(Grid, a.gu_a, a.gu_a_all, S, F),
        down_b=op(Grid, a.down_b, a.down_b_all, S, F),
        attn=op(LineSum, a.part, a.attn, G),
    )
    for j in range(R):
        span = (j * G // 2, (j + 1) * G // 2)
        ops[ROWS[j]] = Line(jax.ShapeDtypeStruct((seg, width), BF), S, span), (a.x, j), (a.x_all, j)
    vmem = pl.BlockSpec(memory_space=pltpu.VMEM)
    away = pl.BlockSpec(memory_space=pl.ANY)
    result = pl.pallas_call(
        functools.partial(front_kernel, dims, slots, ops),
        out_shape=list(outs.values()),
        in_specs=[away if id(slots[name]) in far else vmem for name in given],
        out_specs=[away if id(slots[name]) in far else vmem for name in outs],
        scratch_shapes=[pltpu.VMEM(a.shape, a.dtype) for a in scratch.values()]
        + [entry for kind, _, _ in ops.values() for entry in kind.scratch],
        compiler_params=pltpu.CompilerParams(
            collective_id=collective_id, has_side_effects=True, vmem_limit_bytes=62 << 20
        ),
    )(*given.values())
    return Bag(zip(outs, result))


def norm_back(G_in, h, g):
    q = lax.rsqrt(jnp.mean(h * h, axis=-1, keepdims=True) + EPSILON)
    gg = G_in * g
    d_gain = jnp.sum(G_in * (h * q), axis=0, keepdims=True)
    return d_gain, q * gg - h * (q * q * q) * jnp.mean(gg * h, axis=-1, keepdims=True)


def back_kernel(dims, slots, ops, *refs):
    S, F, R, seg, L, kb, rb, hb, ob = dims
    v, t = unpack(slots, ops, refs)
    own = R * seg
    G = S // R
    C = G // HEADS
    qlen = L // C
    width = v.resid.shape[1]
    scale = HEAD**-0.5
    s = lax.axis_index("seq")
    chunk = lax.rem(s, C)
    meet([("seq", S), ("fsdp", F)])
    t.down.start()

    gain_two, back = norm_back(v.d_n2[...], v.resid[...], v.gains[1:2, :])
    d_resid = v.cot_own[...].astype(F32) + back
    v.d_resid[...] = d_resid
    v.d_attn_own[...] = d_resid.astype(BF)
    t.d_attn.start()
    activations = (v.resid[...] + v.ffn_sum[...]).astype(BF)
    for j in range(R):
        v.act_rows[j] = activations[j * seg : j * seg + seg, :]
    t.activations.start()
    for put, got, home in ((v.s_gu_a, v.f_gu_a, t.gu_a_home), (v.s_down_b, v.f_down_b, t.down_b_home)):
        put[...] = got[...].astype(BF)
        home.start()
    t.gate_home.start()
    t.up_home.start()
    for d in range(1, t.d_attn.steps + 1):
        t.d_attn.step(d)
    t.d_attn.finish()

    blocks = qlen // own
    first = chunk * blocks
    v.da[:, :width] = v.d_attn[pl.ds(first, blocks)].reshape(qlen, width)
    v.da[:, width:] = mm_nt(v.da[:, :width], v.out_b[...]).astype(BF)
    v.d_mixed[...] = mm_nt(v.da[...], v.wo[...]).astype(BF)

    @pl.loop(0, qlen // 128)
    def _(i):
        rows = pl.ds(pl.multiple_of(i * 128, 128), 128)
        p = v.probs[rows, :]
        d_probs = mm_nt(v.d_mixed[rows, :], v.value[...])
        delta = jnp.sum(p * d_probs, axis=-1, keepdims=True)
        v.d_scores[rows, :] = (p * (d_probs - delta)).astype(BF)
        v.probs_low[rows, :] = p.astype(BF)

    def unrot(g, rows):
        half = HEAD // 2
        cosine, sine = v.cosine[rows, :], v.sine[rows, :]
        a, b = g[:, :half], g[:, half:]
        return (a * cosine + b * sine).astype(BF), (b * cosine - a * sine).astype(BF)

    half = HEAD // 2
    mine = pl.ds(pl.multiple_of(chunk * qlen, own), qlen)
    if C > 1:
        v.d_pu[:, :HEAD] = jnp.zeros((L, HEAD), BF)
    v.d_pu[mine, :half], v.d_pu[mine, half:HEAD] = unrot(mm(v.d_scores[...], v.key[...]) * scale, mine)
    every = pl.ds(0, L)
    v.d_pu[:, HEAD : HEAD + half], v.d_pu[:, HEAD + half : 2 * HEAD] = unrot(
        mm_tn(v.d_scores[...], v.query[...]) * scale, every
    )
    v.d_pu[:, 2 * HEAD : 3 * HEAD] = mm_tn(v.probs_low[...], v.d_mixed[...]).astype(BF)
    for k in range(3):
        v.d_pu[:, 3 * HEAD + k * RANK : 3 * HEAD + (k + 1) * RANK] = mm_nt(
            v.d_pu[:, k * HEAD : (k + 1) * HEAD], v.up_b[k]
        ).astype(BF)

    @pl.loop(0, L // 256)
    def _(i):
        rows = pl.ds(pl.multiple_of(i * 256, 256), 256)
        out = mm_nt(v.d_pu[rows, :], v.w1[...]).astype(BF)
        v.d_attn[pl.ds(i * (256 // own), 256 // own)] = out.reshape(256 // own, own, width)

    t.d_n1.start()

    out = mm_tn(v.mixed[...], v.da[...]).astype(BF)
    for j in range(HEAD // ob):
        v.t_out[j % F, j // F] = out[j * ob : j * ob + ob, :]
    t.out.start()
    out = mm_tn(v.norm_one[...], v.d_pu[:, :HEAD]).astype(BF)
    for b in range(S * F):
        v.t_q[b % F, b // F] = out[b * kb : b * kb + kb, :]
    t.q.start()
    out = mm_tn(v.u[:, :RANK], v.d_pu[:, :HEAD]).astype(BF)
    for b in range(S * F):
        v.t_qb[b % F, b // F] = out[b * rb : b * rb + rb, :]
    t.qb.start()
    t.d_n1.step(1)

    @pl.loop(0, v.t_1.shape[3] // 256)
    def _(i):
        cols = pl.ds(pl.multiple_of(i * 256, 256), 256)
        src = pl.ds(pl.multiple_of(i * 256 + 256, 256), 256)
        out = mm_tn(v.norm_one[...], v.d_pu[:, src]).astype(BF)
        for b in range(S * F):
            v.t_1[b // F, b % F, :, cols] = out[b * kb : b * kb + kb, :]

    t.one.start()
    for d in range(2, t.d_n1.steps + 1):
        t.d_n1.step(d)
    for k in range(2):
        out = mm_tn(
            v.u[:, (k + 1) * RANK : (k + 2) * RANK], v.d_pu[:, (k + 1) * HEAD : (k + 2) * HEAD]
        ).astype(BF)
        for b in range(S * F):
            v.t_2[b // F, b % F, :, k * HEAD : (k + 1) * HEAD] = out[b * rb : b * rb + rb, :]
    out = mm_tn(v.u_out[...], v.d_attn_own[...]).astype(BF)
    for b in range(S * F):
        v.t_2[b // F, b % F, :, 2 * HEAD :] = out[b * rb : b * rb + rb, :]
    t.two.start()

    t.d_n1.finish()
    gain_one, back = norm_back(v.d_n1_sum[...], v.x_own[...].astype(F32), v.gains[0:1, :])
    grad_input = v.d_resid[...] + back
    for j in range(R):
        v.grad_rows[j] = grad_input[j * seg : j * seg + seg, :]
    t.grad_input.start()
    both = jnp.concatenate([gain_one, gain_two, jnp.zeros((126, width), F32)], axis=0)
    both = jnp.transpose(both)
    for b in range(S * F):
        v.t_3[b // F, b % F] = both[b * kb : b * kb + kb, :].astype(BF)
    t.three.start()
    late = [t.one, t.two, t.three]
    for op in late:
        op.step(1)
    for move, got, put, home in (
        (t.q, v.r_q, v.s_q, t.q_home),
        (t.qb, v.r_qb, v.s_qb, t.qb_home),
        (t.out, v.r_out, v.s_out, t.out_home),
    ):
        move.finish()
        for k in range(put.shape[0]):
            put[k] = over_fsdp(got, (k,), F).astype(BF)
        home.start()
    for d in range(2, t.one.steps + 1):
        for op in late:
            op.step(d)
    for op in late:
        op.finish()
    for put, got, home in (
        (v.s_one, v.f_one, t.one_home),
        (v.s_two, v.f_two, t.two_home),
        (v.s_three, v.f_three, t.three_home),
    ):
        put[...] = got[...].astype(BF)
        home.start()
    homes = [t.one_home, t.two_home, t.three_home, t.gu_a_home, t.down_b_home]
    homes += [t.gate_home, t.up_home, t.down]
    for move in [t.grad_input, t.activations, t.q_home, t.qb_home, t.out_home] + homes:
        move.finish()


def backward(given, dims, collective_id):
    S, F, R, seg, L, kb, rb, hb, ob = dims
    own = R * seg
    G = S // R
    C = G // HEADS
    qlen = L // C
    width = given["resid"].shape[1]
    per_head = S // HEADS
    hp = given["sum_up"].shape[2]
    lora = width + RANK
    one = 2 * HEAD + 3 * RANK
    two = 2 * HEAD + width
    low = functools.partial(jax.ShapeDtypeStruct, dtype=BF)
    full = functools.partial(jax.ShapeDtypeStruct, dtype=F32)

    def to_rows(at):
        return [(j, lax.rem(at, G) * R + j, at // G) for j in range(R)]

    def to_out(at):
        return [
            (j, lax.rem(at, G) // C * per_head + j, at // G * C + lax.rem(at, C)) for j in range(per_head)
        ]

    outs = dict(
        act_home=low((R, seg, width)),
        grad_home=full((R, seg, width)),
        o_q=low((S, kb, HEAD)),
        o_qb=low((S, rb, HEAD)),
        o_out=low((R * C, ob, lora)),
        o_gate=low((S, kb + rb, hp)),
        o_up=low((S, kb + rb, hp)),
        o_down=low((F, hb, lora)),
        o_one=low((F, kb, one)),
        o_two=low((F, rb, two)),
        o_three=low((F, kb, 128)),
        o_gu_a=low((F, kb, 2 * RANK)),
        o_down_b=low((F, rb, width)),
    )
    scratch = dict(
        d_resid=full((own, width)),
        d_attn_own=low((own, width)),
        d_attn=low((G, own, width)),
        da=low((qlen, lora)),
        d_mixed=low((qlen, HEAD)),
        d_scores=low((qlen, L)),
        probs_low=low((qlen, L)),
        d_pu=low((L, 3 * HEAD + 3 * RANK)),
        d_n1_sum=full((own, width)),
        grad_rows=full((R, seg, width)),
        act_rows=low((R, seg, width)),
        t_out=low((F, per_head, ob, lora)),
        t_q=low((F, S, kb, HEAD)),
        t_qb=low((F, S, rb, HEAD)),
        t_1=low((S, F, kb, one)),
        t_2=low((S, F, rb, two)),
        t_3=low((S, F, kb, 128)),
        r_out=low((F, per_head, ob, lora)),
        r_q=low((F, S, kb, HEAD)),
        r_qb=low((F, S, rb, HEAD)),
        s_out=low((per_head, ob, lora)),
        s_q=low((S, kb, HEAD)),
        s_qb=low((S, rb, HEAD)),
    )
    scratch.update(
        f_one=full((F, kb, one)),
        s_one=low((F, kb, one)),
        f_two=full((F, rb, two)),
        s_two=low((F, rb, two)),
        f_three=full((F, kb, 128)),
        s_three=low((F, kb, 128)),
        s_gu_a=low((F, kb, 2 * RANK)),
        s_down_b=low((F, rb, width)),
    )
    slots = named(given, outs, scratch)
    a = Bag(slots)

    def op(kind, src, dst, *more):
        return kind(src, *more), src, dst

    ops = dict(
        down=op(Direct, a.part_down, a.o_down, "fsdp", F),
        d_attn=op(Line, a.d_attn_own, a.d_attn, G),
        d_n1=op(LineSum, a.d_attn, a.d_n1_sum, G),
        out=op(Direct, a.t_out, a.r_out, "fsdp", F),
        q=op(Direct, a.t_q, a.r_q, "fsdp", F),
        qb=op(Direct, a.t_qb, a.r_qb, "fsdp", F),
        one=op(LineSum, a.t_1, a.f_one, S),
        two=op(LineSum, a.t_2, a.f_two, S),
        three=op(LineSum, a.t_3, a.f_three, S),
        grad_input=op(Post, a.grad_rows, a.grad_home, R, to_rows),
        activations=op(Post, a.act_rows, a.act_home, R, to_rows),
        q_home=op(Direct, a.s_q, a.o_q, "seq", S),
        qb_home=op(Direct, a.s_qb, a.o_qb, "seq", S),
        out_home=op(Post, a.s_out, a.o_out, R * C, to_out),
        gate_home=op(Direct, a.sum_gate, a.o_gate, "seq", S),
        up_home=op(Direct, a.sum_up, a.o_up, "seq", S),
    )
    ops.update(
        one_home=op(Direct, a.s_one, a.o_one, "fsdp", F),
        two_home=op(Direct, a.s_two, a.o_two, "fsdp", F),
        three_home=op(Direct, a.s_three, a.o_three, "fsdp", F),
        gu_a_home=op(Direct, a.s_gu_a, a.o_gu_a, "fsdp", F),
        down_b_home=op(Direct, a.s_down_b, a.o_down_b, "fsdp", F),
    )
    far = [id(x) for x in (a.part_down, a.sum_gate, a.sum_up)]
    vmem = pl.BlockSpec(memory_space=pltpu.VMEM)
    away = pl.BlockSpec(memory_space=pl.ANY)
    result = pl.pallas_call(
        functools.partial(back_kernel, dims, slots, ops),
        out_shape=list(outs.values()),
        in_specs=[away if id(slots[name]) in far else vmem for name in given],
        out_specs=[away] * len(outs),
        scratch_shapes=[pltpu.VMEM(a.shape, a.dtype) for a in scratch.values()]
        + [entry for kind, _, _ in ops.values() for entry in kind.scratch],
        compiler_params=pltpu.CompilerParams(
            collective_id=collective_id, has_side_effects=True, vmem_limit_bytes=62 << 20
        ),
    )(*given.values())
    return Bag(zip(outs, result))


def finish_kernel(dims, slots, *refs):
    S, F, R, kb, rb, hb, ob, hidden, hl, width = dims
    buffers, sem = refs[len(slots) : -1], refs[-1]
    copies = [pltpu.make_async_copy(refs[k], buffers[k], sem.at[k]) for k in range(len(buffers))]
    for copy in copies:
        copy.start()
    for copy in copies:
        copy.wait()
    v = Bag(zip(slots, buffers + refs[len(buffers) : len(slots)]))
    G = S // R
    C = G // HEADS
    v.activations[...] = v.act_home[...]
    v.grad_input[...] = v.grad_home[...]

    def of_head(ref, head):
        parts = [ref[row * G + head * C + c].astype(F32) for row in range(R) for c in range(C)]
        return sum(parts[1:], parts[0])

    for head in range(HEADS):
        cols = slice(head * HEAD, head * HEAD + HEAD)
        v.w_qkv[:, cols] = of_head(v.o_q, head)
        v.q_b[:, cols] = of_head(v.o_qb, head)
    out = over_fsdp(v.o_one, (), F)
    v.w_qkv[:, HEADS * HEAD :] = out[:, : 2 * HEAD]
    v.qkv_a[...] = out[:, 2 * HEAD :]
    out = over_fsdp(v.o_two, (), F)
    v.kv_b[0] = out[:, :HEAD]
    v.kv_b[1] = out[:, HEAD : 2 * HEAD]
    v.out_b[...] = out[:, 2 * HEAD :]
    v.gains[...] = over_fsdp(v.o_three, (), F)
    v.gu_a[...] = over_fsdp(v.o_gu_a, (), F)
    v.down_b[...] = over_fsdp(v.o_down_b, (), F)
    out = over_fsdp(v.o_down, (), F)
    v.w_down[...] = out[:, :width]
    v.down_a[...] = out[:, width:]
    out = over_fsdp(v.o_out, (), R * C)
    v.w_out[...] = out[:, :width]
    v.out_a[...] = out[:, width:]
    for half, ref in ((0, v.o_gate), (1, v.o_up)):
        for j in range(S):
            at = half * hidden + j * hl
            v.w_gu[:, at : at + hl] = ref[j, 0:kb, :hl].astype(F32)
            v.gu_b[half, :, j * hl : j * hl + hl] = ref[j, kb:, :hl].astype(F32)


def finish(got, dims):
    S, F, R, kb, rb, hb, ob, hidden, hl, width = dims
    full = functools.partial(jax.ShapeDtypeStruct, dtype=F32)
    given = vars(got)
    outs = dict(
        activations=got.act_home,
        grad_input=got.grad_home,
        w_qkv=full((kb, (HEADS + 2) * HEAD)),
        qkv_a=full((kb, 3 * RANK)),
        q_b=full((rb, HEADS * HEAD)),
        kv_b=full((2, rb, HEAD)),
        w_out=full((ob, width)),
        out_a=full((ob, RANK)),
        out_b=full((rb, width)),
        w_gu=full((kb, 2 * hidden)),
        gu_a=full((kb, 2 * RANK)),
        gu_b=full((2, rb, hidden)),
        w_down=full((hb, width)),
        down_a=full((hb, RANK)),
        down_b=full((rb, width)),
        gains=full((kb, 128)),
    )
    slots = named(given, outs)
    vmem = pl.BlockSpec(memory_space=pltpu.VMEM)
    result = pl.pallas_call(
        functools.partial(finish_kernel, dims, slots),
        out_shape=[jax.ShapeDtypeStruct(x.shape, x.dtype) for x in outs.values()],
        in_specs=[pl.BlockSpec(memory_space=pl.ANY)] * len(given),
        out_specs=[vmem] * len(outs),
        scratch_shapes=[pltpu.VMEM(x.shape, x.dtype) for x in given.values()]
        + [pltpu.SemaphoreType.DMA((len(given),))],
        compiler_params=pltpu.CompilerParams(vmem_limit_bytes=48 << 20),
    )(*given.values())
    return Bag(zip(outs, result))


def shards(
    S,
    F,
    layer_input,
    document_numbers,
    cotangent,
    w_qkv,
    qkv_a,
    q_b,
    kv_b,
    w_out,
    out_a,
    out_b,
    w_gu,
    gu_a,
    gu_b,
    w_down,
    down_a,
    down_b,
    gain_a,
    gain_f,
):
    R, seg, width = layer_input.shape
    L = seg * S
    own = R * seg
    G = S // R
    C = G // HEADS
    scale = HEAD**-0.5
    kb = w_qkv.shape[0]
    rb = q_b.shape[0]
    hb = w_down.shape[0]
    ob = w_out.shape[0]
    hidden = w_gu.shape[1] // 2
    hl = hidden // S
    hp = (hl + 127) // 128 * 128
    s = lax.axis_index("seq")
    r = s // G
    head = lax.rem(s, G) // C
    chunk = lax.rem(s, C)
    qlen = L // C

    on_seq = ("seq", S)
    h = forward(
        dict(
            x=layer_input,
            ids=document_numbers,
            cot=cotangent,
            w_qkv=w_qkv,
            qkv_a=qkv_a,
            gain_pair=jnp.pad(jnp.stack([gain_a, gain_f], axis=1), ((0, 0), (0, 126))),
            q_b=q_b,
            kv_b=kv_b,
            add_out_b=out_b,
            w_out=w_out,
            out_a=out_a,
            w_gu=w_gu,
            gu_b=gu_b,
            w_down=w_down,
            down_a=down_a,
            gu_a=gu_a,
            down_b=down_b,
        ),
        (S, F, R, seg, kb, rb, ob),
        0,
    )
    cot = h.cot_all

    dims = (S, F, R, seg, kb, rb, hb, hl, hp)
    apart = S * own > 1024
    ffn = feed_forward(
        dict(
            n2_own=h.n2_own,
            gw=h.gw_all,
            dw=h.dw_all,
            cot=cot,
            gu_a=h.gu_a_all,
            down_b=h.down_b_all.reshape(RANK, width),
        ),
        dims,
        apart,
        5,
    )
    if apart:
        ffn.ffn_sum, ffn.f_gu_a, ffn.f_down_b = transfer(
            [LineSum(x, S) for x in (ffn.ffn_part, ffn.g_gu_a, ffn.g_down_b)], [on_seq], 7
        )
    cot_own = lax.dynamic_slice_in_dim(cot, lax.rem(s, G) * R, R, 0)
    cot_own = lax.dynamic_index_in_dim(cot_own, r, 1, keepdims=False).reshape(own, width)

    got = backward(
        dict(
            d_n2=ffn.dn_sum,
            cot_own=cot_own,
            resid=h.resid,
            gains=h.gains,
            x_own=h.x_own,
            out_b=h.out_b,
            wo=h.wo,
            w1=h.w1,
            up_b=h.up_b,
            norm_one=h.norm_one,
            u=h.u,
            u_out=h.u_out,
            query=h.query,
            key=h.key,
            value=h.value,
            cosine=h.cosine,
            sine=h.sine,
            probs=h.probs,
            mixed=h.mixed,
            ffn_sum=ffn.ffn_sum,
            f_gu_a=ffn.f_gu_a,
            f_down_b=ffn.f_down_b,
            part_down=ffn.part_down,
            sum_gate=ffn.sum_gate,
            sum_up=ffn.sum_up,
        ),
        (S, F, R, seg, L, kb, rb, hb, ob),
        8,
    )

    done = finish(got, (S, F, R, kb, rb, hb, ob, hidden, hl, width))
    return (
        done.activations,
        done.grad_input,
        done.w_qkv,
        done.qkv_a,
        done.q_b,
        done.kv_b,
        done.w_out,
        done.out_a,
        done.out_b,
        done.w_gu,
        done.gu_a,
        done.gu_b,
        done.w_down,
        done.down_a,
        done.down_b,
        done.gains[:, 0],
        done.gains[:, 1],
    )


def solution(mesh):
    both = P(("seq", "fsdp"), None)
    second = P(None, ("seq", "fsdp"), None)
    tokens = P("fsdp", "seq", None)
    gain = P(("seq", "fsdp"))
    return jax.shard_map(
        functools.partial(shards, mesh.shape["seq"], mesh.shape["fsdp"]),
        mesh=mesh,
        in_specs=(tokens, P("fsdp", "seq"), tokens)
        + (both, both, both, second, both, both, both, both, both, second, both, both, both, gain, gain),
        out_specs=(tokens, tokens)
        + (both, both, both, second, both, both, both, both, both, second, both, both, both, gain, gain),
        check_vma=False,
    )
```

time: 583 us -> 470 us (0.81)
  local copies, waits for them, and re-layouts: 56.2 us -> 16.1 us
  other arithmetic: 25.1 us -> 0.68 us
  blocking collectives: 15.4 us -> 0 us
  between operations: 15 us -> 1.24 us
  matrix products: 7.87 us -> 0 us
  Pallas kernels: 452 us -> 446 us
    slice x18 -> x1, local copies, waits for them, and re-layouts: 20.6 us -> 0.7 us  [shards(): done.gains[:, 1]]
    all_gather x1 -> x0, blocking collectives: 15.4 us -> none  [shards(): f_down_b = lax.all_gather(f_down_b, 'seq', axis=0).reshape(RANK, width)]
    reshape x8 -> x0, local copies, waits for them, and re-layouts: 13.3 us -> none  [the longest x1 7.93 us: shards(): p1 = p1.reshape(width, -1)]
    dot_general x8 -> x0, matrix products: 7.87 us -> none  [the longest x7 7.41 us: mm(): return jnp.dot(left, right, preferred_element_type=F32)]
    concatenate x9 -> x0, other arithmetic: 7.39 us -> none  [the longest x1 2.02 us: shards(): w1 = jnp.concatenate([wq, p1[:, q0:q0 + 2 * HEAD + 3 * RANK]], axis=1)]
    unnamed x94 -> x26, local copies, waits for them, and re-layouts: 5.77 us -> 13 us
    convert_element_type x5 -> x0, other arithmetic: 6.01 us -> none  [the longest x1 2.15 us: shards(): norm_one = norm_apply(xrow, gain_one).astype(BF)]
    reduce_sum x11 -> x0, other arithmetic: 5.91 us -> none  [the longest x6 4.41 us: total(): return jnp.sum(t.astype(F32), axis=0)]
  transfers between devices with their start and end apart: 4 -> 0, of which waited for: 0 -> 0; matrix products, arithmetic and copies ran while one was open for 11% -> 0% of each run, Pallas kernels for 30% -> 0%
where the time goes in v4:
time: 470 us; the launch traced here: 464 us
  Pallas kernels  446 us (95%)
  local copies, waits for them, and re-layouts  16.1 us (3%)
    pallas_call x1, Pallas kernels, forward(): pl.pallas_call(functools.partial(front_kernel, dims, slots, ops), out_sha...  151 us
    pallas_call x1, Pallas kernels, feed_forward(): pl.pallas_call(kernel, out_shape=list(outs.values()), in_specs=[away if i...  149 us
    pallas_call x1, Pallas kernels, backward(): pl.pallas_call(functools.partial(back_kernel, dims, slots, ops), out_shap...  140 us
    unnamed x26, local copies, waits for them, and re-layouts  13 us

profile of v4, /device:TPU:17, one launch (start us, length us, event | category | flops | bytes accessed | tf_op | source)
XLA Modules:
  0.0 464.1 jit_solution(7928670733816513023)
XLA Ops:
  0.7 0.7 pad_maximum_fusion
  1.3 0.1 copy.39
  1.5 0.6 pad.4.refs_5_
  2.1 151.5 %shard_map.305 = (bf16[1152,1536]{1,0:T(8,128)(2,1)}, bf16[512,1152]{1,0:T(8,128)(2,1)}, bf16[512,768]{1,0:T(8,128)(2,1)}, bf16[512,256]{1,0:T(8,128)(2,1)}, bf1...) custom-call(bf16[2,64,1152]{2,1,0:T(8,128)(2,1)} %refs_0_.1, ...), custom_call_target="tpu_custom_call" | custom-call | tf_op jit(solution)/shard_map/pallas_call | solution.py:1134
  153.5 149.1 %shard_map.306 = (f32[128,1152]{1,0:T(8,128)}, bf16[4,216,1408]{2,1,0:T(8,128)(2,1)}, bf16[8,44,896]{2,1,0:T(8,128)(2,1)}, bf16[8,44,896]{2,1,0:T(8,128)(2,1)}, ...) custom-call(bf16[128,1152]{1,0:T(8,128)(2,1)} %get-tuple-element.76., ...), custom_call_target="tpu_custom_call" | custom-call | tf_op jit(solution)/shard_map/pallas_call | solution.py:835
  302.7 1.7 constant_dynamic-slice_fusion
  304.4 140.2 %shard_map.307 = (bf16[2,64,1152]{2,1,0:T(8,128)(2,1)}, f32[2,64,1152]{2,1,0:T(8,128)}, bf16[8,36,256]{2,1,0:T(8,128)(2,1)}, bf16[8,8,256]{2,1,0:T(8,128)(2,1)},...) custom-call(f32[128,1152]{1,0:T(8,128)} %get-tuple-element.82.refs_0, ...), custom_call_target="tpu_custom_call" | custom-call | tf_op jit(solution)/shard_map/pallas_call | solution.py:1415
  444.6 0.0 copy-start
  444.6 1.7 copy-done
  446.3 0.0 copy-start.1
  446.3 1.1 copy-done.1
  447.4 1.1 copy-done.2
  448.5 1.1 copy-done.3
  449.5 1.0 copy-done.4
  450.5 1.0 copy-done.5
  451.5 0.9 copy-done.6
  452.4 0.9 copy-done.7
  453.3 0.9 copy-done.8
  454.3 0.9 copy-done.9
  455.2 0.9 copy-done.10
  456.0 0.8 copy-done.11
  456.8 0.8 copy-done.12
  457.6 5.4 %shard_map.308 = (bf16[2,64,1152]{2,1,0:T(8,128)(2,1)}, f32[2,64,1152]{2,1,0:T(8,128)}, f32[36,1536]{1,0:T(8,128)}, f32[36,768]{1,0:T(8,128)}, f32[8,1024]{1,0:T...) custom-call(bf16[2,64,1152]{2,1,0:T(8,128)(2,1)S(1)} %copy-done.5, ...), custom_call_target="tpu_custom_call" | custom-call | tf_op jit(solution)/shard_map/pallas_call | solution.py:1498
  462.9 0.7 slice_reduce_fusion
  (11 shorter events, 0.0 us)
Async XLA Ops:
  444.6 1.7 copy-start
  446.3 1.1 copy-start.1
  447.4 1.1 copy-start.2
  448.5 1.1 copy-start.3
  449.5 1.0 copy-start.4
  450.5 1.0 copy-start.5
  451.5 0.9 copy-start.6
  452.4 0.9 copy-start.7
  453.3 0.9 copy-start.8
  454.3 0.9 copy-start.9
  455.2 0.9 copy-start.10
  456.0 0.8 copy-start.11
  456.8 0.8 copy-start.12

commit v5 on v4

--- a/solution.py
+++ b/solution.py
@@ -279,19 +279,26 @@
             def _():
                 self.copy(blk, o.at[blk], self.sib, 4 * d + 3).start()
 
+    def from_core(self, q):
+        blk = 2 * q + 1 - self.core
+        self.copy(blk, self.o_ref.at[blk], self.sib, 0).wait_recv()
+
     def finish(self):
-        p, n2, o = self.p, self.n2, self.o_ref
+        @pl.when(self.inside)
+        def _():
+            for q in range(self.n2):
+                self.from_core(q)
+
+        self.settle()
+        self.own.wait()
+
+    def settle(self):
+        p, n2 = self.p, self.n2
 
         def sent(k, sure):
             @pl.when(sure)
             def _():
                 self.copy(self.i, self.x_ref, self.sib, k).wait_send()
-
-        @pl.when(self.inside)
-        def _():
-            for q in range(n2):
-                blk = 2 * q + 1 - self.core
-                self.copy(blk, o.at[blk], self.sib, 0).wait_recv()
 
         sent(0, p + 1 < self.hi)
         sent(1, p > self.lo)
@@ -301,7 +308,6 @@
             sent(4 * d + 1, (p - d >= 0) & self.inside)
             sent(4 * d + 2, (p + d < n2) & (p > self.lo))
             sent(4 * d + 3, (p + d < n2) & self.inside)
-        self.own.wait()
 
 
 class Grid:
@@ -621,11 +627,11 @@
             gw[b * kb : b * kb + kb, :] = v.stage[s % 2, f, 0:kb, :]
             gb[b * rb : b * rb + rb, :] = v.stage[s % 2, f, kb : kb + rb, :]
             gu_a[b * kb : b * kb + kb, :] = v.gu_a[s, f]
-        if s + 1 <= gather.steps:
-            gather.step(s + 1)
+        if s == S // 2 and gather.steps >= 1:
+            gather.step(1)
     for move in moves:
         move.wait()
-    tile = 256
+    tile = 2 * own
     tiles = tokens // tile
 
     @pl.loop(0, tiles)
@@ -637,12 +643,13 @@
         dw[f * hb : f * hb + hb, :] = v.dw[f]
     if hp > hl:
         dw[hl:hp, :] = jnp.zeros((hp - hl, dw.shape[1]), BF)
-    gather.finish()
+    gather.own.wait()
+    if gather.steps >= 2:
+        gather.step(2)
     inner = math.sqrt(2.0 / math.pi)
-    per_tile = tile // own
-
-    @pl.loop(0, tiles)
-    def _(k):
+    per_tile = 2
+
+    def one_chip(k):
         rows = pl.ds(pl.multiple_of(k * tile, tile), tile)
         n = n2[pl.ds(k * per_tile, per_tile)].reshape(tile, width)
         u = mm(n, gu_a[...]).astype(BF)
@@ -665,6 +672,23 @@
         out = mm_nt(d_gu[rows, :], gw[...]) + mm_nt(d_u_gu[rows, :], gu_a[...])
         v.dn[pl.ds(k * per_tile, per_tile)] = out.astype(BF).reshape(per_tile, own, width)
 
+    @pl.loop(0, 2 * tiles - 1)
+    def _(turn):
+        for d in range(3, gather.steps + 1):
+
+            @pl.when(turn == 2 * d - 3)
+            def _():
+                gather.step(d)
+
+        away = (turn + 1) // 2
+        k = jnp.where(lax.rem(turn, 2) == 1, gather.p - away, gather.p + away)
+
+        @pl.when((k >= 0) & (k < tiles))
+        def _():
+            gather.from_core(k)
+            one_chip(k)
+
+    gather.settle()
     scatter.start()
 
     def gate_or_up(half, part, move):
@@ -716,7 +740,7 @@
         v.g_gu_a[b // F, b % F] = out[b * kb : b * kb + kb, :]
     for op in early[:2]:
         op.start()
-    for op in early[2:] + early[:2]:
+    for op in early:
         op.step(1)
     step = 128
 
@@ -727,14 +751,7 @@
         for f in range(F):
             v.part_down[f, :, cols] = out[f * hb : f * hb + hb, :]
 
-    for op in early:
-        for d in range(2, op.steps + 1):
-            op.step(d)
-    for op in early:
-        op.finish()
-
-    for move, came, put in ((t.gate, v.came_gate, v.sum_gate), (t.up, v.came_up, v.sum_up)):
-
+    def sum_up(move, came, put):
         def load(s):
             return pltpu.make_async_copy(
                 came.at[:, s], v.stage.at[s % 2].at[:, :, pl.ds(0, hp)], stage_sem.at[s % 2]
@@ -750,6 +767,15 @@
             for f in range(1, F):
                 total += v.stage[s % 2, f, :, :hp].astype(F32)
             put[s] = total.astype(BF)
+
+    for d in range(2, scatter.steps + 1):
+        for op in early:
+            op.step(d)
+        if d == 2:
+            sum_up(t.gate, v.came_gate, v.sum_gate)
+    for op in early:
+        op.finish()
+    sum_up(t.up, v.came_up, v.sum_up)
 
 
 def over_fsdp(ref, at, F):
@@ -894,6 +920,7 @@
     t.gw.start()
     v.dws[:, :width] = v.w_down[...]
     v.dws[:, width:] = v.down_a[...]
+    t.dw.start()
     later = [t.gu_a, t.down_b]
     for op in later:
         op.start()
@@ -929,12 +956,9 @@
     for k in range(1, F):
         for op in (t.one, t.two):
             op.relay(k)
-    t.dw.start()
     for d in range(1, t.gu_a.steps + 1):
         for op in later:
             op.step(d)
-    t.gw.finish()
-    t.gw_all.start()
     for op in (t.one, t.two):
         op.finish()
     for op in rows_in:
@@ -965,6 +989,9 @@
     for e in range(R):
         v.x_own[e * seg : e * seg + seg, :] = v.x_all[r, mine + e]
 
+    for k in range(1, F):
+        for op in later:
+            op.relay(k)
     half = HEAD // 2
 
     @pl.loop(0, L // 256)
@@ -982,10 +1009,9 @@
         out = pu[:, 2 * HEAD : 3 * HEAD] + mm(u[:, 2 * RANK :], v.up_b[2])
         v.value[rows, :] = out.astype(BF)
 
+    t.gw.finish()
+    t.gw_all.start()
     t.cot.step(1)
-    for k in range(1, F):
-        for op in later:
-            op.relay(k)
     t.wo.finish()
     for j in range(S // HEADS):
         for f in range(F):
@@ -1013,7 +1039,6 @@
 
     t.attn.start()
     t.gw_all.relay()
-    t.dw.relay()
     for d in range(1, t.attn.steps + 1):
         t.attn.step(d)
     t.attn.finish()
@@ -1119,7 +1144,7 @@
         three=op(Direct, a.p3, a.p3_all, "fsdp", F, True),
         wo=op(Post, a.p3_all, a.wo_in, per_head, to_head),
         gw=op(Direct, a.gws, a.gw_mid, "seq", S),
-        dw=op(Square, a.dws, a.dw_all, 1) if F == 4 else op(Direct, a.dws, a.dw_all, "fsdp", F, True),
+        dw=op(Direct, a.dws, a.dw_all, "fsdp", F, True),
         gw_all=op(Square, a.gw_mid, a.gw_all, 0) if F == 4 else op(Direct, a.gw_mid, a.gw_all, "fsdp", F, True),
         cot=op(Line, a.cot, a.cot_all, S),
         gu_a=op(Grid, a.gu_a, a.gu_a_all, S, F),
@@ -1502,7 +1527,7 @@
         out_specs=[vmem] * len(outs),
         scratch_shapes=[pltpu.VMEM(x.shape, x.dtype) for x in given.values()]
         + [pltpu.SemaphoreType.DMA((len(given),))],
-        compiler_params=pltpu.CompilerParams(vmem_limit_bytes=48 << 20),
+        compiler_params=pltpu.CompilerParams(vmem_limit_bytes=62 << 20),
     )(*given.values())
     return Bag(zip(outs, result))
 

time: 470 us -> 435 us (0.926)
  Pallas kernels: 446 us -> 424 us
  local copies, waits for them, and re-layouts: 16.1 us -> 3.94 us
    pallas_call x1, Pallas kernels: 151 us -> 137 us  [forward(): pl.pallas_call(functools.partial(front_kernel, dims, slots, ops), out_sha...]
    unnamed x26 -> x0, local copies, waits for them, and re-layouts: 13 us -> none
    pallas_call x1, Pallas kernels: 140 us -> 130 us  [backward(): pl.pallas_call(functools.partial(back_kernel, dims, slots, ops), out_shap...]
where the time goes in v5:
time: 435 us; the launch traced here: 429 us
  Pallas kernels  424 us (97%)
    pallas_call x1, Pallas kernels, feed_forward(): pl.pallas_call(kernel, out_shape=list(outs.values()), in_specs=[away if i...  151 us
    pallas_call x1, Pallas kernels, forward(): pl.pallas_call(functools.partial(front_kernel, dims, slots, ops), out_sha...  137 us
    pallas_call x1, Pallas kernels, backward(): pl.pallas_call(functools.partial(back_kernel, dims, slots, ops), out_shap...  130 us

profile of v5, /device:TPU:17, one launch (start us, length us, event | category | flops | bytes accessed | tf_op | source)
XLA Modules:
  0.0 429.4 jit_solution(5800984212178655952)
XLA Ops:
  0.7 0.7 pad_maximum_fusion
  1.3 0.1 copy.39
  1.5 0.6 pad.4.refs_5_
  2.1 137.3 %shard_map.305 = (bf16[1152,1536]{1,0:T(8,128)(2,1)}, bf16[512,1152]{1,0:T(8,128)(2,1)}, bf16[512,768]{1,0:T(8,128)(2,1)}, bf16[512,256]{1,0:T(8,128)(2,1)}, bf1...) custom-call(bf16[2,64,1152]{2,1,0:T(8,128)(2,1)} %refs_0_.1, ...), custom_call_target="tpu_custom_call" | custom-call | tf_op jit(solution)/shard_map/pallas_call | solution.py:1159
  139.3 151.3 %shard_map.306 = (f32[128,1152]{1,0:T(8,128)}, bf16[4,216,1408]{2,1,0:T(8,128)(2,1)}, bf16[8,44,896]{2,1,0:T(8,128)(2,1)}, bf16[8,44,896]{2,1,0:T(8,128)(2,1)}, ...) custom-call(bf16[128,1152]{1,0:T(8,128)(2,1)} %get-tuple-element.76., ...), custom_call_target="tpu_custom_call" | custom-call | tf_op jit(solution)/shard_map/pallas_call | solution.py:861
  290.7 1.7 constant_dynamic-slice_fusion
  292.4 129.6 %shard_map.307 = (bf16[2,64,1152]{2,1,0:T(8,128)(2,1)}, f32[2,64,1152]{2,1,0:T(8,128)}, bf16[8,36,256]{2,1,0:T(8,128)(2,1)}, bf16[8,8,256]{2,1,0:T(8,128)(2,1)},...) custom-call(f32[128,1152]{1,0:T(8,128)} %get-tuple-element.82.refs_0, ...), custom_call_target="tpu_custom_call" | custom-call | tf_op jit(solution)/shard_map/pallas_call | solution.py:1440
  422.0 5.5 %shard_map.308 = (bf16[2,64,1152]{2,1,0:T(8,128)(2,1)}, f32[2,64,1152]{2,1,0:T(8,128)}, f32[36,1536]{1,0:T(8,128)}, f32[36,768]{1,0:T(8,128)}, f32[8,1024]{1,0:T...) custom-call(bf16[2,64,1152]{2,1,0:T(8,128)(2,1)} %get-tuple-element., ...), custom_call_target="tpu_custom_call" | custom-call | tf_op jit(solution)/shard_map/pallas_call | solution.py:1523
  427.5 1.5 slice_reduce_fusion

commit v6 on v5

--- a/solution.py
+++ b/solution.py
@@ -631,6 +631,7 @@
             gather.step(1)
     for move in moves:
         move.wait()
+    v.cot_own[...] = cot_u[pl.ds(pl.multiple_of(lax.axis_index("seq") * own, own), own), :width]
     tile = 2 * own
     tiles = tokens // tile
 
@@ -753,19 +754,20 @@
 
     def sum_up(move, came, put):
         def load(s):
-            return pltpu.make_async_copy(
-                came.at[:, s], v.stage.at[s % 2].at[:, :, pl.ds(0, hp)], stage_sem.at[s % 2]
-            )
+            place = v.stage.at[s % 2].at[:, :, pl.ds(s // 2 % 2 * hp, hp)]
+            return pltpu.make_async_copy(came.at[:, s], place, stage_sem.at[s % 4])
 
         move.finish()
-        load(0).start()
+        for s in range(3):
+            load(s).start()
         for s in range(S):
-            if s + 1 < S:
-                load(s + 1).start()
+            if s + 3 < S:
+                load(s + 3).start()
             load(s).wait()
-            total = v.stage[s % 2, 0, :, :hp].astype(F32)
+            cols = slice(s // 2 % 2 * hp, s // 2 % 2 * hp + hp)
+            total = v.stage[s % 2, 0, :, cols].astype(F32)
             for f in range(1, F):
-                total += v.stage[s % 2, f, :, :hp].astype(F32)
+                total += v.stage[s % 2, f, :, cols].astype(F32)
             put[s] = total.astype(BF)
 
     for d in range(2, scatter.steps + 1):
@@ -795,6 +797,7 @@
     lora = width + RANK
     outs = dict(
         dn_sum=full((own, width)),
+        cot_own=low((own, width)),
         part_down=low((F, hb, lora)),
         sum_gate=low((S, kb + rb, hp)),
         sum_up=low((S, kb + rb, hp)),
@@ -864,7 +867,7 @@
         in_specs=[away if id(slots[name]) in far else vmem for name in given],
         out_specs=[away if id(slots[name]) in far else vmem for name in outs],
         scratch_shapes=[pltpu.VMEM(x.shape, x.dtype) for x in scratch.values()]
-        + [pltpu.SemaphoreType.DMA((2,)), pltpu.SemaphoreType.DMA((S * R,))]
+        + [pltpu.SemaphoreType.DMA((4,)), pltpu.SemaphoreType.DMA((S * R,))]
         + [entry for kind, _, _ in ops.values() for entry in kind.scratch],
         compiler_params=pltpu.CompilerParams(
             collective_id=collective_id, has_side_effects=True, vmem_limit_bytes=62 << 20
@@ -1618,13 +1621,10 @@
         ffn.ffn_sum, ffn.f_gu_a, ffn.f_down_b = transfer(
             [LineSum(x, S) for x in (ffn.ffn_part, ffn.g_gu_a, ffn.g_down_b)], [on_seq], 7
         )
-    cot_own = lax.dynamic_slice_in_dim(cot, lax.rem(s, G) * R, R, 0)
-    cot_own = lax.dynamic_index_in_dim(cot_own, r, 1, keepdims=False).reshape(own, width)
-
     got = backward(
         dict(
             d_n2=ffn.dn_sum,
-            cot_own=cot_own,
+            cot_own=ffn.cot_own,
             resid=h.resid,
             gains=h.gains,
             x_own=h.x_own,

time: 435 us -> 431 us (level)
  no operation moved by 1% of the time
where the time goes in v6:
time: 431 us; the launch traced here: 426 us
  Pallas kernels  422 us (98%)
    pallas_call x1, Pallas kernels, feed_forward(): pl.pallas_call(kernel, out_shape=list(outs.values()), in_specs=[away if i...  150 us
    pallas_call x1, Pallas kernels, forward(): pl.pallas_call(functools.partial(front_kernel, dims, slots, ops), out_sha...  137 us
    pallas_call x1, Pallas kernels, backward(): pl.pallas_call(functools.partial(back_kernel, dims, slots, ops), out_shap...  130 us

profile of v6, /device:TPU:17, one launch (start us, length us, event | category | flops | bytes accessed | tf_op | source)
XLA Modules:
  0.0 426.0 jit_solution(8364698413381700149)
XLA Ops:
  0.7 0.7 pad_maximum_fusion
  1.3 0.1 copy.39
  1.5 0.6 pad.4.refs_5_
  2.1 137.2 %shard_map.305 = (bf16[1152,1536]{1,0:T(8,128)(2,1)}, bf16[512,1152]{1,0:T(8,128)(2,1)}, bf16[512,768]{1,0:T(8,128)(2,1)}, bf16[512,256]{1,0:T(8,128)(2,1)}, bf1...) custom-call(bf16[2,64,1152]{2,1,0:T(8,128)(2,1)} %refs_0_.1, ...), custom_call_target="tpu_custom_call" | custom-call | tf_op jit(solution)/shard_map/pallas_call | solution.py:1162
  139.3 149.5 %shard_map.306 = (f32[128,1152]{1,0:T(8,128)}, bf16[128,1152]{1,0:T(8,128)(2,1)}, bf16[4,216,1408]{2,1,0:T(8,128)(2,1)}, bf16[8,44,896]{2,1,0:T(8,128)(2,1)}, bf...) custom-call(bf16[128,1152]{1,0:T(8,128)(2,1)} %get-tuple-element.77., ...), custom_call_target="tpu_custom_call" | custom-call | tf_op jit(solution)/shard_map/pallas_call | solution.py:864
  288.9 129.7 %shard_map.307 = (bf16[2,64,1152]{2,1,0:T(8,128)(2,1)}, f32[2,64,1152]{2,1,0:T(8,128)}, bf16[8,36,256]{2,1,0:T(8,128)(2,1)}, bf16[8,8,256]{2,1,0:T(8,128)(2,1)},...) custom-call(f32[128,1152]{1,0:T(8,128)} %get-tuple-element.83.refs_0, ...), custom_call_target="tpu_custom_call" | custom-call | tf_op jit(solution)/shard_map/pallas_call | solution.py:1443
  418.6 5.5 %shard_map.308 = (bf16[2,64,1152]{2,1,0:T(8,128)(2,1)}, f32[2,64,1152]{2,1,0:T(8,128)}, f32[36,1536]{1,0:T(8,128)}, f32[36,768]{1,0:T(8,128)}, f32[8,1024]{1,0:T...) custom-call(bf16[2,64,1152]{2,1,0:T(8,128)(2,1)} %get-tuple-element., ...), custom_call_target="tpu_custom_call" | custom-call | tf_op jit(solution)/shard_map/pallas_call | solution.py:1526
  424.1 1.5 slice_reduce_fusion
